TPU v7x, 256 devices: a whole 4x4x8 slice. The times are simulated.
256 devices in a mesh: tm: 16 (over y, z_hi, core), sx: 4 (over x), sy: 4 (over z_lo).
Axes of the slice: x: 4, y: 4, z: 8 (z_hi: 2, z_lo: 4; z = z_hi * 4 + z_lo), core: 2. Of those that a mesh axis runs over, the one named last changes fastest.
Arguments:
- forcing: float32 [2, 32, 1024, 1024], P(None, 'tm', 'sx', 'sy'), may hold values from -6 to 6
- initial: float32 [2, 1024, 1024], P(None, 'sx', 'sy'), may hold values from -6 to 6
- previous_last: float32 [2, 1024, 1024], P(None, 'sx', 'sy'), may hold values from -16 to 16
- cell_class: int32 [1024, 1024], P('sx', 'sy'), may hold values from 0 to 7
- courant_table: float32 [8], replicated, may hold values from 0.02 to 0.25
Outputs:
- next_iterate: float32 [2, 32, 1024, 1024], P(None, 'tm', 'sx', 'sy')
All inputs are finite; a program needn't handle non-finite values.
Results may differ from a plain program's by a relative error of at most 0.00019.
Values sent between devices are 32-bit elements; how exact they have to be, the bound alone decides.
No kernel may reach another device: no remote copies, remote signals or barrier semaphores. Data moves between devices by JAX's collectives and lax.ppermute only.
A program may use at most 64 MiB of HBM per device.

v0:
```python
import math

import jax
import jax.numpy as jnp
from jax import lax
from jax.sharding import PartitionSpec as P

SWEEPS = 8


circulant_alpha = 0.1


def swapped(value, axis, distance):
    mask = 2**distance
    pairs = [(source, source ^ mask) for source in range(lax.axis_size(axis))]
    return lax.ppermute(value, axis, pairs)


def padded_2(shard, sides, width):
    for axis, dim in sides:
        size, length = (lax.axis_size(axis), shard.shape[dim])
        up = [(i, (i + 1) % size) for i in range(size - 1)]
        down = [(j, i) for i, j in up]
        last = lax.slice_in_dim(shard, length - width, length, axis=dim)
        leading = lax.slice_in_dim(shard, 0, width, axis=dim)
        before = lax.ppermute(last, axis, up)
        after = lax.ppermute(leading, axis, down)
        shard = jnp.concatenate([before, shard, after], axis=dim)
    return shard


def complex_times(left_re, left_im, right_re, right_im):
    return (left_re * right_re - left_im * right_im, left_re * right_im + left_im * right_re)


def reversed_bits(value, nbits):
    result = jnp.zeros_like(value)
    for bit in range(nbits):
        result = result * 2 + (value >> bit & 1)
    return result


def neighbours(padded):
    return (
        padded[..., 2:, 1:-1]
        + padded[..., :-2, 1:-1]
        + padded[..., 1:-1, 2:]
        + padded[..., 1:-1, :-2]
    )


def inverse_diagonal(courant, lam_re, lam_im):
    diag_re = lam_re * lam_re - lam_im * lam_im + 4.0 * courant
    diag_im = 2.0 * lam_re * lam_im + jnp.zeros_like(courant)
    magnitude = diag_re * diag_re + diag_im * diag_im
    return (diag_re / magnitude, -diag_im / magnitude)


def angle_table(rows_freq, cols_step, total):
    product = rows_freq[:, None] * cols_step[None, :] % total
    return 2.0 * math.pi * product.astype(jnp.float32) / total


def per_device(forcing, initial, previous_last, cell_class, courant_table):
    highest = lax.Precision.HIGHEST
    count = lax.axis_size("tm")
    nbits = count.bit_length() - 1
    place = lax.axis_index("tm")
    local_steps = forcing.shape[1]
    total = count * local_steps
    decay_log = math.log(circulant_alpha) / total
    factor = math.exp(decay_log)
    first = jnp.where(place == 0, 1.0, 0.0).astype(jnp.float32)
    right = forcing.at[:, 0].add((initial - circulant_alpha * previous_last) * first)
    step_index = (place * local_steps + jnp.arange(local_steps)).astype(jnp.float32)
    weighted = right * jnp.exp(step_index * decay_log)[None, :, None, None]
    local_range = jnp.arange(local_steps)
    classes = jnp.arange(courant_table.shape[0])
    courant = jnp.sum(
        jnp.where(cell_class[None] == classes[:, None, None], courant_table[:, None, None], 0.0),
        axis=0,
    )
    spec_re = weighted
    spec_im = None
    for level in range(nbits):
        bit = nbits - 1 - level
        half = 1 << bit
        packed = spec_re[None] if spec_im is None else jnp.stack((spec_re, spec_im))
        partner = swapped(packed, "tm", bit)
        own_im = jnp.zeros_like(spec_re) if spec_im is None else spec_im
        other_im = jnp.zeros_like(spec_re) if spec_im is None else partner[1]
        upper = place >> bit & 1
        angle = -math.pi * (place & half - 1).astype(jnp.float32) / half
        diff_re, diff_im = complex_times(
            partner[0] - spec_re, other_im - own_im, jnp.cos(angle), jnp.sin(angle)
        )
        spec_re, spec_im = (
            jnp.where(upper == 1, diff_re, spec_re + partner[0]),
            jnp.where(upper == 1, diff_im, own_im + other_im),
        )
    freq_int = reversed_bits(place, nbits) + count * local_range
    theta = angle_table(freq_int, local_range, total)
    cos_t = jnp.cos(theta)
    sin_t = jnp.sin(theta)
    spectrum_re = jnp.einsum("jq,cqxy->cjxy", cos_t, spec_re, precision=highest) + jnp.einsum(
        "jq,cqxy->cjxy", sin_t, spec_im, precision=highest
    )
    spectrum_im = jnp.einsum("jq,cqxy->cjxy", cos_t, spec_im, precision=highest) - jnp.einsum(
        "jq,cqxy->cjxy", sin_t, spec_re, precision=highest
    )
    phase = 2.0 * math.pi * freq_int.astype(jnp.float32) / total
    lam_re = (1.0 - factor * jnp.cos(phase))[:, None, None]
    lam_im = (factor * jnp.sin(phase))[:, None, None]
    lifted_re, lifted_im = complex_times(lam_re, lam_im, spectrum_re[0], spectrum_im[0])
    g_re = spectrum_re[1] + lifted_re
    g_im = spectrum_im[1] + lifted_im
    inv_re, inv_im = inverse_diagonal(courant[None], lam_re, lam_im)
    field_re, field_im = complex_times(g_re, g_im, inv_re, inv_im)
    for sweep in range(SWEEPS - 1):
        padded = padded_2(jnp.stack((field_re, field_im)), (("sx", 2), ("sy", 3)), 1)
        beside = neighbours(padded)
        field_re, field_im = complex_times(
            g_re + courant * beside[0], g_im + courant * beside[1], inv_re, inv_im
        )
    moved_re, moved_im = complex_times(lam_re, lam_im, field_re, field_im)
    out_re = jnp.stack((field_re, moved_re - spectrum_re[0]))
    out_im = jnp.stack((field_im, moved_im - spectrum_im[0]))
    theta = angle_table(freq_int, local_range, total)
    cos_t = jnp.cos(theta)
    sin_t = jnp.sin(theta)
    value_re = jnp.einsum("jq,cjxy->cqxy", cos_t, out_re, precision=highest) - jnp.einsum(
        "jq,cjxy->cqxy", sin_t, out_im, precision=highest
    )
    value_im = jnp.einsum("jq,cjxy->cqxy", cos_t, out_im, precision=highest) + jnp.einsum(
        "jq,cjxy->cqxy", sin_t, out_re, precision=highest
    )
    for bit in range(nbits):
        half = 1 << bit
        partner = swapped(jnp.stack((value_re, value_im)), "tm", bit)
        upper = place >> bit & 1
        angle = math.pi * (place & half - 1).astype(jnp.float32) / half
        target_re = jnp.where(upper == 1, value_re, partner[0])
        target_im = jnp.where(upper == 1, value_im, partner[1])
        rot_re, rot_im = complex_times(target_re, target_im, jnp.cos(angle), jnp.sin(angle))
        value_re, value_im = (
            jnp.where(upper == 1, partner[0] - rot_re, value_re + rot_re),
            jnp.where(upper == 1, partner[1] - rot_im, value_im + rot_im),
        )
    result = value_re / total
    return result * jnp.exp(-step_index * decay_log)[None, :, None, None]


def solution(mesh):
    in_specs = (
        P(None, "tm", "sx", "sy"),
        P(None, "sx", "sy"),
        P(None, "sx", "sy"),
        P("sx", "sy"),
        P(),
    )
    out_specs = P(None, "tm", "sx", "sy")
    return jax.shard_map(
        per_device, mesh=mesh, in_specs=in_specs, out_specs=out_specs, check_vma=False
    )
```

profile of v0, /device:TPU:118, one launch (start us, length us, event | category | flops | bytes accessed | tf_op | source)
XLA Modules:
  0.0 566.2 jit_solution(15689264436966280288)
XLA Ops:
  2.4 26.0 %collective-permute-done = f32[1,2,2,256,256]{4,3,2,1,0:T(8,128)} collective-permute-done((f32[1,2,2,256,256]{4,3,2,1,0:T(8,128)S(1)}, f32[1,2,2,256,256]{4,3,2,1,0:T(8,128)}, u32[]{:S(2)}, u32[]{:S(2)}) %collective-permute-start) | collective-permute-done | bytes 1048608 | tf_op jit(solution)/shard_map/ppermute | solution.py:17
  33.1 45.4 %collective-permute-done.1 = f32[2,2,2,256,256]{4,3,2,1,0:T(8,128)} collective-permute-done((f32[2,2,2,256,256]{4,3,2,1,0:T(8,128)}, f32[2,2,2,256,256]{4,3,2,1,0:T(8,128)}, u32[]{:S(2)}, u32[]{:S(2)}) %collective-permute-start.1) | collective-permute-done | bytes 2097184 | tf_op jit(solution)/shard_map/ppermute | solution.py:17
  81.8 4.5 collective-permute-start.2
  86.4 81.3 %collective-permute-done.2 = f32[2,2,2,256,256]{4,3,2,1,0:T(8,128)} collective-permute-done((f32[2,2,2,256,256]{4,3,2,1,0:T(8,128)S(1)}, f32[2,2,2,256,256]{4,3,2,1,0:T(8,128)}, u32[]{:S(2)}, u32[]{:S(2)}) %collective-permute-start.2) | collective-permute-done | bytes 2097184 | tf_op jit(solution)/shard_map/ppermute | solution.py:17
  173.0 4.0 collective-permute-done.3
  178.8 4.1 fusion.47
  183.0 4.1 fusion.49
  187.1 4.1 fusion.53
  191.3 4.1 fusion.51
  201.9 4.2 collective-permute-done.5
  208.5 10.7 %collective-permute-start.6 = (f32[2,2,258,1]{2,1,3,0:T(2,128)S(1)}, f32[2,2,258,1]{2,1,3,0:T(2,128)S(1)}, u32[]{:S(2)}, u32[]{:S(2)}) collective-permute-start(f32[2,2,258,1]{2,1,3,0:T(2,128)S(1)} %copy.95), channel_id=1, source_target_pairs={{1,0},{2,1},{3,2},{5,4},{6,5},{7,6},{9,8},{10,9},{11,10},{13,12},{... | collective-permute-start | bytes 12392 | tf_op jit(solution)/shard_map/ppermute | solution.py:28
  233.0 4.2 collective-permute-done.9
  242.6 4.0 collective-permute-done.11
  252.7 4.2 collective-permute-done.13
  261.2 4.0 collective-permute-done.15
  270.8 4.2 collective-permute-done.17
  279.3 4.0 collective-permute-done.19
  289.0 4.2 collective-permute-done.21
  297.5 4.0 collective-permute-done.23
  307.1 4.2 collective-permute-done.25
  315.6 4.0 collective-permute-done.27
  325.4 4.0 collective-permute-done.29
  333.7 4.0 collective-permute-done.31
  339.8 4.0 fusion.41
  343.9 4.1 fusion.39
  348.3 4.1 fusion.45
  352.3 4.0 fusion.43
  357.2 4.1 collective-permute-done.32
  363.3 6.0 %collective-permute-start.33 = (f32[2,2,2,256,256]{4,3,2,1,0:T(8,128)}, f32[2,2,2,256,256]{4,3,2,1,0:T(8,128)}, u32[]{:S(2)}, u32[]{:S(2)}) collective-permute-start(f32[2,2,2,256,256]{4,3,2,1,0:T(8,128)} %pad_maximum_fusion.4), channel_id=1, source_target_pairs={{0,32},{16,48},{32,0},{48,16},{64,96},{80,112},{96,64},{112,80},{1... | collective-permute-start | bytes 6291464 | tf_op jit(solution)/shard_map/ppermute | solution.py:17
  369.5 91.5 %collective-permute-done.33 = f32[2,2,2,256,256]{4,3,2,1,0:T(8,128)} collective-permute-done((f32[2,2,2,256,256]{4,3,2,1,0:T(8,128)}, f32[2,2,2,256,256]{4,3,2,1,0:T(8,128)}, u32[]{:S(2)}, u32[]{:S(2)}) %collective-permute-start.33) | collective-permute-done | bytes 2097184 | tf_op jit(solution)/shard_map/ppermute | solution.py:17
  465.4 45.8 %collective-permute-done.34 = f32[2,2,2,256,256]{4,3,2,1,0:T(8,128)} collective-permute-done((f32[2,2,2,256,256]{4,3,2,1,0:T(8,128)S(1)}, f32[2,2,2,256,256]{4,3,2,1,0:T(8,128)}, u32[]{:S(2)}, u32[]{:S(2)}) %collective-permute-start.34) | collective-permute-done | bytes 2097184 | tf_op jit(solution)/shard_map/ppermute | solution.py:17
  515.6 47.5 %collective-permute-done.35 = f32[2,2,2,256,256]{4,3,2,1,0:T(8,128)} collective-permute-done((f32[2,2,2,256,256]{4,3,2,1,0:T(8,128)}, f32[2,2,2,256,256]{4,3,2,1,0:T(8,128)}, u32[]{:S(2)}, u32[]{:S(2)}) %collective-permute-start.35) | collective-permute-done | bytes 2097184 | tf_op jit(solution)/shard_map/ppermute | solution.py:17
  (172 shorter events, 111.5 us)
Async XLA Ops:
  1.8 26.6 %collective-permute-start = (f32[1,2,2,256,256]{4,3,2,1,0:T(8,128)S(1)}, f32[1,2,2,256,256]{4,3,2,1,0:T(8,128)}, u32[]{:S(2)}, u32[]{:S(2)}) collective-permute-start(f32[1,2,2,256,256]{4,3,2,1,0:T(8,128)S(1)} %multiply_bitcast_fusion), channel_id=1, source_target_pairs={{0,128},{16,144},{32,160},{48,176},{64,192},{80,208},{96,224},{112... | collective-permute-start | bytes 3145736 | tf_op jit(solution)/shard_map/ppermute | solution.py:17
  31.6 46.8 %collective-permute-start.1 = (f32[2,2,2,256,256]{4,3,2,1,0:T(8,128)}, f32[2,2,2,256,256]{4,3,2,1,0:T(8,128)}, u32[]{:S(2)}, u32[]{:S(2)}) collective-permute-start(f32[2,2,2,256,256]{4,3,2,1,0:T(8,128)} %pad_maximum_fusion), channel_id=1, source_target_pairs={{0,64},{16,80},{32,96},{48,112},{64,0},{80,16},{96,32},{112,48},{1... | collective-permute-start | bytes 6291464 | tf_op jit(solution)/shard_map/ppermute | solution.py:17
  81.8 86.0 %collective-permute-start.2 = (f32[2,2,2,256,256]{4,3,2,1,0:T(8,128)S(1)}, f32[2,2,2,256,256]{4,3,2,1,0:T(8,128)}, u32[]{:S(2)}, u32[]{:S(2)}) collective-permute-start(f32[2,2,2,256,256]{4,3,2,1,0:T(8,128)S(1)} %pad_maximum_fusion.1), channel_id=1, source_target_pairs={{0,32},{16,48},{32,0},{48,16},{64,96},{80,112},{96,64},{112,80},{1... | collective-permute-start | bytes 6291464 | tf_op jit(solution)/shard_map/ppermute | solution.py:17
  171.9 5.0 collective-permute-start.3
  197.8 4.0 collective-permute-start.4
  200.6 5.5 collective-permute-start.5
  208.5 12.5 %collective-permute-start.6 = (f32[2,2,258,1]{2,1,3,0:T(2,128)S(1)}, f32[2,2,258,1]{2,1,3,0:T(2,128)S(1)}, u32[]{:S(2)}, u32[]{:S(2)}) collective-permute-start(f32[2,2,258,1]{2,1,3,0:T(2,128)S(1)} %copy.95), channel_id=1, source_target_pairs={{1,0},{2,1},{3,2},{5,4},{6,5},{7,6},{9,8},{10,9},{11,10},{13,12},{... | collective-permute-start | bytes 12392 | tf_op jit(solution)/shard_map/ppermute | solution.py:28
  219.5 5.5 collective-permute-start.7
  229.3 3.8 collective-permute-start.8
  231.7 5.5 collective-permute-start.9
  237.8 4.5 collective-permute-start.10
  241.0 5.5 collective-permute-start.11
  248.9 3.8 collective-permute-start.12
  251.4 5.5 collective-permute-start.13
  257.5 3.5 collective-permute-start.14
  259.7 5.5 collective-permute-start.15
  269.5 5.5 collective-permute-start.17
  275.6 3.5 collective-permute-start.18
  277.8 5.5 collective-permute-start.19
  287.6 5.5 collective-permute-start.21
  293.7 3.5 collective-permute-start.22
  295.9 5.5 collective-permute-start.23
  305.8 5.5 collective-permute-start.25
  311.8 3.5 collective-permute-start.26
  314.0 5.5 collective-permute-start.27
  323.9 5.5 collective-permute-start.29
  330.0 3.5 collective-permute-start.30
  332.2 5.5 collective-permute-start.31
  356.8 4.5 collective-permute-start.32
  363.3 97.7 %collective-permute-start.33 = (f32[2,2,2,256,256]{4,3,2,1,0:T(8,128)}, f32[2,2,2,256,256]{4,3,2,1,0:T(8,128)}, u32[]{:S(2)}, u32[]{:S(2)}) collective-permute-start(f32[2,2,2,256,256]{4,3,2,1,0:T(8,128)} %pad_maximum_fusion.4), channel_id=1, source_target_pairs={{0,32},{16,48},{32,0},{48,16},{64,96},{80,112},{96,64},{112,80},{1... | collective-permute-start | bytes 6291464 | tf_op jit(solution)/shard_map/ppermute | solution.py:17
  464.0 47.2 %collective-permute-start.34 = (f32[2,2,2,256,256]{4,3,2,1,0:T(8,128)S(1)}, f32[2,2,2,256,256]{4,3,2,1,0:T(8,128)}, u32[]{:S(2)}, u32[]{:S(2)}) collective-permute-start(f32[2,2,2,256,256]{4,3,2,1,0:T(8,128)S(1)} %pad_maximum_fusion.5), channel_id=1, source_target_pairs={{0,64},{16,80},{32,96},{48,112},{64,0},{80,16},{96,32},{112,48},{1... | collective-permute-start | bytes 6291464 | tf_op jit(solution)/shard_map/ppermute | solution.py:17
  515.1 48.0 %collective-permute-start.35 = (f32[2,2,2,256,256]{4,3,2,1,0:T(8,128)}, f32[2,2,2,256,256]{4,3,2,1,0:T(8,128)}, u32[]{:S(2)}, u32[]{:S(2)}) collective-permute-start(f32[2,2,2,256,256]{4,3,2,1,0:T(8,128)} %pad_maximum_fusion.6), channel_id=1, source_target_pairs={{0,128},{16,144},{32,160},{48,176},{64,192},{80,208},{96,224},{112... | collective-permute-start | bytes 6291464 | tf_op jit(solution)/shard_map/ppermute | solution.py:17
  (18 other events, 34.7 us)
where the time goes:
time: 571 us; the launch traced here: 566 us
  waiting for transfers between devices  402 us (70%)
  starting transfers between devices  71.7 us (13%)
  other arithmetic  40.6 us (7%)
  matrix products  32.7 us (6%)
  local copies, waits for them, and re-layouts  16.5 us (3%)
    ppermute x8, waiting for transfers between devices, swapped(): return lax.ppermute(value, axis, pairs)  346 us
    ppermute x14, waiting for transfers between devices, padded_2(): before = lax.ppermute(last, axis, up)  56.8 us
    ppermute x14, starting transfers between devices, padded_2(): after = lax.ppermute(leading, axis, down)  38.6 us
    ppermute x14, starting transfers between devices, padded_2(): before = lax.ppermute(last, axis, up)  18.5 us
    ppermute x8, starting transfers between devices, swapped(): return lax.ppermute(value, axis, pairs)  14.6 us
  transfers between devices with their start and end apart: 36, of which 22 were waited for; matrix products, arithmetic and copies ran while one was open for 1% of the time, Pallas kernels for 0%

commit v1 on v0

v1 whole, which is shorter than its diff:
```python
import functools
import math

import jax
import jax.numpy as jnp
import numpy as np
from jax import lax
from jax.experimental import pallas as pl
from jax.experimental.pallas import tpu as pltpu
from jax.sharding import PartitionSpec as P

STEPS = 32
SWEEPS = 8
ALPHA = 0.1
DECAY = math.log(ALPHA) / STEPS
FACTOR = math.exp(DECAY)
AXES = ("tm", "sx", "sy")


def flat(tm, sx, sy):
    return (tm * 4 + sx) * 4 + sy


def device_of(row, col):
    row, col = row % 16, col % 16
    sx, upper, core = row // 4, row // 2 % 2, row % 2
    sy, quarter = col // 4, col % 4
    y = quarter ^ (3 * (sy & 1))
    z = upper ^ (sx & 1)
    return flat(y * 4 + z * 2 + core, sx, sy)


def pairs_of(move):
    return [
        (device_of(row, col), device_of(*move(row, col))) for row in range(16) for col in range(16)
    ]


TO_RIGHT = pairs_of(lambda row, col: (row, col + 1))
TO_LEFT = pairs_of(lambda row, col: (row, col - 1))
TO_CORE = pairs_of(lambda row, col: (row ^ 1, col))
TO_CROSS = pairs_of(lambda row, col: (row - 1 if row % 2 == 0 else row + 1, col))


def lanes(rows):
    return lax.broadcasted_iota(jnp.int32, (rows, 128), 1)


def half_turn(value):
    return pltpu.roll(value, 64, 1)


def pack_left(value, low):
    return jnp.where(low, value[:32], half_turn(value[32:]))


def pack_right(value, low):
    return jnp.where(low, half_turn(value[:32]), value[32:])


def slot_of(info, quarter, upper, core):
    return (quarter ^ info[1]) * 4 + (upper ^ info[2]) * 2 + core


def prepare_kernel(info, weight, forcing, initial, last, out):
    block = pl.program_id(0)
    upper, core = block >> 1, block & 1
    low = lanes(32) < 64
    first = weight[3]
    for side in range(2):
        cols = slice(128 * side, 128 * side + 128)
        first_u = forcing[0, 0, :, cols] + first * (initial[0, :, cols] - ALPHA * last[0, :, cols])
        first_w = forcing[1, 0, :, cols] + first * (initial[1, :, cols] - ALPHA * last[1, :, cols])
        second_u = forcing[0, 1, :, cols]
        second_w = forcing[1, 1, :, cols]
        units = (
            weight[0] * (first_w + first_u),
            weight[1] * (second_w + second_u - first_u),
            -weight[2] * second_u,
        )
        left = slot_of(info, 2 * side, upper, core)
        right = slot_of(info, 2 * side + 1, upper, core)
        for k, unit in enumerate(units):
            out[left, 32 * k : 32 * k + 32, :] = pack_left(unit, low)
            out[right, 32 * k : 32 * k + 32, :] = pack_right(unit, low)


def prepare(info, weight, forcing, initial, last):
    return pl.pallas_call(
        prepare_kernel,
        grid=(4,),
        in_specs=[
            pl.BlockSpec(memory_space=pltpu.SMEM),
            pl.BlockSpec(memory_space=pltpu.SMEM),
            pl.BlockSpec((2, 2, 64, 256), lambda i: (0, 0, i, 0)),
            pl.BlockSpec((2, 64, 256), lambda i: (0, i, 0)),
            pl.BlockSpec((2, 64, 256), lambda i: (0, i, 0)),
        ],
        out_specs=pl.BlockSpec((16, 96, 128), lambda i: (0, 0, 0)),
        out_shape=jax.ShapeDtypeStruct((16, 96, 128), jnp.float32),
        name="prepare",
    )(info, weight, forcing, initial, last)


def scaled(factor, value):
    if abs(factor) < 1e-12:
        return None
    if abs(factor - 1.0) < 1e-12:
        return value
    if abs(factor + 1.0) < 1e-12:
        return -value
    return np.float32(factor) * value


def total_of(terms):
    terms = [term for term in terms if term is not None]
    result = terms[0]
    for term in terms[1:]:
        result = result + term
    return result


def angle(index):
    return 2.0 * math.pi * (index % STEPS) / STEPS


def forward(steps):
    even = [steps[0]] + [steps[n] + steps[32 - n] for n in range(1, 16)] + [steps[16]]
    odd = [None] + [steps[n] - steps[32 - n] for n in range(1, 16)]
    planes = [None] * 32
    for j in range(9):
        cos_even = total_of([scaled(math.cos(angle(j * n)), even[n]) for n in range(0, 17, 2)])
        cos_odd = (
            None if j == 8 else total_of([scaled(math.cos(angle(j * n)), even[n]) for n in range(1, 17, 2)])
        )
        high, lowp = (
            (cos_even, None) if cos_odd is None else (cos_even + cos_odd, cos_even - cos_odd)
        )
        if j == 0:
            planes[0], planes[1] = high, lowp
            continue
        planes[2 * j] = high
        if j < 8:
            planes[2 * (16 - j)] = lowp
        sin_odd = total_of([scaled(math.sin(angle(j * n)), odd[n]) for n in range(1, 16, 2)])
        if j == 8:
            planes[2 * j + 1] = -sin_odd
            continue
        sin_even = total_of([scaled(math.sin(angle(j * n)), odd[n]) for n in range(2, 16, 2)])
        planes[2 * j + 1] = -(sin_even + sin_odd)
        planes[2 * (16 - j) + 1] = sin_even - sin_odd
    return planes


def backward(planes):
    real = [planes[0]] + [planes[2 * j] * 2.0 for j in range(1, 16)] + [planes[1]]
    imag = [None] + [planes[2 * j + 1] * 2.0 for j in range(1, 16)]
    steps = [None] * 32

    def put(n, cosine, sine):
        if n in (0, 16):
            steps[n] = cosine
            return
        steps[n] = cosine - sine
        steps[32 - n] = cosine + sine

    for n in range(9):
        cos_even = total_of([scaled(math.cos(angle(j * n)), real[j]) for j in range(0, 17, 2)])
        if n == 8:
            sine = total_of([scaled(math.sin(angle(j * n)), imag[j]) for j in range(1, 16, 2)])
            put(8, cos_even, sine)
            continue
        cos_odd = total_of([scaled(math.cos(angle(j * n)), real[j]) for j in range(1, 17, 2)])
        if n == 0:
            put(0, cos_even + cos_odd, None)
            put(16, cos_even - cos_odd, None)
            continue
        sin_odd = total_of([scaled(math.sin(angle(j * n)), imag[j]) for j in range(1, 16, 2)])
        sin_even = total_of([scaled(math.sin(angle(j * n)), imag[j]) for j in range(2, 16, 2)])
        put(n, cos_even + cos_odd, sin_even + sin_odd)
        put(16 - n, cos_even - cos_odd, sin_odd - sin_even)
    return steps


def transform_kernel(info, table, cell_class, received, planes_out, left_out, right_out, core_out, cross_out):
    upper, core, quarter = info[3], info[4], info[5]
    low8 = lanes(8) < 64
    lane8 = lanes(8) % 64
    row0 = pl.multiple_of((upper * 2 + core) * 64, 64)
    col0 = pl.multiple_of((quarter >> 1) * 128, 128)
    classes = cell_class[pl.ds(row0, 64), pl.ds(col0, 128)]
    courant = jnp.zeros(classes.shape, jnp.float32)
    for k in range(8):
        courant = jnp.where(classes == k, table[k], courant)
    courant = jnp.where((quarter & 1) == 1, half_turn(courant), courant)
    courant = pack_left(courant, lanes(32) < 64)
    planes_out[32] = courant
    for r in range(4):
        rows = slice(8 * r, 8 * r + 8)
        steps = []
        for t in range(16):
            steps.append(received[t, 8 * r : 8 * r + 8, :] + received[(t + 15) % 16, 64 + 8 * r : 72 + 8 * r, :])
            steps.append(received[t, 32 + 8 * r : 40 + 8 * r, :])
        planes = forward(steps)
        for p in range(32):
            planes_out[p, rows, :] = planes[p]
        planes = planes + [courant[rows]]
        for g in range(5):
            left = jnp.zeros((8, 128), jnp.float32)
            right = left
            for m, plane in enumerate(planes[8 * g : 8 * g + 8]):
                here = (lane8 >= 8 * m) & (lane8 < 8 * m + 8)
                left = jnp.where(here, pltpu.roll(plane, 8 * m, 1) if m else plane, left)
                right = jnp.where(here, pltpu.roll(plane, (8 * m - 56) % 128, 1), right)
            left_out[g, rows, :] = left
            right_out[g, rows, :] = right
        planes = planes + [planes[-1]]
        if r == 0:
            for j in range(17):
                top = jnp.where(low8, planes[2 * j], half_turn(planes[2 * j + 1]))

                @pl.when(core == 0)
                def _():
                    cross_out[j] = top

                @pl.when(core == 1)
                def _():
                    core_out[j] = top

        if r == 3:
            for j in range(17):
                bottom = jnp.where(low8, half_turn(planes[2 * j]), planes[2 * j + 1])

                @pl.when(core == 0)
                def _():
                    core_out[j] = bottom

                @pl.when(core == 1)
                def _():
                    cross_out[j] = bottom


def transform(info, table, cell_class, received):
    shapes = ((33, 32, 128), (5, 32, 128), (5, 32, 128), (17, 8, 128), (17, 8, 128))
    return pl.pallas_call(
        transform_kernel,
        in_specs=[
            pl.BlockSpec(memory_space=pltpu.SMEM),
            pl.BlockSpec(memory_space=pltpu.SMEM),
            pl.BlockSpec(memory_space=pltpu.VMEM),
            pl.BlockSpec(memory_space=pltpu.VMEM),
        ],
        out_specs=[pl.BlockSpec(memory_space=pltpu.VMEM)] * 5,
        out_shape=[jax.ShapeDtypeStruct(shape, jnp.float32) for shape in shapes],
        name="transform",
    )(info, table, cell_class, received)


def around(value):
    rows = value.shape[0]
    return (
        pltpu.roll(value, 1, 0)
        + pltpu.roll(value, rows - 1, 0)
        + pltpu.roll(value, 1, 1)
        + pltpu.roll(value, 127, 1)
    )


def solve_kernel(info, lam, planes, from_left, from_right, from_core, from_cross, out, solved):
    core, row0, col0 = info[4], info[6], info[7]
    low = lanes(32) < 64
    lane32 = lanes(32)
    lane8 = lanes(8)
    is_lower = core == 1

    def halo(index):
        return (
            jnp.where(is_lower, from_core[index], from_cross[index]),
            jnp.where(is_lower, from_cross[index], from_core[index]),
        )

    def turn(value, shift):
        return pltpu.roll(value, shift & 127 if isinstance(shift, int) else lax.rem(shift + 256, 128), 1)

    def merged(lane, centre, right, left):
        value = jnp.where(lane < 64, centre, right)
        return jnp.where(lane < 72, value, jnp.where(lane >= 120, left, 0.0))

    def extended(p, pair, odd, group, offset):
        centre = planes[p]
        right, left = from_right[group], from_left[group]
        top_main, bottom_main = halo(pair)
        if odd:
            top_main, bottom_main = half_turn(top_main), half_turn(bottom_main)
        top_left, bottom_left = halo(17 + group)
        top_right, bottom_right = halo(22 + group)
        return jnp.concatenate(
            [
                merged(lane8, top_main, turn(top_right, -offset), turn(top_left, 56 - offset)),
                merged(lane32, centre, turn(right, 64 - offset), turn(left, 120 - offset)),
                merged(lane32, half_turn(centre), turn(right, -offset), turn(left, 56 - offset)),
                merged(lane8, bottom_main, turn(bottom_right, 64 - offset), turn(bottom_left, 120 - offset)),
            ],
            axis=0,
        )

    def packed(value):
        return jnp.where(low, value[8:40], half_turn(value[40:72]))

    rows = lax.broadcasted_iota(jnp.int32, (80, 128), 0) - 8 + row0
    lane80 = lanes(80)
    cols = jnp.where(lane80 >= 120, lane80 - 128, lane80) + col0
    inside = (rows >= 0) & (rows < 1024) & (cols >= 0) & (cols < 1024) & ((lane80 < 72) | (lane80 >= 120))
    courant = jnp.where(inside, extended(32, 16, False, 4, 0), 0.0)
    inner = jnp.where(inside, 1.0, 0.0)

    for p in range(2):
        g = extended(p, 0, p == 1, 0, 8 * p)
        inverse = inner / (lam[0, p] + 4.0 * courant)
        field = g * inverse
        for _ in range(SWEEPS - 1):
            field = (g + courant * around(field)) * inverse
        solved[p] = packed(field)

    def frequency(j, carry):
        group, offset = j >> 2, (j & 3) * 16
        g_re = extended(2 * j, j, False, group, offset)
        g_im = extended(2 * j + 1, j, True, group, offset + 8)
        diag_re = lam[j, 0] + 4.0 * courant
        diag_im = lam[j, 1]
        scale = inner / (diag_re * diag_re + diag_im * diag_im)
        inv_re = diag_re * scale
        inv_im = -diag_im * scale
        re = g_re * inv_re - g_im * inv_im
        im = g_re * inv_im + g_im * inv_re
        for _ in range(SWEEPS - 1):
            all_re = g_re + courant * around(re)
            all_im = g_im + courant * around(im)
            re = all_re * inv_re - all_im * inv_im
            im = all_re * inv_im + all_im * inv_re
        solved[2 * j] = packed(re)
        solved[2 * j + 1] = packed(im)
        return carry

    lax.fori_loop(1, 16, frequency, 0)

    for r in range(4):
        part = slice(8 * r, 8 * r + 8)
        steps = backward([solved[p, part, :] for p in range(32)])
        for n in range(32):
            value = steps[n] * np.float32(math.exp(-n * DECAY) / STEPS)
            t, second = n // 2, n % 2
            out[t, 32 + 32 * second + 8 * r : 40 + 32 * second + 8 * r, :] = value
            if second:
                before = value * np.float32(ALPHA) if n == 31 else value
                out[(t + 1) % 16, part, :] = before


def solve(info, lam, planes, from_left, from_right, from_core, from_cross):
    return pl.pallas_call(
        solve_kernel,
        in_specs=[pl.BlockSpec(memory_space=pltpu.SMEM)] * 2
        + [pl.BlockSpec(memory_space=pltpu.VMEM)] * 5,
        out_specs=pl.BlockSpec(memory_space=pltpu.VMEM),
        out_shape=jax.ShapeDtypeStruct((16, 96, 128), jnp.float32),
        scratch_shapes=[pltpu.VMEM((32, 32, 128), jnp.float32)],
        name="solve",
    )(info, lam, planes, from_left, from_right, from_core, from_cross)


def finish_kernel(info, weight, received, forcing, initial, last, out):
    block = pl.program_id(0)
    upper, core = block >> 1, block & 1
    low = lanes(32) < 64
    first = weight[3]
    for side in range(2):
        cols = slice(128 * side, 128 * side + 128)
        left = slot_of(info, 2 * side, upper, core)
        right = slot_of(info, 2 * side + 1, upper, core)
        for half in range(2):
            rows = slice(32 * half, 32 * half + 32)
            values = []
            for k in range(3):
                one = received[left, 32 * k : 32 * k + 32, :]
                two = received[right, 32 * k : 32 * k + 32, :]
                if half == 0:
                    values.append(jnp.where(low, one, half_turn(two)))
                else:
                    values.append(jnp.where(low, half_turn(one), two))
            before, now, after = values
            start = forcing[0, 0, rows, cols] + first * (
                initial[0, rows, cols] - ALPHA * last[0, rows, cols]
            )
            out[0, 0, rows, cols] = now
            out[0, 1, rows, cols] = after
            out[1, 0, rows, cols] = now - before - start
            out[1, 1, rows, cols] = after - now - forcing[0, 1, rows, cols]


def finish(info, weight, received, forcing, initial, last):
    return pl.pallas_call(
        finish_kernel,
        grid=(4,),
        in_specs=[
            pl.BlockSpec(memory_space=pltpu.SMEM),
            pl.BlockSpec(memory_space=pltpu.SMEM),
            pl.BlockSpec((16, 96, 128), lambda i: (0, 0, 0)),
            pl.BlockSpec((1, 2, 64, 256), lambda i: (0, 0, i, 0)),
            pl.BlockSpec((1, 64, 256), lambda i: (0, i, 0)),
            pl.BlockSpec((1, 64, 256), lambda i: (0, i, 0)),
        ],
        out_specs=pl.BlockSpec((2, 2, 64, 256), lambda i: (0, 0, i, 0)),
        out_shape=jax.ShapeDtypeStruct((2, 2, 256, 256), jnp.float32),
        name="finish",
    )(info, weight, received, forcing, initial, last)


def lam_squares():
    rows = []
    for j in range(16):
        lam = 1.0 - FACTOR * complex(math.cos(angle(j)), -math.sin(angle(j)))
        square = lam * lam
        rows.append((square.real, square.imag))
    rows[0] = ((1.0 - FACTOR) ** 2, (1.0 + FACTOR) ** 2)
    return np.array(rows, np.float32)


def per_device(forcing, initial, previous_last, cell_class, courant_table):
    tm, sx, sy = (lax.axis_index(axis) for axis in AXES)
    flip_y, flip_z = 3 * (sy & 1), sx & 1
    upper, core, quarter = (tm >> 1 & 1) ^ flip_z, tm & 1, (tm >> 2) ^ flip_y
    row0 = sx * 256 + upper * 128 + core * 64
    col0 = sy * 256 + quarter * 64
    info = jnp.stack([tm, flip_y, flip_z, upper, core, quarter, row0, col0]).astype(jnp.int32)
    powers = jnp.asarray(np.exp(DECAY * np.arange(STEPS + 1)), jnp.float32)
    weight = jnp.concatenate(
        [
            lax.dynamic_slice_in_dim(powers, 2 * tm, 3),
            jnp.where(tm == 0, 1.0, 0.0).astype(jnp.float32)[None],
        ]
    )
    lam = jnp.asarray(lam_squares())
    pieces = prepare(info, weight, forcing, initial, previous_last)
    received = lax.all_to_all(pieces, "tm", 0, 0, tiled=True)
    planes, left, right, to_core, to_cross = transform(info, courant_table, cell_class, received)
    from_left = lax.ppermute(right, AXES, TO_RIGHT)
    from_right = lax.ppermute(left, AXES, TO_LEFT)

    def strip(main, start):
        corners = [
            lax.dynamic_slice_in_dim(value, start, 8, axis=1) for value in (from_left, from_right)
        ]
        return jnp.concatenate([main] + corners, axis=0)

    from_core = lax.ppermute(strip(to_core, 24 * (1 - core)), AXES, TO_CORE)
    from_cross = lax.ppermute(strip(to_cross, 24 * core), AXES, TO_CROSS)
    solved = solve(info, lam, planes, from_left, from_right, from_core, from_cross)
    returned = lax.all_to_all(solved, "tm", 0, 0, tiled=True)
    return finish(info, weight, returned, forcing, initial, previous_last)


def solution(mesh):
    in_specs = (
        P(None, "tm", "sx", "sy"),
        P(None, "sx", "sy"),
        P(None, "sx", "sy"),
        P("sx", "sy"),
        P(),
    )
    out_specs = P(None, "tm", "sx", "sy")
    return jax.shard_map(
        per_device, mesh=mesh, in_specs=in_specs, out_specs=out_specs, check_vma=False
    )
```

time: 571 us -> 110 us (0.19)
  the two profiles are of different devices: /device:TPU:118 before, /device:TPU:33 now
where the time goes in v1:
time: 110 us
  blocking collectives  64.8 us (59%)
  Pallas kernels  26.9 us (24%)
  waiting for transfers between devices  11.3 us (10%)
  starting transfers between devices  3.67 us (3%)
  local copies, waits for them, and re-layouts  2.58 us (2%)
    all_to_all x1, blocking collectives, per_device(): received = lax.all_to_all(pieces, 'tm', 0, 0, tiled=True)  36.1 us
    all_to_all x1, blocking collectives, per_device(): returned = lax.all_to_all(solved, 'tm', 0, 0, tiled=True)  28.7 us
    pallas_call x1, Pallas kernels, solve(): pl.pallas_call(solve_kernel, in_specs=[pl.BlockSpec(memory_space=pltpu.SM...  14.6 us
    ppermute x1, waiting for transfers between devices, per_device(): from_cross = lax.ppermute(strip(to_cross, 24 * core), AXES, TO_CROSS)  7.4 us
    pallas_call x1, Pallas kernels, transform(): pl.pallas_call(transform_kernel, in_specs=[pl.BlockSpec(memory_space=pltp...  4.9 us
    pallas_call x1, Pallas kernels, finish(): pl.pallas_call(finish_kernel, grid=(4,), in_specs=[pl.BlockSpec(memory_sp...  3.92 us
    pallas_call x1, Pallas kernels, prepare(): pl.pallas_call(prepare_kernel, grid=(4,), in_specs=[pl.BlockSpec(memory_s...  3.46 us
  transfers between devices with their start and end apart: 4, of which 4 were waited for; matrix products, arithmetic and copies ran while one was open for 0% of the time, Pallas kernels for 0%

profile of v1, /device:TPU:33, one launch (start us, length us, event | category | flops | bytes accessed | tf_op | source)
XLA Modules:
  0.0 110.0 jit_solution(1098180471378736712)
XLA Ops:
  0.0 0.0 copy-start.6
  0.0 0.7 copy-done.6
  0.7 0.1 dynamic_slice.15
  0.7 0.7 pad_maximum_fusion.2.weight
  1.4 0.6 stack.35.info
  2.0 3.5 %prepare.1 = f32[16,96,128]{2,1,0:T(8,128)} custom-call(s32[8]{0:T(128)} %stack.35.info, f32[4]{0:T(128)} %pad_maximum_fusion.2.weight, f32[2,2,256,256]{3,2,1,0:T(8,128)} %forcing.3, f32[2,256,256]{2,1,0:T(8,128)} %initial.3, f32[2,256,256]{2,1,0:T(8,128)} %last.3), custom_call_target="tpu_custom_call" | custom-call | tf_op jit(solution)/shard_map/prepare/pallas_call | solution.py:89
  5.5 36.1 %all_to_all.10.received = f32[16,96,128]{2,1,0:T(8,128)} all-to-all(f32[16,96,128]{2,1,0:T(8,128)} %prepare.1), channel_id=1, replica_groups=mesh['tm'=16,'sx'=4,'sy'=4] {'tm'}, dimensions={0} | all-to-all | bytes 1572864 | tf_op jit(solution)/shard_map/all_to_all | solution.py:444
  41.6 4.9 %transform.1 = (f32[33,32,128]{2,1,0:T(8,128)}, f32[5,32,128]{2,1,0:T(8,128)}, f32[5,32,128]{2,1,0:T(8,128)}, f32[17,8,128]{2,1,0:T(8,128)}, f32[17,8,128]{2,1,0:T(8,128)}) custom-call(s32[8]{0:T(128)} %stack.35.info, f32[8]{0:T(128)} %table.1, s32[256,256]{1,0:T(8,128)} %cell_class.1, f32[16,96,128]{2,1,0:T(8,128)} %all_to_all.10.received), custom_call_target="tpu_custom_call" | custom-call | tf_op jit(solution)/shard_map/transform/pallas_call | solution.py:245
  46.5 0.7 collective-permute-start
  47.2 0.0 copy-start.5
  47.2 0.7 collective-permute-start.1
  47.9 2.0 %collective-permute-done.from_left = f32[5,32,128]{2,1,0:T(8,128)S(1)} collective-permute-done((f32[5,32,128]{2,1,0:T(8,128)}, f32[5,32,128]{2,1,0:T(8,128)S(1)}, u32[]{:S(2)}, u32[]{:S(2)}) %collective-permute-start) | collective-permute-done | bytes 81952 | tf_op jit(solution)/shard_map/ppermute | solution.py:446
  50.0 0.0 copy-start
  50.0 1.0 collective-permute-done.1.from_right
  51.0 0.0 copy-start.1
  51.0 0.0 copy-done
  51.0 0.0 copy-done.5
  51.0 0.0 copy-start.4
  51.1 0.6 copy-done.1
  51.7 2.1 %collective-permute-start.2 = (f32[27,8,128]{2,1,0:T(8,128)S(1)}, f32[27,8,128]{2,1,0:T(8,128)S(1)}, u32[]{:S(2)}, u32[]{:S(2)}) collective-permute-start(f32[27,8,128]{2,1,0:T(8,128)S(1)} %pad_maximum_fusion), channel_id=1, source_target_pairs={{0,16},{64,80},{128,144},{192,208},{193,209},{129,145},{65,81},{1,... | collective-permute-start | bytes 331784 | tf_op jit(solution)/shard_map/ppermute | solution.py:455
  53.8 0.0 copy-done.4
  53.8 0.1 collective-permute-start.3
  53.9 0.8 collective-permute-done.2.from_core
  54.7 0.0 copy-start.2
  54.7 7.4 %collective-permute-done.3.from_cross = f32[27,8,128]{2,1,0:T(8,128)S(1)} collective-permute-done((f32[27,8,128]{2,1,0:T(8,128)S(1)}, f32[27,8,128]{2,1,0:T(8,128)S(1)}, u32[]{:S(2)}, u32[]{:S(2)}) %collective-permute-start.3) | collective-permute-done | bytes 110624 | tf_op jit(solution)/shard_map/ppermute | solution.py:456
  62.1 0.0 copy-start.3
  62.1 0.0 copy-done.2
  62.1 0.6 copy-done.3
  62.8 14.6 %solve.1 = f32[16,96,128]{2,1,0:T(8,128)} custom-call(s32[8]{0:T(128)} %stack.35.info, f32[16,2]{1,0:T(8,128)} %constant.41.clone.lam, f32[33,32,128]{2,1,0:T(8,128)} %get-tuple-element.10.planes, f32[5,32,128]{2,1,0:T(8,128)} %copy-done, f32[5,32,128]{2,1,0:T(8,128)} %copy-done.1, f32[27,8,128]{2,1,0:T(8,128)} %copy-done.2, f32[27,8,128]{2,1,0:T(8,128)} %copy-done.3), custom_call_target="tpu_custom_call" | custom-call | tf_op jit(solution)/shard_map/solve/pallas_call | solution.py:360
  77.4 28.7 %all_to_all.11.received = f32[16,96,128]{2,1,0:T(8,128)} all-to-all(f32[16,96,128]{2,1,0:T(8,128)} %solve.1), channel_id=1, replica_groups=mesh['tm'=16,'sx'=4,'sy'=4] {'tm'}, dimensions={0} | all-to-all | bytes 1572864 | tf_op jit(solution)/shard_map/all_to_all | solution.py:458
  106.1 3.9 %finish.1 = f32[2,2,256,256]{3,2,1,0:T(8,128)} custom-call(s32[8]{0:T(128)} %stack.35.info, f32[4]{0:T(128)} %pad_maximum_fusion.2.weight, f32[16,96,128]{2,1,0:T(8,128)} %all_to_all.11.received, f32[2,2,256,256]{3,2,1,0:T(8,128)} %forcing.3, f32[2,256,256]{2,1,0:T(8,128)} %initial.3, f32[2,256,256]{2,1,0:T(8,128)} %last.3), custom_call_target="tpu_custom_call" | custom-call | tf_op jit(solution)/shard_map/finish/pallas_call | solution.py:401
  (4 shorter events, 0.0 us)
Async XLA Ops:
  0.0 0.7 copy-start.6
  46.5 3.5 %collective-permute-start = (f32[5,32,128]{2,1,0:T(8,128)}, f32[5,32,128]{2,1,0:T(8,128)S(1)}, u32[]{:S(2)}, u32[]{:S(2)}) collective-permute-start(f32[5,32,128]{2,1,0:T(8,128)} %get-tuple-element.11), channel_id=1, source_target_pairs={{0,64},{64,128},{128,192},{192,193},{193,129},{129,65},{65,1},{1,2... | collective-permute-start | bytes 245768 | tf_op jit(solution)/shard_map/ppermute | solution.py:446
  47.2 3.8 %copy-start.5 = (f32[17,8,128]{2,1,0:T(8,128)S(1)}, f32[17,8,128]{2,1,0:T(8,128)}, u32[]{:S(2)}) copy-start(f32[17,8,128]{2,1,0:T(8,128)} %get-tuple-element.13) | copy-start | bytes 208900
  47.2 3.8 %collective-permute-start.1 = (f32[5,32,128]{2,1,0:T(8,128)}, f32[5,32,128]{2,1,0:T(8,128)S(1)}, u32[]{:S(2)}, u32[]{:S(2)}) collective-permute-start(f32[5,32,128]{2,1,0:T(8,128)} %get-tuple-element.12), channel_id=1, source_target_pairs={{0,3},{64,0},{128,64},{192,128},{193,192},{129,193},{65,129},{1,65... | collective-permute-start | bytes 245768 | tf_op jit(solution)/shard_map/ppermute | solution.py:447
  50.0 1.1 copy-start
  51.0 0.6 copy-start.1
  51.0 2.7 %copy-start.4 = (f32[17,8,128]{2,1,0:T(8,128)S(1)}, f32[17,8,128]{2,1,0:T(8,128)}, u32[]{:S(2)}) copy-start(f32[17,8,128]{2,1,0:T(8,128)} %get-tuple-element.14) | copy-start | bytes 208900
  51.7 3.1 %collective-permute-start.2 = (f32[27,8,128]{2,1,0:T(8,128)S(1)}, f32[27,8,128]{2,1,0:T(8,128)S(1)}, u32[]{:S(2)}, u32[]{:S(2)}) collective-permute-start(f32[27,8,128]{2,1,0:T(8,128)S(1)} %pad_maximum_fusion), channel_id=1, source_target_pairs={{0,16},{64,80},{128,144},{192,208},{193,209},{129,145},{65,81},{1,... | collective-permute-start | bytes 331784 | tf_op jit(solution)/shard_map/ppermute | solution.py:455
  53.8 8.3 %collective-permute-start.3 = (f32[27,8,128]{2,1,0:T(8,128)S(1)}, f32[27,8,128]{2,1,0:T(8,128)S(1)}, u32[]{:S(2)}, u32[]{:S(2)}) collective-permute-start(f32[27,8,128]{2,1,0:T(8,128)S(1)} %pad_maximum_fusion.1), channel_id=1, source_target_pairs={{0,28},{64,92},{128,156},{192,220},{193,221},{129,157},{65,93},{1,... | collective-permute-start | bytes 331784 | tf_op jit(solution)/shard_map/ppermute | solution.py:456
  54.7 7.4 %copy-start.2 = (f32[27,8,128]{2,1,0:T(8,128)}, f32[27,8,128]{2,1,0:T(8,128)S(1)}, u32[]{:S(2)}) copy-start(f32[27,8,128]{2,1,0:T(8,128)S(1)} %collective-permute-done.2.from_core) | copy-start | bytes 331780
  62.1 0.6 copy-start.3

commit v2 on v1

--- a/solution.py
+++ b/solution.py
@@ -1,4 +1,3 @@
-import functools
 import math
 
 import jax
@@ -11,10 +10,12 @@
 
 STEPS = 32
 SWEEPS = 8
+BATCH = 4
 ALPHA = 0.1
 DECAY = math.log(ALPHA) / STEPS
 FACTOR = math.exp(DECAY)
 AXES = ("tm", "sx", "sy")
+VMEM = 16 * 2**20
 
 
 def flat(tm, sx, sy):
@@ -58,48 +59,69 @@
     return jnp.where(low, half_turn(value[:32]), value[32:])
 
 
-def slot_of(info, quarter, upper, core):
-    return (quarter ^ info[1]) * 4 + (upper ^ info[2]) * 2 + core
-
-
-def prepare_kernel(info, weight, forcing, initial, last, out):
-    block = pl.program_id(0)
-    upper, core = block >> 1, block & 1
+def place():
+    tm, sx, sy = (lax.axis_index(axis) for axis in AXES)
+    flip_y, flip_z = 3 * (sy & 1), sx & 1
+    upper, core, quarter = (tm >> 1 & 1) ^ flip_z, tm & 1, (tm >> 2) ^ flip_y
+    row0 = sx * 256 + upper * 128 + core * 64
+    col0 = sy * 256 + quarter * 64
+    return tm, flip_y, flip_z, upper, core, quarter, row0, col0
+
+
+def params():
+    return pltpu.CompilerParams(vmem_limit_bytes=VMEM)
+
+
+def prepare_kernel(forcing, initial, last, out):
+    tm, flip_y, flip_z = place()[:3]
     low = lanes(32) < 64
-    first = weight[3]
-    for side in range(2):
-        cols = slice(128 * side, 128 * side + 128)
-        first_u = forcing[0, 0, :, cols] + first * (initial[0, :, cols] - ALPHA * last[0, :, cols])
-        first_w = forcing[1, 0, :, cols] + first * (initial[1, :, cols] - ALPHA * last[1, :, cols])
-        second_u = forcing[0, 1, :, cols]
-        second_w = forcing[1, 1, :, cols]
-        units = (
-            weight[0] * (first_w + first_u),
-            weight[1] * (second_w + second_u - first_u),
-            -weight[2] * second_u,
-        )
-        left = slot_of(info, 2 * side, upper, core)
-        right = slot_of(info, 2 * side + 1, upper, core)
-        for k, unit in enumerate(units):
-            out[left, 32 * k : 32 * k + 32, :] = pack_left(unit, low)
-            out[right, 32 * k : 32 * k + 32, :] = pack_right(unit, low)
-
-
-def prepare(info, weight, forcing, initial, last):
-    return pl.pallas_call(
+    first = jnp.where(tm == 0, 1.0, 0.0).astype(jnp.float32)
+    weight = jnp.float32(1.0)
+    for bit in range(4):
+        weight = weight * jnp.where((tm >> bit & 1) == 1, math.exp(DECAY * 2 ** (bit + 1)), 1.0).astype(jnp.float32)
+    weight_two = weight * np.float32(FACTOR)
+    weight_three = weight * np.float32(-FACTOR * FACTOR)
+    for upper in range(2):
+        for side in range(2):
+            cols = slice(128 * side, 128 * side + 128)
+            first_u = forcing[0, 0, upper, 0, :, cols] + first * (
+                initial[0, upper, 0, :, cols] - ALPHA * last[0, upper, 0, :, cols]
+            )
+            first_w = forcing[1, 0, upper, 0, :, cols] + first * (
+                initial[1, upper, 0, :, cols] - ALPHA * last[1, upper, 0, :, cols]
+            )
+            second_u = forcing[0, 1, upper, 0, :, cols]
+            second_w = forcing[1, 1, upper, 0, :, cols]
+            units = (
+                weight * (first_w + first_u),
+                weight_two * (second_w + second_u - first_u),
+                weight_three * second_u,
+            )
+            for k, unit in enumerate(units):
+                rows = slice(32 * k, 32 * k + 32)
+                out[(2 * side) ^ flip_y, upper ^ flip_z, 0, rows, :] = pack_left(unit, low)
+                out[(2 * side + 1) ^ flip_y, upper ^ flip_z, 0, rows, :] = pack_right(unit, low)
+
+
+def prepare(forcing, initial, last):
+    pieces = pl.pallas_call(
         prepare_kernel,
-        grid=(4,),
+        grid=(2,),
         in_specs=[
-            pl.BlockSpec(memory_space=pltpu.SMEM),
-            pl.BlockSpec(memory_space=pltpu.SMEM),
-            pl.BlockSpec((2, 2, 64, 256), lambda i: (0, 0, i, 0)),
-            pl.BlockSpec((2, 64, 256), lambda i: (0, i, 0)),
-            pl.BlockSpec((2, 64, 256), lambda i: (0, i, 0)),
+            pl.BlockSpec((2, 2, 2, 1, 64, 256), lambda i: (0, 0, 0, i, 0, 0)),
+            pl.BlockSpec((2, 2, 1, 64, 256), lambda i: (0, 0, i, 0, 0)),
+            pl.BlockSpec((2, 2, 1, 64, 256), lambda i: (0, 0, i, 0, 0)),
         ],
-        out_specs=pl.BlockSpec((16, 96, 128), lambda i: (0, 0, 0)),
-        out_shape=jax.ShapeDtypeStruct((16, 96, 128), jnp.float32),
+        out_specs=pl.BlockSpec((4, 2, 1, 96, 128), lambda i: (0, 0, i, 0, 0)),
+        out_shape=jax.ShapeDtypeStruct((4, 2, 2, 96, 128), jnp.float32),
+        compiler_params=params(),
         name="prepare",
-    )(info, weight, forcing, initial, last)
+    )(
+        forcing.reshape(2, 2, 2, 2, 64, 256),
+        initial.reshape(2, 2, 2, 64, 256),
+        last.reshape(2, 2, 2, 64, 256),
+    )
+    return pieces.reshape(16, 96, 128)
 
 
 def scaled(factor, value):
@@ -182,8 +204,8 @@
     return steps
 
 
-def transform_kernel(info, table, cell_class, received, planes_out, left_out, right_out, core_out, cross_out):
-    upper, core, quarter = info[3], info[4], info[5]
+def transform_kernel(table, cell_class, received, planes_out, left_out, right_out, core_out, cross_out):
+    upper, core, quarter = place()[3:6]
     low8 = lanes(8) < 64
     lane8 = lanes(8) % 64
     row0 = pl.multiple_of((upper * 2 + core) * 64, 64)
@@ -240,34 +262,35 @@
                     cross_out[j] = bottom
 
 
-def transform(info, table, cell_class, received):
+def transform(table, cell_class, received):
     shapes = ((33, 32, 128), (5, 32, 128), (5, 32, 128), (17, 8, 128), (17, 8, 128))
     return pl.pallas_call(
         transform_kernel,
         in_specs=[
-            pl.BlockSpec(memory_space=pltpu.SMEM),
             pl.BlockSpec(memory_space=pltpu.SMEM),
             pl.BlockSpec(memory_space=pltpu.VMEM),
             pl.BlockSpec(memory_space=pltpu.VMEM),
         ],
         out_specs=[pl.BlockSpec(memory_space=pltpu.VMEM)] * 5,
         out_shape=[jax.ShapeDtypeStruct(shape, jnp.float32) for shape in shapes],
+        compiler_params=params(),
         name="transform",
-    )(info, table, cell_class, received)
-
-
-def around(value):
-    rows = value.shape[0]
-    return (
-        pltpu.roll(value, 1, 0)
-        + pltpu.roll(value, rows - 1, 0)
-        + pltpu.roll(value, 1, 1)
-        + pltpu.roll(value, 127, 1)
-    )
-
-
-def solve_kernel(info, lam, planes, from_left, from_right, from_core, from_cross, out, solved):
-    core, row0, col0 = info[4], info[6], info[7]
+    )(table, cell_class, received)
+
+
+def around(field):
+    first = pltpu.roll(field[9], 1, 0)
+    last = pltpu.roll(field[0], 7, 0)
+    above = [first] + field[:9]
+    below = field[1:] + [last]
+    return [
+        (up + down) + (pltpu.roll(own, 1, 1) + pltpu.roll(own, 127, 1))
+        for up, own, down in zip(above, field, below)
+    ]
+
+
+def solve_kernel(lam, planes, from_left, from_right, from_core, from_cross, out, solved, wide, own):
+    core, _, row0, col0 = place()[4:]
     low = lanes(32) < 64
     lane32 = lanes(32)
     lane8 = lanes(8)
@@ -304,45 +327,80 @@
             axis=0,
         )
 
-    def packed(value):
-        return jnp.where(low, value[8:40], half_turn(value[40:72]))
+    def spread(slot, value):
+        wide[slot] = value
+        return [wide[slot, pl.ds(v, 8, stride=10), :] for v in range(10)]
+
+    def keep(p, slot, field):
+        for v in range(10):
+            wide[slot, pl.ds(v, 8, stride=10), :] = field[v]
+        solved[p] = jnp.where(low, wide[slot, 8:40, :], half_turn(wide[slot, 40:72, :]))
 
     rows = lax.broadcasted_iota(jnp.int32, (80, 128), 0) - 8 + row0
     lane80 = lanes(80)
     cols = jnp.where(lane80 >= 120, lane80 - 128, lane80) + col0
     inside = (rows >= 0) & (rows < 1024) & (cols >= 0) & (cols < 1024) & ((lane80 < 72) | (lane80 >= 120))
-    courant = jnp.where(inside, extended(32, 16, False, 4, 0), 0.0)
-    inner = jnp.where(inside, 1.0, 0.0)
-
-    for p in range(2):
-        g = extended(p, 0, p == 1, 0, 8 * p)
-        inverse = inner / (lam[0, p] + 4.0 * courant)
-        field = g * inverse
+    courant = spread(0, jnp.where(inside, extended(32, 16, False, 4, 0), 0.0))
+    inner = spread(1, jnp.where(inside, 1.0, 0.0))
+    for v in range(10):
+        own[0, v] = courant[v]
+        own[1, v] = inner[v]
+
+    def prepared(j, slot, special, group, offset):
+        g_re = spread(2 * slot, extended(2 * j, j, False, group, offset))
+        g_im = spread(2 * slot + 1, extended(2 * j + 1, j, True, group, offset + 8))
+        start_re, start_im, gain_re, gain_im = [], [], [], []
+        for v in range(10):
+            speed, kept = own[0, v], own[1, v]
+            if special:
+                inv_re = kept / (lam[0, 0] + 4.0 * speed)
+                inv_im = kept / (lam[0, 1] + 4.0 * speed)
+                start_re.append(g_re[v] * inv_re)
+                start_im.append(g_im[v] * inv_im)
+            else:
+                diag_re = lam[j, 0] + 4.0 * speed
+                diag_im = lam[j, 1]
+                scale = kept / (diag_re * diag_re + diag_im * diag_im)
+                inv_re = diag_re * scale
+                inv_im = -diag_im * scale
+                start_re.append(g_re[v] * inv_re - g_im[v] * inv_im)
+                start_im.append(g_re[v] * inv_im + g_im[v] * inv_re)
+            gain_re.append(speed * inv_re)
+            gain_im.append(speed * inv_im)
+        return start_re, start_im, gain_re, gain_im
+
+    def swept(special, start_re, start_im, gain_re, gain_im, re, im):
+        all_re, all_im = around(re), around(im)
+        if special:
+            return (
+                [start_re[v] + gain_re[v] * all_re[v] for v in range(10)],
+                [start_im[v] + gain_im[v] * all_im[v] for v in range(10)],
+            )
+        return (
+            [start_re[v] + (gain_re[v] * all_re[v] - gain_im[v] * all_im[v]) for v in range(10)],
+            [start_im[v] + (gain_re[v] * all_im[v] + gain_im[v] * all_re[v]) for v in range(10)],
+        )
+
+    def batch(k, has_special):
+        sets, fields = [], []
+        for i in range(BATCH):
+            special = has_special and i == 0
+            j = k * BATCH + i
+            sets.append((special,) + prepared(j, i, special, j >> 2, (j & 3) * 16))
+            fields.append((sets[i][1], sets[i][2]))
         for _ in range(SWEEPS - 1):
-            field = (g + courant * around(field)) * inverse
-        solved[p] = packed(field)
-
-    def frequency(j, carry):
-        group, offset = j >> 2, (j & 3) * 16
-        g_re = extended(2 * j, j, False, group, offset)
-        g_im = extended(2 * j + 1, j, True, group, offset + 8)
-        diag_re = lam[j, 0] + 4.0 * courant
-        diag_im = lam[j, 1]
-        scale = inner / (diag_re * diag_re + diag_im * diag_im)
-        inv_re = diag_re * scale
-        inv_im = -diag_im * scale
-        re = g_re * inv_re - g_im * inv_im
-        im = g_re * inv_im + g_im * inv_re
-        for _ in range(SWEEPS - 1):
-            all_re = g_re + courant * around(re)
-            all_im = g_im + courant * around(im)
-            re = all_re * inv_re - all_im * inv_im
-            im = all_re * inv_im + all_im * inv_re
-        solved[2 * j] = packed(re)
-        solved[2 * j + 1] = packed(im)
+            fields = [swept(*sets[i], *fields[i]) for i in range(BATCH)]
+        for i in range(BATCH):
+            j = k * BATCH + i
+            keep(2 * j, 2 * i, fields[i][0])
+            keep(2 * j + 1, 2 * i + 1, fields[i][1])
+
+    def later(k, carry):
+        batch(k, False)
         return carry
 
-    lax.fori_loop(1, 16, frequency, 0)
+    batch(0, True)
+    lax.fori_loop(1, 16 // BATCH, later, 0)
 
     for r in range(4):
         part = slice(8 * r, 8 * r + 8)
@@ -356,63 +414,72 @@
                 out[(t + 1) % 16, part, :] = before
 
 
-def solve(info, lam, planes, from_left, from_right, from_core, from_cross):
+def solve(lam, planes, from_left, from_right, from_core, from_cross):
     return pl.pallas_call(
         solve_kernel,
-        in_specs=[pl.BlockSpec(memory_space=pltpu.SMEM)] * 2
+        in_specs=[pl.BlockSpec(memory_space=pltpu.SMEM)]
         + [pl.BlockSpec(memory_space=pltpu.VMEM)] * 5,
         out_specs=pl.BlockSpec(memory_space=pltpu.VMEM),
         out_shape=jax.ShapeDtypeStruct((16, 96, 128), jnp.float32),
-        scratch_shapes=[pltpu.VMEM((32, 32, 128), jnp.float32)],
+        scratch_shapes=[
+            pltpu.VMEM((32, 32, 128), jnp.float32),
+            pltpu.VMEM((2 * BATCH, 80, 128), jnp.float32),
+            pltpu.VMEM((2, 10, 8, 128), jnp.float32),
+        ],
+        compiler_params=params(),
         name="solve",
-    )(info, lam, planes, from_left, from_right, from_core, from_cross)
-
-
-def finish_kernel(info, weight, received, forcing, initial, last, out):
-    block = pl.program_id(0)
-    upper, core = block >> 1, block & 1
+    )(lam, planes, from_left, from_right, from_core, from_cross)
+
+
+def finish_kernel(received, forcing, initial, last, out):
+    tm, flip_y, flip_z = place()[:3]
     low = lanes(32) < 64
-    first = weight[3]
-    for side in range(2):
-        cols = slice(128 * side, 128 * side + 128)
-        left = slot_of(info, 2 * side, upper, core)
-        right = slot_of(info, 2 * side + 1, upper, core)
-        for half in range(2):
-            rows = slice(32 * half, 32 * half + 32)
-            values = []
-            for k in range(3):
-                one = received[left, 32 * k : 32 * k + 32, :]
-                two = received[right, 32 * k : 32 * k + 32, :]
-                if half == 0:
-                    values.append(jnp.where(low, one, half_turn(two)))
-                else:
-                    values.append(jnp.where(low, half_turn(one), two))
-            before, now, after = values
-            start = forcing[0, 0, rows, cols] + first * (
-                initial[0, rows, cols] - ALPHA * last[0, rows, cols]
-            )
-            out[0, 0, rows, cols] = now
-            out[0, 1, rows, cols] = after
-            out[1, 0, rows, cols] = now - before - start
-            out[1, 1, rows, cols] = after - now - forcing[0, 1, rows, cols]
-
-
-def finish(info, weight, received, forcing, initial, last):
-    return pl.pallas_call(
+    first = jnp.where(tm == 0, 1.0, 0.0).astype(jnp.float32)
+    for upper in range(2):
+        for side in range(2):
+            cols = slice(128 * side, 128 * side + 128)
+            for half in range(2):
+                rows = slice(32 * half, 32 * half + 32)
+                values = []
+                for k in range(3):
+                    unit = slice(32 * k, 32 * k + 32)
+                    one = received[(2 * side) ^ flip_y, upper ^ flip_z, 0, unit, :]
+                    two = received[(2 * side + 1) ^ flip_y, upper ^ flip_z, 0, unit, :]
+                    if half == 0:
+                        values.append(jnp.where(low, one, half_turn(two)))
+                    else:
+                        values.append(jnp.where(low, half_turn(one), two))
+                before, now, after = values
+                start = forcing[0, 0, upper, 0, rows, cols] + first * (
+                    initial[0, upper, 0, rows, cols] - ALPHA * last[0, upper, 0, rows, cols]
+                )
+                out[0, 0, upper, 0, rows, cols] = now
+                out[0, 1, upper, 0, rows, cols] = after
+                out[1, 0, upper, 0, rows, cols] = now - before - start
+                out[1, 1, upper, 0, rows, cols] = after - now - forcing[0, 1, upper, 0, rows, cols]
+
+
+def finish(received, forcing, initial, last):
+    result = pl.pallas_call(
         finish_kernel,
-        grid=(4,),
+        grid=(2,),
         in_specs=[
-            pl.BlockSpec(memory_space=pltpu.SMEM),
-            pl.BlockSpec(memory_space=pltpu.SMEM),
-            pl.BlockSpec((16, 96, 128), lambda i: (0, 0, 0)),
-            pl.BlockSpec((1, 2, 64, 256), lambda i: (0, 0, i, 0)),
-            pl.BlockSpec((1, 64, 256), lambda i: (0, i, 0)),
-            pl.BlockSpec((1, 64, 256), lambda i: (0, i, 0)),
+            pl.BlockSpec((4, 2, 1, 96, 128), lambda i: (0, 0, i, 0, 0)),
+            pl.BlockSpec((1, 2, 2, 1, 64, 256), lambda i: (0, 0, 0, i, 0, 0)),
+            pl.BlockSpec((1, 2, 1, 64, 256), lambda i: (0, 0, i, 0, 0)),
+            pl.BlockSpec((1, 2, 1, 64, 256), lambda i: (0, 0, i, 0, 0)),
         ],
-        out_specs=pl.BlockSpec((2, 2, 64, 256), lambda i: (0, 0, i, 0)),
-        out_shape=jax.ShapeDtypeStruct((2, 2, 256, 256), jnp.float32),
+        out_specs=pl.BlockSpec((2, 2, 2, 1, 64, 256), lambda i: (0, 0, 0, i, 0, 0)),
+        out_shape=jax.ShapeDtypeStruct((2, 2, 2, 2, 64, 256), jnp.float32),
+        compiler_params=params(),
         name="finish",
-    )(info, weight, received, forcing, initial, last)
+    )(
+        received.reshape(4, 2, 2, 96, 128),
+        forcing.reshape(2, 2, 2, 2, 64, 256),
+        initial.reshape(2, 2, 2, 64, 256),
+        last.reshape(2, 2, 2, 64, 256),
+    )
+    return result.reshape(2, 2, 256, 256)
 
 
 def lam_squares():
@@ -426,23 +493,11 @@
 
 
 def per_device(forcing, initial, previous_last, cell_class, courant_table):
-    tm, sx, sy = (lax.axis_index(axis) for axis in AXES)
-    flip_y, flip_z = 3 * (sy & 1), sx & 1
-    upper, core, quarter = (tm >> 1 & 1) ^ flip_z, tm & 1, (tm >> 2) ^ flip_y
-    row0 = sx * 256 + upper * 128 + core * 64
-    col0 = sy * 256 + quarter * 64
-    info = jnp.stack([tm, flip_y, flip_z, upper, core, quarter, row0, col0]).astype(jnp.int32)
-    powers = jnp.asarray(np.exp(DECAY * np.arange(STEPS + 1)), jnp.float32)
-    weight = jnp.concatenate(
-        [
-            lax.dynamic_slice_in_dim(powers, 2 * tm, 3),
-            jnp.where(tm == 0, 1.0, 0.0).astype(jnp.float32)[None],
-        ]
-    )
+    core = lax.axis_index("tm") & 1
     lam = jnp.asarray(lam_squares())
-    pieces = prepare(info, weight, forcing, initial, previous_last)
+    pieces = prepare(forcing, initial, previous_last)
     received = lax.all_to_all(pieces, "tm", 0, 0, tiled=True)
-    planes, left, right, to_core, to_cross = transform(info, courant_table, cell_class, received)
+    planes, left, right, to_core, to_cross = transform(courant_table, cell_class, received)
     from_left = lax.ppermute(right, AXES, TO_RIGHT)
     from_right = lax.ppermute(left, AXES, TO_LEFT)
 
@@ -454,9 +509,9 @@
 
     from_core = lax.ppermute(strip(to_core, 24 * (1 - core)), AXES, TO_CORE)
     from_cross = lax.ppermute(strip(to_cross, 24 * core), AXES, TO_CROSS)
-    solved = solve(info, lam, planes, from_left, from_right, from_core, from_cross)
+    solved = solve(lam, planes, from_left, from_right, from_core, from_cross)
     returned = lax.all_to_all(solved, "tm", 0, 0, tiled=True)
-    return finish(info, weight, returned, forcing, initial, previous_last)
+    return finish(returned, forcing, initial, previous_last)
 
 
 def solution(mesh):

time: 110 us -> 95.6 us (0.87)
  Pallas kernels: 26.9 us -> 12.6 us
    pallas_call x1, Pallas kernels: 14.6 us -> 7.27 us  [solve(): pl.pallas_call(solve_kernel, in_specs=[pl.BlockSpec(memory_space=pltpu.SM...]
    pallas_call x2, Pallas kernels: 7.38 us -> 1.96 us  [the longest x1 1.34 us: finish(): pl.pallas_call(finish_kernel, grid=(2,), in_specs=[pl.BlockSpec((4, 2, 1,...]
    pallas_call x1, Pallas kernels: 4.9 us -> 3.34 us  [transform(): pl.pallas_call(transform_kernel, in_specs=[pl.BlockSpec(memory_space=pltp...]
    unnamed x14 -> x18, local copies, waits for them, and re-layouts: 1.89 us -> 3.34 us
where the time goes in v2:
time: 95.6 us; the launch traced here: 95.3 us
  blocking collectives  64.4 us (67%)
  Pallas kernels  12.6 us (13%)
  waiting for transfers between devices  11.1 us (12%)
  starting transfers between devices  3.76 us (4%)
  local copies, waits for them, and re-layouts  3.35 us (4%)
    all_to_all x1, blocking collectives, per_device(): received = lax.all_to_all(pieces, 'tm', 0, 0, tiled=True)  35.9 us
    all_to_all x1, blocking collectives, per_device(): returned = lax.all_to_all(solved, 'tm', 0, 0, tiled=True)  28.5 us
    ppermute x1, waiting for transfers between devices, per_device(): from_cross = lax.ppermute(strip(to_cross, 24 * core), AXES, TO_CROSS)  7.4 us
    pallas_call x1, Pallas kernels, solve(): pl.pallas_call(solve_kernel, in_specs=[pl.BlockSpec(memory_space=pltpu.SM...  7.27 us
    pallas_call x1, Pallas kernels, transform(): pl.pallas_call(transform_kernel, in_specs=[pl.BlockSpec(memory_space=pltp...  3.34 us
    unnamed x18, local copies, waits for them, and re-layouts  3.34 us
    ppermute x1, starting transfers between devices, per_device(): from_core = lax.ppermute(strip(to_core, 24 * (1 - core)), AXES, TO_CORE)  2.2 us
  transfers between devices with their start and end apart: 4, of which 4 were waited for; matrix products, arithmetic and copies ran while one was open for 0% of the time, Pallas kernels for 0%

profile of v2, /device:TPU:33, one launch (start us, length us, event | category | flops | bytes accessed | tf_op | source)
XLA Modules:
  0.0 95.3 jit_solution(7724982153180222973)
XLA Ops:
  0.0 0.0 copy-start
  0.0 1.2 %copy-done = f32[2,2,256,256]{3,2,1,0:T(8,128)S(1)} copy-done((f32[2,2,256,256]{3,2,1,0:T(8,128)S(1)}, f32[2,2,256,256]{3,2,1,0:T(8,128)}, u32[]{:S(2)}) %copy-start) | copy-done | bytes 1048600
  1.2 0.0 copy-start.2
  1.2 1.0 %copy-done.2 = f32[2,256,256]{2,1,0:T(8,128)S(1)} copy-done((f32[2,256,256]{2,1,0:T(8,128)S(1)}, f32[2,256,256]{2,1,0:T(8,128)}, u32[]{:S(2)}) %copy-start.2) | copy-done | bytes 524312
  2.3 0.0 copy-start.4
  2.3 1.0 %copy-done.4 = f32[2,256,256]{2,1,0:T(8,128)S(1)} copy-done((f32[2,256,256]{2,1,0:T(8,128)S(1)}, f32[2,256,256]{2,1,0:T(8,128)}, u32[]{:S(2)}) %copy-start.4) | copy-done | bytes 524312
  3.3 0.6 prepare.1
  3.9 0.0 copy-start.6
  3.9 0.0 copy-start.8
  4.0 35.9 %all_to_all.10.received = f32[16,96,128]{2,1,0:T(8,128)S(1)} all-to-all(f32[16,96,128]{2,1,0:T(8,128)S(1)} %bitcast.8), channel_id=1, replica_groups=mesh['tm'=16,'sx'=4,'sy'=4] {'tm'}, dimensions={0} | all-to-all | bytes 1572864 | tf_op jit(solution)/shard_map/all_to_all | solution.py:499
  39.9 0.0 copy-done.6
  39.9 0.0 copy-done.8
  39.9 3.3 %transform.1 = (f32[33,32,128]{2,1,0:T(8,128)S(1)}, f32[5,32,128]{2,1,0:T(8,128)S(1)}, f32[5,32,128]{2,1,0:T(8,128)S(1)}, f32[17,8,128]{2,1,0:T(8,128)S(1)}, f32[17,8,128]{2,1,0:T(8,128)S(1)}) custom-call(f32[8]{0:T(128)S(1)} %copy-done.8, s32[256,256]{1,0:T(8,128)S(1)} %copy-done.6, f32[16,96,128]{2,1,0:T(8,128)S(1)} %all_to_all.10.received), custom_call_target="tpu_custom_call" | custom-call | tf_op jit(solution)/shard_map/transform/pallas_call | solution.py:267
  43.2 0.7 collective-permute-start
  44.0 0.7 collective-permute-start.1
  44.7 1.8 %collective-permute-done.from_left = f32[5,32,128]{2,1,0:T(8,128)S(1)} collective-permute-done((f32[5,32,128]{2,1,0:T(8,128)S(1)}, f32[5,32,128]{2,1,0:T(8,128)S(1)}, u32[]{:S(2)}, u32[]{:S(2)}) %collective-permute-start) | collective-permute-done | bytes 81952 | tf_op jit(solution)/shard_map/ppermute | solution.py:501
  46.5 1.0 %collective-permute-done.1.from_right = f32[5,32,128]{2,1,0:T(8,128)S(1)} collective-permute-done((f32[5,32,128]{2,1,0:T(8,128)S(1)}, f32[5,32,128]{2,1,0:T(8,128)S(1)}, u32[]{:S(2)}, u32[]{:S(2)}) %collective-permute-start.1) | collective-permute-done | bytes 81952 | tf_op jit(solution)/shard_map/ppermute | solution.py:502
  47.6 2.2 %collective-permute-start.2 = (f32[27,8,128]{2,1,0:T(8,128)S(1)}, f32[27,8,128]{2,1,0:T(8,128)S(1)}, u32[]{:S(2)}, u32[]{:S(2)}) collective-permute-start(f32[27,8,128]{2,1,0:T(8,128)S(1)} %pad_maximum_fusion), channel_id=1, source_target_pairs={{0,16},{64,80},{128,144},{192,208},{193,209},{129,145},{65,81},{1,... | collective-permute-start | bytes 331784 | tf_op jit(solution)/shard_map/ppermute | solution.py:510
  49.8 0.0 copy-start.7
  49.8 0.1 collective-permute-start.3
  49.9 0.8 collective-permute-done.2.from_core
  50.7 7.4 %collective-permute-done.3.from_cross = f32[27,8,128]{2,1,0:T(8,128)S(1)} collective-permute-done((f32[27,8,128]{2,1,0:T(8,128)S(1)}, f32[27,8,128]{2,1,0:T(8,128)S(1)}, u32[]{:S(2)}, u32[]{:S(2)}) %collective-permute-start.3) | collective-permute-done | bytes 110624 | tf_op jit(solution)/shard_map/ppermute | solution.py:511
  58.1 0.0 copy-done.7
  58.1 0.0 copy-start.5
  58.1 7.3 %solve.1 = f32[16,96,128]{2,1,0:T(8,128)S(1)} custom-call(f32[16,2]{1,0:T(8,128)S(1)} %copy-done.7, f32[33,32,128]{2,1,0:T(8,128)S(1)} %get-tuple-element.10.planes, f32[5,32,128]{2,1,0:T(8,128)S(1)} %collective-permute-done.from_left, f32[5,32,128]{2,1,0:T(8,128)S(1)} %collective-permute-done.1.from_right, ...), custom_call_target="tpu_custom_call" | custom-call | tf_op jit(solution)/shard_map/solve/pallas_call | solution.py:418
  65.4 0.0 copy-start.1
  65.4 0.0 copy-start.3
  65.4 28.5 %all_to_all.11 = f32[16,96,128]{2,1,0:T(8,128)S(1)} all-to-all(f32[16,96,128]{2,1,0:T(8,128)S(1)} %solve.1), channel_id=1, replica_groups=mesh['tm'=16,'sx'=4,'sy'=4] {'tm'}, dimensions={0} | all-to-all | bytes 1572864 | tf_op jit(solution)/shard_map/all_to_all | solution.py:513
  93.9 0.0 copy-done.5
  93.9 0.0 copy-done.1
  93.9 0.0 copy-done.3
  94.0 1.3 %finish.1 = f32[2,2,2,2,64,256]{5,4,3,2,1,0:T(8,128)} custom-call(f32[4,2,2,96,128]{4,3,2,1,0:T(8,128)S(1)} %bitcast.9, f32[2,2,2,2,64,256]{5,4,3,2,1,0:T(8,128)S(1)} %bitcast.7, f32[2,2,2,64,256]{4,3,2,1,0:T(8,128)S(1)} %bitcast.11, f32[2,2,2,64,256]{4,3,2,1,0:T(8,128)S(1)} %bitcast.13), custom_call_target="tpu_custom_call" | custom-call | tf_op jit(solution)/shard_map/finish/pallas_call | solution.py:463
  (4 shorter events, 0.0 us)
Async XLA Ops:
  0.0 1.2 %copy-start = (f32[2,2,256,256]{3,2,1,0:T(8,128)S(1)}, f32[2,2,256,256]{3,2,1,0:T(8,128)}, u32[]{:S(2)}) copy-start(f32[2,2,256,256]{3,2,1,0:T(8,128)} %param.6) | copy-start | bytes 3145732
  1.2 1.0 %copy-start.2 = (f32[2,256,256]{2,1,0:T(8,128)S(1)}, f32[2,256,256]{2,1,0:T(8,128)}, u32[]{:S(2)}) copy-start(f32[2,256,256]{2,1,0:T(8,128)} %param.7) | copy-start | bytes 1572868
  2.3 1.0 %copy-start.4 = (f32[2,256,256]{2,1,0:T(8,128)S(1)}, f32[2,256,256]{2,1,0:T(8,128)}, u32[]{:S(2)}) copy-start(f32[2,256,256]{2,1,0:T(8,128)} %param.8) | copy-start | bytes 1572868
  3.9 36.0 %copy-start.6 = (s32[256,256]{1,0:T(8,128)S(1)}, s32[256,256]{1,0:T(8,128)}, u32[]{:S(2)}) copy-start(s32[256,256]{1,0:T(8,128)} %cell_class.1) | copy-start | bytes 786436
  3.9 35.9 %copy-start.8 = (f32[8]{0:T(128)S(1)}, f32[8]{0:T(128)}, u32[]{:S(2)}) copy-start(f32[8]{0:T(128)} %table.1) | copy-start | bytes 100
  43.2 3.3 %collective-permute-start = (f32[5,32,128]{2,1,0:T(8,128)S(1)}, f32[5,32,128]{2,1,0:T(8,128)S(1)}, u32[]{:S(2)}, u32[]{:S(2)}) collective-permute-start(f32[5,32,128]{2,1,0:T(8,128)S(1)} %get-tuple-element.11), channel_id=1, source_target_pairs={{0,64},{64,128},{128,192},{192,193},{193,129},{129,65},{65,1},{1,2... | collective-permute-start | bytes 245768 | tf_op jit(solution)/shard_map/ppermute | solution.py:501
  44.0 3.6 %collective-permute-start.1 = (f32[5,32,128]{2,1,0:T(8,128)S(1)}, f32[5,32,128]{2,1,0:T(8,128)S(1)}, u32[]{:S(2)}, u32[]{:S(2)}) collective-permute-start(f32[5,32,128]{2,1,0:T(8,128)S(1)} %get-tuple-element.12), channel_id=1, source_target_pairs={{0,3},{64,0},{128,64},{192,128},{193,192},{129,193},{65,129},{1,65... | collective-permute-start | bytes 245768 | tf_op jit(solution)/shard_map/ppermute | solution.py:502
  47.6 3.2 %collective-permute-start.2 = (f32[27,8,128]{2,1,0:T(8,128)S(1)}, f32[27,8,128]{2,1,0:T(8,128)S(1)}, u32[]{:S(2)}, u32[]{:S(2)}) collective-permute-start(f32[27,8,128]{2,1,0:T(8,128)S(1)} %pad_maximum_fusion), channel_id=1, source_target_pairs={{0,16},{64,80},{128,144},{192,208},{193,209},{129,145},{65,81},{1,... | collective-permute-start | bytes 331784 | tf_op jit(solution)/shard_map/ppermute | solution.py:510
  49.8 8.4 %copy-start.7 = (f32[16,2]{1,0:T(8,128)S(1)}, f32[16,2]{1,0:T(8,128)}, u32[]{:S(2)}) copy-start(f32[16,2]{1,0:T(8,128)} %constant.15.clone.lam) | copy-start | bytes 388
  49.8 8.3 %collective-permute-start.3 = (f32[27,8,128]{2,1,0:T(8,128)S(1)}, f32[27,8,128]{2,1,0:T(8,128)S(1)}, u32[]{:S(2)}, u32[]{:S(2)}) collective-permute-start(f32[27,8,128]{2,1,0:T(8,128)S(1)} %pad_maximum_fusion.1), channel_id=1, source_target_pairs={{0,28},{64,92},{128,156},{192,220},{193,221},{129,157},{65,93},{1,... | collective-permute-start | bytes 331784 | tf_op jit(solution)/shard_map/ppermute | solution.py:511
  58.1 35.8 %copy-start.5 = (f32[2,256,256]{2,1,0:T(8,128)S(1)}, f32[2,256,256]{2,1,0:T(8,128)}, u32[]{:S(2)}) copy-start(f32[2,256,256]{2,1,0:T(8,128)} %param.8) | copy-start | bytes 1572868
  65.4 28.5 %copy-start.1 = (f32[2,2,256,256]{3,2,1,0:T(8,128)S(1)}, f32[2,2,256,256]{3,2,1,0:T(8,128)}, u32[]{:S(2)}) copy-start(f32[2,2,256,256]{3,2,1,0:T(8,128)} %param.6) | copy-start | bytes 3145732
  65.4 28.5 %copy-start.3 = (f32[2,256,256]{2,1,0:T(8,128)S(1)}, f32[2,256,256]{2,1,0:T(8,128)}, u32[]{:S(2)}) copy-start(f32[2,256,256]{2,1,0:T(8,128)} %param.7) | copy-start | bytes 1572868

commit v3 on v2

v3 whole, which is shorter than its diff:
```python
import math

import jax
import jax.numpy as jnp
import numpy as np
from jax import lax
from jax.experimental import pallas as pl
from jax.experimental.pallas import tpu as pltpu
from jax.sharding import PartitionSpec as P

STEPS = 32
SWEEPS = 8
BATCH = 4
ALPHA = 0.1
DECAY = math.log(ALPHA) / STEPS
FACTOR = math.exp(DECAY)
AXES = ("tm", "sx", "sy")
VMEM = 16 * 2**20


def chip_of(half, upper, inner, odd_x, odd_y):
    half_y, upper_y = half ^ odd_y, upper ^ odd_x
    return (2 * half_y + (upper_y ^ half_y)) * 2 + (inner ^ half)


def device_of(row, col):
    row, col = row % 16, col % 16
    sx, upper, core = row // 4, row // 2 % 2, row % 2
    sy, half, inner = col // 4, col // 2 % 2, col % 2
    tm = chip_of(half, upper, inner, sx & 1, sy & 1) * 2 + core
    return (tm * 4 + sx) * 4 + sy


def pairs_of(move):
    return [
        (device_of(row, col), device_of(*move(row, col))) for row in range(16) for col in range(16)
    ]


def away(index):
    return index - 1 if index % 2 == 0 else index + 1


TO_SIDE = pairs_of(lambda row, col: (row, away(col)))
TO_CORE = pairs_of(lambda row, col: (row ^ 1, col))
TO_CROSS = pairs_of(lambda row, col: (away(row), col))
CHIPS = [[chip * 2 + core for chip in range(8)] for core in range(2)]
CORES = [(tm, tm ^ 1) for tm in range(16)]


def lanes(rows):
    return lax.broadcasted_iota(jnp.int32, (rows, 128), 1)


def half_turn(value):
    return pltpu.roll(value, 64, 1)


def pack_left(value, low):
    return jnp.where(low, value[:32], half_turn(value[32:]))


def pack_right(value, low):
    return jnp.where(low, half_turn(value[:32]), value[32:])


def place():
    tm, sx, sy = (lax.axis_index(axis) for axis in AXES)
    odd_x, odd_y = sx & 1, sy & 1
    y, z, core = tm >> 2, tm >> 1 & 1, tm & 1
    half_y = y >> 1
    upper_y = (y & 1) ^ half_y
    half, upper = half_y ^ odd_y, upper_y ^ odd_x
    inner = z ^ half
    row0 = sx * 256 + upper * 128 + core * 64
    col0 = sy * 256 + half * 128 + inner * 64
    return tm, odd_x, odd_y, core, upper, half, inner, row0, col0


def params():
    return pltpu.CompilerParams(vmem_limit_bytes=VMEM)


def turn(value, shift):
    if isinstance(shift, int):
        return pltpu.roll(value, shift % 128, 1) if shift % 128 else value
    return pltpu.roll(value, lax.rem(shift + 256, 128), 1)


def prepare_kernel(forcing, mine, theirs):
    tm, odd_x, odd_y, own_core = place()[:4]
    low = lanes(32) < 64
    weight = jnp.float32(1.0)
    for bit in range(4):
        step = math.exp(DECAY * 2 ** (bit + 1))
        weight = weight * jnp.where((tm >> bit & 1) == 1, step, 1.0).astype(jnp.float32)
    weight_two = weight * np.float32(FACTOR)
    weight_three = weight * np.float32(-FACTOR * FACTOR)
    for out, core in ((mine, own_core), (theirs, 1 - own_core)):
        for upper in range(2):
            for half in range(2):
                cols = slice(128 * half, 128 * half + 128)
                first_u, second_u = forcing[0, 0, upper, core, :, cols], forcing[0, 1, upper, core, :, cols]
                first_w, second_w = forcing[1, 0, upper, core, :, cols], forcing[1, 1, upper, core, :, cols]
                units = (
                    weight * (first_w + first_u),
                    weight_two * (second_w + second_u - first_u),
                    weight_three * second_u,
                )
                left = chip_of(half, upper, 0, odd_x, odd_y)
                right = chip_of(half, upper, 1, odd_x, odd_y)
                for k, unit in enumerate(units):
                    rows = slice(32 * k, 32 * k + 32)
                    out[left, rows, :] = pack_left(unit, low)
                    out[right, rows, :] = pack_right(unit, low)


def prepare(forcing):
    return pl.pallas_call(
        prepare_kernel,
        in_specs=[pl.BlockSpec(memory_space=pltpu.VMEM)],
        out_specs=[pl.BlockSpec(memory_space=pltpu.VMEM)] * 2,
        out_shape=[jax.ShapeDtypeStruct((8, 96, 128), jnp.float32)] * 2,
        compiler_params=params(),
        name="prepare",
    )(forcing.reshape(2, 2, 2, 2, 64, 256))


def merge_kernel(mine, received, out):
    _, odd_x, odd_y, core = place()[:4]
    is_first = core == 0
    lane8 = lanes(8) % 64
    for chip in range(8):
        for k in range(3):
            rows = slice(32 * k, 32 * k + 32)
            own, other = mine[chip, rows, :], received[chip, rows, :]
            early, late = jnp.where(is_first, own, other), jnp.where(is_first, other, own)
            if k < 2:
                out[chip, 32 * k : 32 * k + 32, :] = early
                kept = late if k == 0 else kept
                if k == 1:
                    out[chip, 96:128, :] = late
            else:
                out[chip, 64:96, :] = kept + early
                out[chip, 128:160, :] = late
    for chip in range(8):
        inner = (chip & 1) ^ (chip >> 2) ^ odd_y
        for tile in range(3):
            value = jnp.zeros((8, 128), jnp.float32)
            for m in range(8):
                k, r = (8 * tile + m) // 4, m % 4
                if k == 5:
                    break
                beside = out[chip ^ 1, 32 * k + 8 * r : 32 * k + 8 * r + 8, :]
                here = (lane8 >= 8 * m) & (lane8 < 8 * m + 8)
                value = jnp.where(here, turn(beside, 8 * m - 56 * inner), value)
            out[chip, 160 + 8 * tile : 168 + 8 * tile, :] = value


def merge(mine, received):
    return pl.pallas_call(
        merge_kernel,
        in_specs=[pl.BlockSpec(memory_space=pltpu.VMEM)] * 2,
        out_specs=pl.BlockSpec(memory_space=pltpu.VMEM),
        out_shape=jax.ShapeDtypeStruct((8, 184, 128), jnp.float32),
        compiler_params=params(),
        name="merge",
    )(mine, received)


def scaled(factor, value):
    if abs(factor) < 1e-12:
        return None
    if abs(factor - 1.0) < 1e-12:
        return value
    if abs(factor + 1.0) < 1e-12:
        return -value
    return np.float32(factor) * value


def total_of(terms):
    terms = [term for term in terms if term is not None]
    result = terms[0]
    for term in terms[1:]:
        result = result + term
    return result


def angle(index):
    return 2.0 * math.pi * (index % STEPS) / STEPS


def forward(steps):
    even = [steps[0]] + [steps[n] + steps[32 - n] for n in range(1, 16)] + [steps[16]]
    odd = [None] + [steps[n] - steps[32 - n] for n in range(1, 16)]
    planes = [None] * 32
    for j in range(9):
        cos_even = total_of([scaled(math.cos(angle(j * n)), even[n]) for n in range(0, 17, 2)])
        cos_odd = (
            None if j == 8 else total_of([scaled(math.cos(angle(j * n)), even[n]) for n in range(1, 17, 2)])
        )
        high, lowp = (
            (cos_even, None) if cos_odd is None else (cos_even + cos_odd, cos_even - cos_odd)
        )
        if j == 0:
            planes[0], planes[1] = high, lowp
            continue
        planes[2 * j] = high
        if j < 8:
            planes[2 * (16 - j)] = lowp
        sin_odd = total_of([scaled(math.sin(angle(j * n)), odd[n]) for n in range(1, 16, 2)])
        if j == 8:
            planes[2 * j + 1] = -sin_odd
            continue
        sin_even = total_of([scaled(math.sin(angle(j * n)), odd[n]) for n in range(2, 16, 2)])
        planes[2 * j + 1] = -(sin_even + sin_odd)
        planes[2 * (16 - j) + 1] = sin_even - sin_odd
    return planes


def backward(planes):
    real = [planes[0]] + [planes[2 * j] * 2.0 for j in range(1, 16)] + [planes[1]]
    imag = [None] + [planes[2 * j + 1] * 2.0 for j in range(1, 16)]
    steps = [None] * 32

    def put(n, cosine, sine):
        if n in (0, 16):
            steps[n] = cosine
            return
        steps[n] = cosine - sine
        steps[32 - n] = cosine + sine

    for n in range(9):
        cos_even = total_of([scaled(math.cos(angle(j * n)), real[j]) for j in range(0, 17, 2)])
        if n == 8:
            sine = total_of([scaled(math.sin(angle(j * n)), imag[j]) for j in range(1, 16, 2)])
            put(8, cos_even, sine)
            continue
        cos_odd = total_of([scaled(math.cos(angle(j * n)), real[j]) for j in range(1, 17, 2)])
        if n == 0:
            put(0, cos_even + cos_odd, None)
            put(16, cos_even - cos_odd, None)
            continue
        sin_odd = total_of([scaled(math.sin(angle(j * n)), imag[j]) for j in range(1, 16, 2)])
        sin_even = total_of([scaled(math.sin(angle(j * n)), imag[j]) for j in range(2, 16, 2)])
        put(n, cos_even + cos_odd, sin_even + sin_odd)
        put(16 - n, cos_even - cos_odd, sin_odd - sin_even)
    return steps


def transform_kernel(
    table, cell_class, initial, last, received, planes_out, beside_out, side_out, core_out, cross_out
):
    _, _, _, core, upper, half, inner = place()[:7]
    low8, low32 = lanes(8) < 64, lanes(32) < 64
    lane8 = lanes(8) % 64
    rows = pl.ds(pl.multiple_of((upper * 2 + core) * 64, 64), 64)
    cols = pl.ds(pl.multiple_of(half * 128, 128), 128)
    is_right = inner == 1

    def slots(m):
        return (lane8 >= 8 * m) & (lane8 < 8 * m + 8)

    def own_and_beside(value):
        turned = half_turn(value)
        own = pack_left(jnp.where(is_right, turned, value), low32)
        other = pack_left(jnp.where(is_right, value, turned), low32)
        beside = jnp.zeros((8, 128), jnp.float32)
        for r in range(4):
            beside = jnp.where(slots(r), turn(other[8 * r : 8 * r + 8], 8 * r - 56 * inner), beside)
        return [own[8 * r : 8 * r + 8] for r in range(4)] + [beside]

    classes = cell_class[rows, cols]
    courant = jnp.zeros(classes.shape, jnp.float32)
    for k in range(8):
        courant = jnp.where(classes == k, table[k], courant)
    courant = own_and_beside(courant)
    start_u, start_w = (
        own_and_beside(initial[c, rows, cols] - ALPHA * last[c, rows, cols]) for c in range(2)
    )

    for r in range(5):
        steps = []
        for t in range(8):
            before = (t + 7) % 8
            if r < 4:
                part = [received[t, 32 * k + 8 * r : 32 * k + 8 * r + 8, :] for k in range(4)]
                part[0] = part[0] + received[before, 128 + 8 * r : 136 + 8 * r, :]
            else:
                one, two = received[t, 160:168, :], received[t, 168:176, :]
                part = [one + received[before, 176:184, :], turn(one, -32), two, turn(two, -32)]
            steps.extend(part)
        steps[0] = steps[0] + (start_w[r] + start_u[r])
        steps[1] = steps[1] - np.float32(FACTOR) * start_u[r]
        planes = forward(steps) + [courant[r]]
        if r == 4:
            for p in range(33):
                beside_out[p] = planes[p]
        else:
            for p in range(33):
                planes_out[p, 8 * r : 8 * r + 8, :] = planes[p]
            for g in range(5):
                value = jnp.zeros((8, 128), jnp.float32)
                for m, plane in enumerate(planes[8 * g : 8 * g + 8]):
                    value = jnp.where(slots(m), turn(plane, 8 * m - 56 * inner), value)
                side_out[g, 8 * r : 8 * r + 8, :] = value
        if r == 0:
            pairs = planes + [planes[32]]
            top = [jnp.where(low8, pairs[2 * j], half_turn(pairs[2 * j + 1])) for j in range(17)]
        if r == 3:
            pairs = planes + [planes[32]]
            bottom = [jnp.where(low8, half_turn(pairs[2 * j]), pairs[2 * j + 1]) for j in range(17)]
        if r == 4:
            for strip, start in ((top, 0), (bottom, 88)):
                for g in range(5):
                    value = jnp.zeros((8, 128), jnp.float32)
                    for m, plane in enumerate(planes[8 * g : 8 * g + 8]):
                        value = jnp.where(slots(m), turn(plane, 8 * m - start), value)
                    strip.append(value)
    for i in range(22):
        core_out[i] = jnp.where(core == 0, bottom[i], top[i])
        cross_out[i] = jnp.where(core == 0, top[i], bottom[i])


def transform(table, cell_class, initial, last, received):
    shapes = ((33, 32, 128), (33, 8, 128), (5, 32, 128), (22, 8, 128), (22, 8, 128))
    return pl.pallas_call(
        transform_kernel,
        in_specs=[pl.BlockSpec(memory_space=pltpu.SMEM)] + [pl.BlockSpec(memory_space=pltpu.VMEM)] * 4,
        out_specs=[pl.BlockSpec(memory_space=pltpu.VMEM)] * 5,
        out_shape=[jax.ShapeDtypeStruct(shape, jnp.float32) for shape in shapes],
        compiler_params=params(),
        name="transform",
    )(table, cell_class, initial, last, received)


def around(field):
    first = pltpu.roll(field[9], 1, 0)
    last = pltpu.roll(field[0], 7, 0)
    above = [first] + field[:9]
    below = field[1:] + [last]
    return [
        (up + down) + (pltpu.roll(own, 1, 1) + pltpu.roll(own, 127, 1))
        for up, own, down in zip(above, field, below)
    ]


def solve_kernel(lam, planes, beside, from_side, from_core, from_cross, out, solved, wide, own):
    core, _, _, inner, row0, col0 = place()[3:]
    low = lanes(32) < 64
    is_lower = core == 1
    side_base = 120 - 56 * inner
    beside_base = 64 + 56 * inner

    def within(lane, base):
        return (lane >= base) & (lane < base + 8)

    side_lanes, beside_lanes = within(lanes(8), side_base), within(lanes(8), beside_base)
    low8 = lanes(8) < 64

    def halo(index):
        return (
            jnp.where(is_lower, from_core[index], from_cross[index]),
            jnp.where(is_lower, from_cross[index], from_core[index]),
        )

    def merged(centre, side, other):
        value = jnp.where(low8, centre, 0.0)
        value = jnp.where(side_lanes, side, value)
        return jnp.where(beside_lanes, other, value)

    def extended(p, pair, odd, group, offset):
        edge = beside[p]
        top_main, bottom_main = halo(pair)
        if odd:
            top_main, bottom_main = half_turn(top_main), half_turn(bottom_main)
        top_beside, bottom_beside = halo(17 + group)
        top_side, bottom_side = halo(22 + group)
        parts = [
            merged(
                top_main,
                turn(top_side, side_base - 64 - offset),
                turn(top_beside, beside_base - offset),
            )
        ]
        for r in range(8):
            part = slice(8 * (r % 4), 8 * (r % 4) + 8)
            centre, shift = planes[p, part, :], 0 if r < 4 else 64
            parts.append(
                merged(
                    turn(centre, shift),
                    turn(from_side[group, part, :], side_base - shift - offset),
                    turn(edge, beside_base - shift - 8 * (r % 4)),
                )
            )
        parts.append(
            merged(
                bottom_main,
                turn(bottom_side, side_base - offset),
                turn(bottom_beside, beside_base - offset),
            )
        )
        return jnp.concatenate(parts, axis=0)

    def spread(slot, value):
        wide[slot] = value
        return [wide[slot, pl.ds(v, 8, stride=10), :] for v in range(10)]

    def keep(p, slot, field):
        for v in range(10):
            wide[slot, pl.ds(v, 8, stride=10), :] = field[v]
        solved[p] = jnp.where(low, wide[slot, 8:40, :], half_turn(wide[slot, 40:72, :]))

    rows = lax.broadcasted_iota(jnp.int32, (80, 128), 0) - 8 + row0
    lane80 = lanes(80)
    cols = jnp.where(lane80 >= 120, lane80 - 128, lane80) + col0
    inside = (rows >= 0) & (rows < 1024) & (cols >= 0) & (cols < 1024) & ((lane80 < 72) | (lane80 >= 120))
    courant = spread(0, jnp.where(inside, extended(32, 16, False, 4, 0), 0.0))
    inner = spread(1, jnp.where(inside, 1.0, 0.0))
    for v in range(10):
        own[0, v] = courant[v]
        own[1, v] = inner[v]

    def prepared(j, slot, special, group, offset):
        g_re = spread(2 * slot, extended(2 * j, j, False, group, offset))
        g_im = spread(2 * slot + 1, extended(2 * j + 1, j, True, group, offset + 8))
        start_re, start_im, gain_re, gain_im = [], [], [], []
        for v in range(10):
            speed, kept = own[0, v], own[1, v]
            if special:
                inv_re = kept / (lam[0, 0] + 4.0 * speed)
                inv_im = kept / (lam[0, 1] + 4.0 * speed)
                start_re.append(g_re[v] * inv_re)
                start_im.append(g_im[v] * inv_im)
            else:
                diag_re = lam[j, 0] + 4.0 * speed
                diag_im = lam[j, 1]
                scale = kept / (diag_re * diag_re + diag_im * diag_im)
                inv_re = diag_re * scale
                inv_im = -diag_im * scale
                start_re.append(g_re[v] * inv_re - g_im[v] * inv_im)
                start_im.append(g_re[v] * inv_im + g_im[v] * inv_re)
            gain_re.append(speed * inv_re)
            gain_im.append(speed * inv_im)
        return start_re, start_im, gain_re, gain_im

    def swept(special, start_re, start_im, gain_re, gain_im, re, im):
        all_re, all_im = around(re), around(im)
        if special:
            return (
                [start_re[v] + gain_re[v] * all_re[v] for v in range(10)],
                [start_im[v] + gain_im[v] * all_im[v] for v in range(10)],
            )
        return (
            [start_re[v] + (gain_re[v] * all_re[v] - gain_im[v] * all_im[v]) for v in range(10)],
            [start_im[v] + (gain_re[v] * all_im[v] + gain_im[v] * all_re[v]) for v in range(10)],
        )

    def batch(k, has_special):
        sets, fields = [], []
        for i in range(BATCH):
            special = has_special and i == 0
            j = k * BATCH + i
            sets.append((special,) + prepared(j, i, special, j >> 2, (j & 3) * 16))
            fields.append((sets[i][1], sets[i][2]))
        for _ in range(SWEEPS - 1):
            fields = [swept(*sets[i], *fields[i]) for i in range(BATCH)]
        for i in range(BATCH):
            j = k * BATCH + i
            keep(2 * j, 2 * i, fields[i][0])
            keep(2 * j + 1, 2 * i + 1, fields[i][1])

    def later(k, carry):
        batch(k, False)
        return carry

    batch(0, True)
    lax.fori_loop(1, 16 // BATCH, later, 0)

    for r in range(4):
        part = slice(8 * r, 8 * r + 8)
        steps = backward([solved[p, part, :] for p in range(32)])
        for n in range(32):
            value = steps[n] * np.float32(math.exp(-n * DECAY) / STEPS)
            t, k = n // 4, n % 4
            out[t, 32 * k + 32 + 8 * r : 32 * k + 40 + 8 * r, :] = value
            if k == 3:
                out[(t + 1) % 8, part, :] = value * np.float32(ALPHA) if n == 31 else value


def solve(lam, planes, beside, from_side, from_core, from_cross):
    return pl.pallas_call(
        solve_kernel,
        in_specs=[pl.BlockSpec(memory_space=pltpu.SMEM)] + [pl.BlockSpec(memory_space=pltpu.VMEM)] * 5,
        out_specs=pl.BlockSpec(memory_space=pltpu.VMEM),
        out_shape=jax.ShapeDtypeStruct((8, 160, 128), jnp.float32),
        scratch_shapes=[
            pltpu.VMEM((32, 32, 128), jnp.float32),
            pltpu.VMEM((2 * BATCH, 80, 128), jnp.float32),
            pltpu.VMEM((2, 10, 8, 128), jnp.float32),
        ],
        compiler_params=params(),
        name="solve",
    )(lam, planes, beside, from_side, from_core, from_cross)


def finish_kernel(returned, received, forcing, initial, last, out):
    tm, odd_x, odd_y, core = place()[:4]
    is_own = pl.program_id(0) == core
    low = lanes(32) < 64
    first = jnp.where(tm == 0, 1.0, 0.0).astype(jnp.float32)

    def unit(chip, k):
        start = pl.multiple_of(64 * core + 32 * k, 32)
        return jnp.where(is_own, returned[chip, pl.ds(start, 32), :], received[chip, 32 * k : 32 * k + 32, :])

    for upper in range(2):
        for half in range(2):
            cols = slice(128 * half, 128 * half + 128)
            left = chip_of(half, upper, 0, odd_x, odd_y)
            right = chip_of(half, upper, 1, odd_x, odd_y)
            ones, twos = ([unit(chip, k) for k in range(3)] for chip in (left, right))
            for part in range(2):
                rows = slice(32 * part, 32 * part + 32)
                if part == 0:
                    values = [jnp.where(low, one, half_turn(two)) for one, two in zip(ones, twos)]
                else:
                    values = [jnp.where(low, half_turn(one), two) for one, two in zip(ones, twos)]
                before, now, after = values
                start = forcing[0, 0, upper, 0, rows, cols] + first * (
                    initial[0, upper, 0, rows, cols] - ALPHA * last[0, upper, 0, rows, cols]
                )
                out[0, 0, upper, 0, rows, cols] = now
                out[0, 1, upper, 0, rows, cols] = after
                out[1, 0, upper, 0, rows, cols] = now - before - start
                out[1, 1, upper, 0, rows, cols] = after - now - forcing[0, 1, upper, 0, rows, cols]


def finish(returned, received, forcing, initial, last):
    result = pl.pallas_call(
        finish_kernel,
        grid=(2,),
        in_specs=[
            pl.BlockSpec((8, 160, 128), lambda i: (0, 0, 0)),
            pl.BlockSpec((8, 96, 128), lambda i: (0, 0, 0)),
            pl.BlockSpec((1, 2, 2, 1, 64, 256), lambda i: (0, 0, 0, i, 0, 0)),
            pl.BlockSpec((1, 2, 1, 64, 256), lambda i: (0, 0, i, 0, 0)),
            pl.BlockSpec((1, 2, 1, 64, 256), lambda i: (0, 0, i, 0, 0)),
        ],
        out_specs=pl.BlockSpec((2, 2, 2, 1, 64, 256), lambda i: (0, 0, 0, i, 0, 0)),
        out_shape=jax.ShapeDtypeStruct((2, 2, 2, 2, 64, 256), jnp.float32),
        compiler_params=params(),
        name="finish",
    )(
        returned,
        received,
        forcing.reshape(2, 2, 2, 2, 64, 256),
        initial.reshape(2, 2, 2, 64, 256),
        last.reshape(2, 2, 2, 64, 256),
    )
    return result.reshape(2, 2, 256, 256)


def lam_squares():
    rows = []
    for j in range(16):
        lam = 1.0 - FACTOR * complex(math.cos(angle(j)), -math.sin(angle(j)))
        square = lam * lam
        rows.append((square.real, square.imag))
    rows[0] = ((1.0 - FACTOR) ** 2, (1.0 + FACTOR) ** 2)
    return np.array(rows, np.float32)


def chips_exchange(pieces):
    return lax.all_to_all(pieces, "tm", 0, 0, axis_index_groups=CHIPS, tiled=True)


def per_device(forcing, initial, previous_last, cell_class, courant_table):
    core = lax.axis_index("tm") & 1
    lam = jnp.asarray(lam_squares())
    mine, theirs = prepare(forcing)
    received = chips_exchange(merge(mine, lax.ppermute(theirs, "tm", CORES)))
    planes, beside, side, to_core, to_cross = transform(
        courant_table, cell_class, initial, previous_last, received
    )
    from_side = lax.ppermute(side, AXES, TO_SIDE)

    def strip(main, start):
        return jnp.concatenate([main, lax.dynamic_slice_in_dim(from_side, start, 8, axis=1)], axis=0)

    from_core = lax.ppermute(strip(to_core, 24 * (1 - core)), AXES, TO_CORE)
    from_cross = lax.ppermute(strip(to_cross, 24 * core), AXES, TO_CROSS)
    returned = chips_exchange(solve(lam, planes, beside, from_side, from_core, from_cross))
    wanted = lax.dynamic_slice_in_dim(returned, 64 * (1 - core), 96, axis=1)
    other = lax.ppermute(wanted, "tm", CORES)
    return finish(returned, other, forcing, initial, previous_last)


def solution(mesh):
    in_specs = (
        P(None, "tm", "sx", "sy"),
        P(None, "sx", "sy"),
        P(None, "sx", "sy"),
        P("sx", "sy"),
        P(),
    )
    out_specs = P(None, "tm", "sx", "sy")
    return jax.shard_map(
        per_device, mesh=mesh, in_specs=in_specs, out_specs=out_specs, check_vma=False
    )
```

time: 95.6 us -> 87 us (0.910)
  blocking collectives: 64.4 us -> 33.6 us
  waiting for transfers between devices: 11.1 us -> 31 us
  starting transfers between devices: 3.76 us -> 9.21 us
  local copies, waits for them, and re-layouts: 3.35 us -> 1.29 us
  Pallas kernels: 12.6 us -> 11.2 us
    all_to_all x2 -> x1, blocking collectives: 64.4 us -> 33.6 us  [chips_exchange(): lax.all_to_all(pieces, 'tm', 0, 0, axis_index_groups=CHIPS, tiled=True)]
    all_to_all x0 -> x1, waiting for transfers between devices: none -> 21.6 us  [chips_exchange(): lax.all_to_all(pieces, 'tm', 0, 0, axis_index_groups=CHIPS, tiled=True)]
    ppermute x1, waiting for transfers between devices: 7.4 us -> 3.61 us  [per_device(): from_cross = lax.ppermute(strip(to_cross, 24 * core), AXES, TO_CROSS)]
    all_to_all x0 -> x1, starting transfers between devices: none -> 3.67 us  [chips_exchange(): lax.all_to_all(pieces, 'tm', 0, 0, axis_index_groups=CHIPS, tiled=True)]
    ppermute x2 -> x3, waiting for transfers between devices: 2.85 us -> 5.23 us  [the longest x1 2.53 us: per_device(): from_side = lax.ppermute(side, AXES, TO_SIDE)]
    pallas_call x1, Pallas kernels: 3.34 us -> 1.23 us  [transform(): pl.pallas_call(transform_kernel, in_specs=[pl.BlockSpec(memory_space=pltp...]
    unnamed x18 -> x14, local copies, waits for them, and re-layouts: 3.34 us -> 1.26 us
    ppermute x2 -> x3, starting transfers between devices: 1.47 us -> 2.19 us  [the longest x1 0.84 us: per_device(): from_side = lax.ppermute(side, AXES, TO_SIDE)]
  transfers between devices with their start and end apart: 4 -> 6, of which waited for: 4 -> 6; matrix products, arithmetic and copies ran while one was open for 0% -> 0% of each run, Pallas kernels for 0% -> 0%
where the time goes in v3:
time: 87 us; the launch traced here: 86.4 us
  blocking collectives  33.6 us (39%)
  waiting for transfers between devices  31 us (36%)
  Pallas kernels  11.2 us (13%)
  starting transfers between devices  9.21 us (11%)
  local copies, waits for them, and re-layouts  1.29 us (1%)
    all_to_all x1, blocking collectives, chips_exchange(): lax.all_to_all(pieces, 'tm', 0, 0, axis_index_groups=CHIPS, tiled=True)  33.6 us
    all_to_all x1, waiting for transfers between devices, chips_exchange(): lax.all_to_all(pieces, 'tm', 0, 0, axis_index_groups=CHIPS, tiled=True)  21.6 us
    pallas_call x1, Pallas kernels, solve(): pl.pallas_call(solve_kernel, in_specs=[pl.BlockSpec(memory_space=pltpu.SM...  8.11 us
    all_to_all x1, starting transfers between devices, chips_exchange(): lax.all_to_all(pieces, 'tm', 0, 0, axis_index_groups=CHIPS, tiled=True)  3.67 us
    ppermute x1, waiting for transfers between devices, per_device(): from_cross = lax.ppermute(strip(to_cross, 24 * core), AXES, TO_CROSS)  3.61 us
    ppermute x1, starting transfers between devices, per_device(): from_core = lax.ppermute(strip(to_core, 24 * (1 - core)), AXES, TO_CORE)  2.95 us
    ppermute x1, waiting for transfers between devices, per_device(): from_side = lax.ppermute(side, AXES, TO_SIDE)  2.53 us
  transfers between devices with their start and end apart: 6, of which 6 were waited for; matrix products, arithmetic and copies ran while one was open for 0% of the time, Pallas kernels for 0%

profile of v3, /device:TPU:33, one launch (start us, length us, event | category | flops | bytes accessed | tf_op | source)
XLA Modules:
  0.0 86.4 jit_solution(10105066401233809413)
XLA Ops:
  0.0 0.0 copy-start
  0.0 1.2 %copy-done = f32[2,2,256,256]{3,2,1,0:T(8,128)S(1)} copy-done((f32[2,2,256,256]{3,2,1,0:T(8,128)S(1)}, f32[2,2,256,256]{3,2,1,0:T(8,128)}, u32[]{:S(2)}) %copy-start) | copy-done | bytes 1048600
  1.2 0.3 prepare.1
  1.5 0.8 collective-permute-start
  2.3 1.3 %collective-permute-done.received = f32[8,96,128]{2,1,0:T(8,128)S(1)} collective-permute-done((f32[8,96,128]{2,1,0:T(8,128)S(1)}, f32[8,96,128]{2,1,0:T(8,128)S(1)}, u32[]{:S(2)}, u32[]{:S(2)}) %collective-permute-start) | collective-permute-done | bytes 393248 | tf_op jit(solution)/shard_map/ppermute | solution.py:582
  3.6 0.2 merge.1
  3.9 0.0 copy-start.2
  3.9 0.0 copy-start.3
  3.9 0.0 copy-start.4
  3.9 0.0 copy-start.6
  3.9 33.6 %all_to_all.10.received = f32[8,184,128]{2,1,0:T(8,128)S(1)} all-to-all(f32[8,184,128]{2,1,0:T(8,128)S(1)} %merge.1), channel_id=1, replica_groups={{0,32,64,96,128,160,192,224},{16,48,80,112,144,176,208,240},{1,33,65,97..., dimensions={0} | all-to-all | bytes 1507328 | tf_op jit(solution)/shard_map/all_to_all | solution.py:575
  37.5 0.0 copy-done.2
  37.5 0.0 copy-done.3
  37.5 0.0 copy-done.4
  37.5 0.0 copy-done.6
  37.6 1.2 %transform.1 = (f32[33,32,128]{2,1,0:T(8,128)S(1)}, f32[33,8,128]{2,1,0:T(8,128)S(1)}, f32[5,32,128]{2,1,0:T(8,128)S(1)}, f32[22,8,128]{2,1,0:T(8,128)S(1)}, f32[22,8,128]{2,1,0:T(8,128)S(1)}) custom-call(f32[8]{0:T(128)S(1)} %copy-done.6, s32[256,256]{1,0:T(8,128)S(1)} %copy-done.4, f32[2,256,256]{2,1,0:T(8,128)S(1)} %copy-done.2, ...), custom_call_target="tpu_custom_call" | custom-call | tf_op jit(solution)/shard_map/transform/pallas_call | solution.py:327
  38.8 0.8 collective-permute-start.1
  39.6 2.5 %collective-permute-done.1.from_side = f32[5,32,128]{2,1,0:T(8,128)S(1)} collective-permute-done((f32[5,32,128]{2,1,0:T(8,128)S(1)}, f32[5,32,128]{2,1,0:T(8,128)S(1)}, u32[]{:S(2)}, u32[]{:S(2)}) %collective-permute-start.1) | collective-permute-done | bytes 81952 | tf_op jit(solution)/shard_map/ppermute | solution.py:586
  42.2 2.9 %collective-permute-start.2 = (f32[27,8,128]{2,1,0:T(8,128)S(1)}, f32[27,8,128]{2,1,0:T(8,128)S(1)}, u32[]{:S(2)}, u32[]{:S(2)}) collective-permute-start(f32[27,8,128]{2,1,0:T(8,128)S(1)} %pad_maximum_fusion), channel_id=1, source_target_pairs={{0,16},{32,48},{224,240},{192,208},{193,209},{225,241},{33,49},{1,... | collective-permute-start | bytes 331784 | tf_op jit(solution)/shard_map/ppermute | solution.py:591
  45.1 0.0 copy-start.5
  45.1 0.4 collective-permute-start.3
  45.6 0.5 collective-permute-done.2.from_core
  46.1 3.6 %collective-permute-done.3.from_cross = f32[27,8,128]{2,1,0:T(8,128)S(1)} collective-permute-done((f32[27,8,128]{2,1,0:T(8,128)S(1)}, f32[27,8,128]{2,1,0:T(8,128)S(1)}, u32[]{:S(2)}, u32[]{:S(2)}) %collective-permute-start.3) | collective-permute-done | bytes 110624 | tf_op jit(solution)/shard_map/ppermute | solution.py:592
  49.7 0.0 copy-done.5
  49.7 8.1 %solve.1 = f32[8,160,128]{2,1,0:T(8,128)} custom-call(f32[16,2]{1,0:T(8,128)S(1)} %copy-done.5, f32[33,32,128]{2,1,0:T(8,128)S(1)} %get-tuple-element.14.planes, f32[33,8,128]{2,1,0:T(8,128)S(1)} %get-tuple-element.15.beside, f32[5,32,128]{2,1,0:T(8,128)S(1)} %collective-permute-done.1.from_side, f32[27,8,128]{2,1,0:T(8,128)S(1)} %collective-permute-done.2.from_core, ...), custom_call_target="tpu_custom_call" | custom-call | tf_op jit(solution)/shard_map/solve/pallas_call | solution.py:492
  57.8 0.0 copy-start.1
  57.8 3.7 %all-to-all-start.1 = ((f32[8,160,128]{2,1,0:T(8,128)}), f32[8,160,128]{2,1,0:T(8,128)S(1)}, u32[]{:S(2)}, u32[]{:S(2)}) async-start(f32[8,160,128]{2,1,0:T(8,128)} %solve.1), calls=%async_computation.1 | async-start | bytes 1310720 | tf_op jit(solution)/shard_map/all_to_all | solution.py:575
  61.5 21.6 %all-to-all-done.1.returned = f32[8,160,128]{2,1,0:T(8,128)S(1)} async-done(((f32[8,160,128]{2,1,0:T(8,128)}), f32[8,160,128]{2,1,0:T(8,128)S(1)}, u32[]{:S(2)}, u32[]{:S(2)}) %all-to-all-start.1) | async-done | bytes 655392 | tf_op jit(solution)/shard_map/all_to_all | solution.py:575
  83.1 0.6 collective-permute-start.4
  83.7 1.3 %collective-permute-done.4.received = f32[8,96,128]{2,1,0:T(8,128)S(1)} collective-permute-done((f32[8,96,128]{2,1,0:T(8,128)S(1)}, f32[8,96,128]{2,1,0:T(8,128)S(1)}, u32[]{:S(2)}, u32[]{:S(2)}) %collective-permute-start.4) | collective-permute-done | bytes 393248 | tf_op jit(solution)/shard_map/ppermute | solution.py:595
  85.1 0.0 copy-done.1
  85.1 1.3 %finish.1 = f32[2,2,2,2,64,256]{5,4,3,2,1,0:T(8,128)} custom-call(f32[8,160,128]{2,1,0:T(8,128)S(1)} %all-to-all-done.1.returned, f32[8,96,128]{2,1,0:T(8,128)S(1)} %collective-permute-done.4.received, f32[2,2,2,2,64,256]{5,4,3,2,1,0:T(8,128)S(1)} %bitcast.5, f32[2,2,2,64,256]{4,3,2,1,0:T(8,128)S(1)} %bitcast.6, f32[2,2,2,64,256]{4,3,2,1,0:T(8,128)S(1)} %bitcast.7), custom_call_target="tpu_custom_call" | custom-call | tf_op jit(solution)/shard_map/finish/pallas_call | solution.py:540
  (4 shorter events, 0.0 us)
Async XLA Ops:
  0.0 1.2 %copy-start = (f32[2,2,256,256]{3,2,1,0:T(8,128)S(1)}, f32[2,2,256,256]{3,2,1,0:T(8,128)}, u32[]{:S(2)}) copy-start(f32[2,2,256,256]{3,2,1,0:T(8,128)} %param.6) | copy-start | bytes 3145732
  1.5 2.1 %collective-permute-start = (f32[8,96,128]{2,1,0:T(8,128)S(1)}, f32[8,96,128]{2,1,0:T(8,128)S(1)}, u32[]{:S(2)}, u32[]{:S(2)}) collective-permute-start(f32[8,96,128]{2,1,0:T(8,128)S(1)} %get-tuple-element.13), channel_id=1, source_target_pairs={{0,16},{16,0},{32,48},{48,32},{64,80},{80,64},{96,112},{112,96},{1... | collective-permute-start | bytes 1179656 | tf_op jit(solution)/shard_map/ppermute | solution.py:582
  3.9 33.7 %copy-start.2 = (f32[2,256,256]{2,1,0:T(8,128)S(1)}, f32[2,256,256]{2,1,0:T(8,128)}, u32[]{:S(2)}) copy-start(f32[2,256,256]{2,1,0:T(8,128)} %initial.1) | copy-start | bytes 1572868
  3.9 33.7 %copy-start.3 = (f32[2,256,256]{2,1,0:T(8,128)S(1)}, f32[2,256,256]{2,1,0:T(8,128)}, u32[]{:S(2)}) copy-start(f32[2,256,256]{2,1,0:T(8,128)} %last.1) | copy-start | bytes 1572868
  3.9 33.6 %copy-start.4 = (s32[256,256]{1,0:T(8,128)S(1)}, s32[256,256]{1,0:T(8,128)}, u32[]{:S(2)}) copy-start(s32[256,256]{1,0:T(8,128)} %cell_class.1) | copy-start | bytes 786436
  3.9 33.6 %copy-start.6 = (f32[8]{0:T(128)S(1)}, f32[8]{0:T(128)}, u32[]{:S(2)}) copy-start(f32[8]{0:T(128)} %table.1) | copy-start | bytes 100
  38.8 3.4 %collective-permute-start.1 = (f32[5,32,128]{2,1,0:T(8,128)S(1)}, f32[5,32,128]{2,1,0:T(8,128)S(1)}, u32[]{:S(2)}, u32[]{:S(2)}) collective-permute-start(f32[5,32,128]{2,1,0:T(8,128)S(1)} %get-tuple-element.16), channel_id=1, source_target_pairs={{0,3},{32,224},{224,32},{192,193},{193,192},{225,33},{33,225},{1,2... | collective-permute-start | bytes 245768 | tf_op jit(solution)/shard_map/ppermute | solution.py:586
  42.2 3.9 %collective-permute-start.2 = (f32[27,8,128]{2,1,0:T(8,128)S(1)}, f32[27,8,128]{2,1,0:T(8,128)S(1)}, u32[]{:S(2)}, u32[]{:S(2)}) collective-permute-start(f32[27,8,128]{2,1,0:T(8,128)S(1)} %pad_maximum_fusion), channel_id=1, source_target_pairs={{0,16},{32,48},{224,240},{192,208},{193,209},{225,241},{33,49},{1,... | collective-permute-start | bytes 331784 | tf_op jit(solution)/shard_map/ppermute | solution.py:591
  45.1 4.6 %copy-start.5 = (f32[16,2]{1,0:T(8,128)S(1)}, f32[16,2]{1,0:T(8,128)}, u32[]{:S(2)}) copy-start(f32[16,2]{1,0:T(8,128)} %constant.19.clone.lam) | copy-start | bytes 388
  45.1 4.6 %collective-permute-start.3 = (f32[27,8,128]{2,1,0:T(8,128)S(1)}, f32[27,8,128]{2,1,0:T(8,128)S(1)}, u32[]{:S(2)}, u32[]{:S(2)}) collective-permute-start(f32[27,8,128]{2,1,0:T(8,128)S(1)} %pad_maximum_fusion.1), channel_id=1, source_target_pairs={{0,28},{32,60},{224,252},{192,220},{193,221},{225,253},{33,61},{1,... | collective-permute-start | bytes 331784 | tf_op jit(solution)/shard_map/ppermute | solution.py:592
  57.8 27.3 %copy-start.1 = (f32[2,2,256,256]{3,2,1,0:T(8,128)S(1)}, f32[2,2,256,256]{3,2,1,0:T(8,128)}, u32[]{:S(2)}) copy-start(f32[2,2,256,256]{3,2,1,0:T(8,128)} %param.6) | copy-start | bytes 3145732
  57.8 25.3 %all-to-all-start.1 = ((f32[8,160,128]{2,1,0:T(8,128)}), f32[8,160,128]{2,1,0:T(8,128)S(1)}, u32[]{:S(2)}, u32[]{:S(2)}) async-start(f32[8,160,128]{2,1,0:T(8,128)} %solve.1), calls=%async_computation.1 | async-start | bytes 1310720 | tf_op jit(solution)/shard_map/all_to_all | solution.py:575
  83.1 1.9 %collective-permute-start.4 = (f32[8,96,128]{2,1,0:T(8,128)S(1)}, f32[8,96,128]{2,1,0:T(8,128)S(1)}, u32[]{:S(2)}, u32[]{:S(2)}) collective-permute-start(f32[8,96,128]{2,1,0:T(8,128)S(1)} %constant_dynamic-slice_fusion), channel_id=1, source_target_pairs={{0,16},{16,0},{32,48},{48,32},{64,80},{80,64},{96,112},{112,96},{1... | collective-permute-start | bytes 1179656 | tf_op jit(solution)/shard_map/ppermute | solution.py:595

commit v4 on v3

--- a/solution.py
+++ b/solution.py
@@ -1,3 +1,4 @@
+import functools
 import math
 
 import jax
@@ -10,7 +11,7 @@
 
 STEPS = 32
 SWEEPS = 8
-BATCH = 4
+BATCH = 8
 ALPHA = 0.1
 DECAY = math.log(ALPHA) / STEPS
 FACTOR = math.exp(DECAY)
@@ -41,7 +42,11 @@
     return index - 1 if index % 2 == 0 else index + 1
 
 
-TO_SIDE = pairs_of(lambda row, col: (row, away(col)))
+def side_of(row, col):
+    return (row, away(col)) if 0 < col < 15 else (row ^ 1, col)
+
+
+TO_SIDE = pairs_of(side_of)
 TO_CORE = pairs_of(lambda row, col: (row ^ 1, col))
 TO_CROSS = pairs_of(lambda row, col: (away(row), col))
 CHIPS = [[chip * 2 + core for chip in range(8)] for core in range(2)]
@@ -81,14 +86,25 @@
     return pltpu.CompilerParams(vmem_limit_bytes=VMEM)
 
 
+def cost(size):
+    return pl.CostEstimate(flops=size, bytes_accessed=size, transcendentals=0)
+
+
 def turn(value, shift):
     if isinstance(shift, int):
         return pltpu.roll(value, shift % 128, 1) if shift % 128 else value
     return pltpu.roll(value, lax.rem(shift + 256, 128), 1)
 
 
-def prepare_kernel(forcing, mine, theirs):
-    tm, odd_x, odd_y, own_core = place()[:4]
+def prepare_kernel(other, forcing, out, held, arrived):
+    tm, odd_x, odd_y, core = place()[:4]
+    core = core ^ other
+    copies = []
+    for upper in range(2):
+        copies.append(
+            pltpu.make_async_copy(forcing.at[:, :, upper, core], held.at[upper], arrived.at[upper])
+        )
+        copies[upper].start()
     low = lanes(32) < 64
     weight = jnp.float32(1.0)
     for bit in range(4):
@@ -96,33 +112,35 @@
         weight = weight * jnp.where((tm >> bit & 1) == 1, step, 1.0).astype(jnp.float32)
     weight_two = weight * np.float32(FACTOR)
     weight_three = weight * np.float32(-FACTOR * FACTOR)
-    for out, core in ((mine, own_core), (theirs, 1 - own_core)):
-        for upper in range(2):
-            for half in range(2):
-                cols = slice(128 * half, 128 * half + 128)
-                first_u, second_u = forcing[0, 0, upper, core, :, cols], forcing[0, 1, upper, core, :, cols]
-                first_w, second_w = forcing[1, 0, upper, core, :, cols], forcing[1, 1, upper, core, :, cols]
-                units = (
-                    weight * (first_w + first_u),
-                    weight_two * (second_w + second_u - first_u),
-                    weight_three * second_u,
-                )
-                left = chip_of(half, upper, 0, odd_x, odd_y)
-                right = chip_of(half, upper, 1, odd_x, odd_y)
-                for k, unit in enumerate(units):
-                    rows = slice(32 * k, 32 * k + 32)
-                    out[left, rows, :] = pack_left(unit, low)
-                    out[right, rows, :] = pack_right(unit, low)
-
-
-def prepare(forcing):
+    for upper in range(2):
+        copies[upper].wait()
+        for half in range(2):
+            cols = slice(128 * half, 128 * half + 128)
+            first_u, second_u = held[upper, 0, 0, :, cols], held[upper, 0, 1, :, cols]
+            first_w, second_w = held[upper, 1, 0, :, cols], held[upper, 1, 1, :, cols]
+            units = (
+                weight * (first_w + first_u),
+                weight_two * (second_w + second_u - first_u),
+                weight_three * second_u,
+            )
+            left = chip_of(half, upper, 0, odd_x, odd_y)
+            right = chip_of(half, upper, 1, odd_x, odd_y)
+            for k, unit in enumerate(units):
+                rows = slice(32 * k, 32 * k + 32)
+                out[left, rows, :] = pack_left(unit, low)
+                out[right, rows, :] = pack_right(unit, low)
+
+
+def prepare(forcing, other):
     return pl.pallas_call(
-        prepare_kernel,
-        in_specs=[pl.BlockSpec(memory_space=pltpu.VMEM)],
-        out_specs=[pl.BlockSpec(memory_space=pltpu.VMEM)] * 2,
-        out_shape=[jax.ShapeDtypeStruct((8, 96, 128), jnp.float32)] * 2,
+        functools.partial(prepare_kernel, other),
+        in_specs=[pl.BlockSpec(memory_space=pltpu.HBM)],
+        out_specs=pl.BlockSpec(memory_space=pltpu.VMEM),
+        out_shape=jax.ShapeDtypeStruct((8, 96, 128), jnp.float32),
+        scratch_shapes=[pltpu.VMEM((2, 2, 2, 64, 256), jnp.float32), pltpu.SemaphoreType.DMA((2,))],
         compiler_params=params(),
-        name="prepare",
+        cost_estimate=cost(2**20),
+        name="prepare_other" if other else "prepare_own",
     )(forcing.reshape(2, 2, 2, 2, 64, 256))
 
 
@@ -504,22 +522,21 @@
     )(lam, planes, beside, from_side, from_core, from_cross)
 
 
-def finish_kernel(returned, received, forcing, initial, last, out):
+def finish_kernel(other, units, forcing, initial, last, *refs):
+    out, held, sent = refs[-3:]
     tm, odd_x, odd_y, core = place()[:4]
-    is_own = pl.program_id(0) == core
     low = lanes(32) < 64
     first = jnp.where(tm == 0, 1.0, 0.0).astype(jnp.float32)
-
-    def unit(chip, k):
-        start = pl.multiple_of(64 * core + 32 * k, 32)
-        return jnp.where(is_own, returned[chip, pl.ds(start, 32), :], received[chip, 32 * k : 32 * k + 32, :])
-
+    begin = 0 if other else pl.multiple_of(64 * core, 64)
+    core = core ^ other
+    copies = []
     for upper in range(2):
         for half in range(2):
             cols = slice(128 * half, 128 * half + 128)
-            left = chip_of(half, upper, 0, odd_x, odd_y)
-            right = chip_of(half, upper, 1, odd_x, odd_y)
-            ones, twos = ([unit(chip, k) for k in range(3)] for chip in (left, right))
+            ones, twos = (
+                [units[chip, pl.ds(begin + 32 * k, 32), :] for k in range(3)]
+                for chip in (chip_of(half, upper, inner, odd_x, odd_y) for inner in range(2))
+            )
             for part in range(2):
                 rows = slice(32 * part, 32 * part + 32)
                 if part == 0:
@@ -527,38 +544,39 @@
                 else:
                     values = [jnp.where(low, half_turn(one), two) for one, two in zip(ones, twos)]
                 before, now, after = values
-                start = forcing[0, 0, upper, 0, rows, cols] + first * (
-                    initial[0, upper, 0, rows, cols] - ALPHA * last[0, upper, 0, rows, cols]
+                start = forcing[0, 0, upper, core, rows, cols] + first * (
+                    initial[0, upper, core, rows, cols] - ALPHA * last[0, upper, core, rows, cols]
                 )
-                out[0, 0, upper, 0, rows, cols] = now
-                out[0, 1, upper, 0, rows, cols] = after
-                out[1, 0, upper, 0, rows, cols] = now - before - start
-                out[1, 1, upper, 0, rows, cols] = after - now - forcing[0, 1, upper, 0, rows, cols]
-
-
-def finish(returned, received, forcing, initial, last):
-    result = pl.pallas_call(
-        finish_kernel,
-        grid=(2,),
-        in_specs=[
-            pl.BlockSpec((8, 160, 128), lambda i: (0, 0, 0)),
-            pl.BlockSpec((8, 96, 128), lambda i: (0, 0, 0)),
-            pl.BlockSpec((1, 2, 2, 1, 64, 256), lambda i: (0, 0, 0, i, 0, 0)),
-            pl.BlockSpec((1, 2, 1, 64, 256), lambda i: (0, 0, i, 0, 0)),
-            pl.BlockSpec((1, 2, 1, 64, 256), lambda i: (0, 0, i, 0, 0)),
-        ],
-        out_specs=pl.BlockSpec((2, 2, 2, 1, 64, 256), lambda i: (0, 0, 0, i, 0, 0)),
+                held[upper, 0, 0, rows, cols] = now
+                held[upper, 0, 1, rows, cols] = after
+                held[upper, 1, 0, rows, cols] = now - before - start
+                held[upper, 1, 1, rows, cols] = after - now - forcing[0, 1, upper, core, rows, cols]
+        copies.append(pltpu.make_async_copy(held.at[upper], out.at[:, :, upper, core], sent.at[upper]))
+        copies[upper].start()
+    for upper in range(2):
+        copies[upper].wait()
+
+
+def finish(units, forcing, initial, last, result=None):
+    other = result is not None
+    return pl.pallas_call(
+        functools.partial(finish_kernel, int(other)),
+        in_specs=[pl.BlockSpec(memory_space=pltpu.VMEM)] * 4
+        + [pl.BlockSpec(memory_space=pltpu.HBM)] * other,
+        out_specs=pl.BlockSpec(memory_space=pltpu.HBM),
         out_shape=jax.ShapeDtypeStruct((2, 2, 2, 2, 64, 256), jnp.float32),
+        scratch_shapes=[pltpu.VMEM((2, 2, 2, 64, 256), jnp.float32), pltpu.SemaphoreType.DMA((2,))],
+        input_output_aliases={4: 0} if other else {},
         compiler_params=params(),
-        name="finish",
+        cost_estimate=cost(2**20),
+        name="finish_other" if other else "finish_own",
     )(
-        returned,
-        received,
+        units,
         forcing.reshape(2, 2, 2, 2, 64, 256),
         initial.reshape(2, 2, 2, 64, 256),
         last.reshape(2, 2, 2, 64, 256),
+        *([result] if other else []),
     )
-    return result.reshape(2, 2, 256, 256)
 
 
 def lam_squares():
@@ -578,8 +596,8 @@
 def per_device(forcing, initial, previous_last, cell_class, courant_table):
     core = lax.axis_index("tm") & 1
     lam = jnp.asarray(lam_squares())
-    mine, theirs = prepare(forcing)
-    received = chips_exchange(merge(mine, lax.ppermute(theirs, "tm", CORES)))
+    theirs = lax.ppermute(prepare(forcing, 1), "tm", CORES)
+    received = chips_exchange(merge(prepare(forcing, 0), theirs))
     planes, beside, side, to_core, to_cross = transform(
         courant_table, cell_class, initial, previous_last, received
     )
@@ -593,7 +611,9 @@
     returned = chips_exchange(solve(lam, planes, beside, from_side, from_core, from_cross))
     wanted = lax.dynamic_slice_in_dim(returned, 64 * (1 - core), 96, axis=1)
     other = lax.ppermute(wanted, "tm", CORES)
-    return finish(returned, other, forcing, initial, previous_last)
+    result = finish(returned, forcing, initial, previous_last)
+    result = finish(other, forcing, initial, previous_last, result)
+    return result.reshape(2, 2, 256, 256)
 
 
 def solution(mesh):

time: 87 us -> 85.9 us (0.987)
  waiting for transfers between devices: 31 us -> 29.5 us
    ppermute x1, waiting for transfers between devices: 1.35 us -> 0.41 us  [per_device(): other = lax.ppermute(wanted, 'tm', CORES)]
    pallas_call x2 -> x4, Pallas kernels: 1.56 us -> 2.45 us  [the longest x2 1.85 us: finish(): pl.pallas_call(functools.partial(finish_kernel, int(other)), in_specs=[pl...]
  transfers between devices with their start and end apart: 6 -> 6, of which waited for: 6 -> 6; matrix products, arithmetic and copies ran while one was open for 0% -> 0% of each run, Pallas kernels for 0% -> 1%
where the time goes in v4:
time: 85.9 us; the launch traced here: 85 us
  blocking collectives  33.6 us (39%)
  waiting for transfers between devices  29.5 us (34%)
  Pallas kernels  11.5 us (13%)
  starting transfers between devices  8.9 us (10%)
  local copies, waits for them, and re-layouts  1.29 us (2%)
    all_to_all x1, blocking collectives, chips_exchange(): lax.all_to_all(pieces, 'tm', 0, 0, axis_index_groups=CHIPS, tiled=True)  33.6 us
    all_to_all x1, waiting for transfers between devices, chips_exchange(): lax.all_to_all(pieces, 'tm', 0, 0, axis_index_groups=CHIPS, tiled=True)  21.1 us
    pallas_call x1, Pallas kernels, solve(): pl.pallas_call(solve_kernel, in_specs=[pl.BlockSpec(memory_space=pltpu.SM...  7.6 us
    all_to_all x1, starting transfers between devices, chips_exchange(): lax.all_to_all(pieces, 'tm', 0, 0, axis_index_groups=CHIPS, tiled=True)  3.67 us
    ppermute x1, waiting for transfers between devices, per_device(): from_cross = lax.ppermute(strip(to_cross, 24 * core), AXES, TO_CROSS)  3.61 us
    ppermute x1, starting transfers between devices, per_device(): from_core = lax.ppermute(strip(to_core, 24 * (1 - core)), AXES, TO_CORE)  2.95 us
    ppermute x1, waiting for transfers between devices, per_device(): from_side = lax.ppermute(side, AXES, TO_SIDE)  2.53 us
    pallas_call x2, Pallas kernels, finish(): pl.pallas_call(functools.partial(finish_kernel, int(other)), in_specs=[pl...  1.85 us
  transfers between devices with their start and end apart: 6, of which 6 were waited for; matrix products, arithmetic and copies ran while one was open for 0% of the time, Pallas kernels for 1%

profile of v4, /device:TPU:33, one launch (start us, length us, event | category | flops | bytes accessed | tf_op | source)
XLA Modules:
  0.0 85.0 jit_solution(1538868012502484224)
XLA Ops:
  0.0 0.0 copy-start
  0.0 1.2 %copy-done = f32[2,2,256,256]{3,2,1,0:T(8,128)S(1)} copy-done((f32[2,2,256,256]{3,2,1,0:T(8,128)S(1)}, f32[2,2,256,256]{3,2,1,0:T(8,128)}, u32[]{:S(2)}) %copy-start) | copy-done | bytes 1048600
  1.2 0.3 prepare_other.1
  1.5 0.8 collective-permute-start
  2.3 0.3 prepare_own.1.mine
  2.6 1.0 %collective-permute-done.received = f32[8,96,128]{2,1,0:T(8,128)S(1)} collective-permute-done((f32[8,96,128]{2,1,0:T(8,128)S(1)}, f32[8,96,128]{2,1,0:T(8,128)S(1)}, u32[]{:S(2)}, u32[]{:S(2)}) %collective-permute-start) | collective-permute-done | bytes 393248 | tf_op jit(solution)/shard_map/ppermute | solution.py:599
  3.6 0.2 merge.1
  3.9 0.0 copy-start.2
  3.9 0.0 copy-start.3
  3.9 0.0 copy-start.4
  3.9 0.0 copy-start.6
  4.0 33.6 %all_to_all.10.received = f32[8,184,128]{2,1,0:T(8,128)S(1)} all-to-all(f32[8,184,128]{2,1,0:T(8,128)S(1)} %merge.1), channel_id=1, replica_groups={{0,32,64,96,128,160,192,224},{16,48,80,112,144,176,208,240},{1,33,65,97..., dimensions={0} | all-to-all | bytes 1507328 | tf_op jit(solution)/shard_map/all_to_all | solution.py:593
  37.6 0.0 copy-done.2
  37.6 0.0 copy-done.3
  37.6 0.0 copy-done.4
  37.6 0.0 copy-done.6
  37.6 1.2 %transform.1 = (f32[33,32,128]{2,1,0:T(8,128)S(1)}, f32[33,8,128]{2,1,0:T(8,128)S(1)}, f32[5,32,128]{2,1,0:T(8,128)S(1)}, f32[22,8,128]{2,1,0:T(8,128)S(1)}, f32[22,8,128]{2,1,0:T(8,128)S(1)}) custom-call(f32[8]{0:T(128)S(1)} %copy-done.6, s32[256,256]{1,0:T(8,128)S(1)} %copy-done.4, f32[2,256,256]{2,1,0:T(8,128)S(1)} %copy-done.2, ...), custom_call_target="tpu_custom_call" | custom-call | tf_op jit(solution)/shard_map/transform/pallas_call | solution.py:345
  38.8 0.8 collective-permute-start.1
  39.7 2.5 %collective-permute-done.1.from_side = f32[5,32,128]{2,1,0:T(8,128)S(1)} collective-permute-done((f32[5,32,128]{2,1,0:T(8,128)S(1)}, f32[5,32,128]{2,1,0:T(8,128)S(1)}, u32[]{:S(2)}, u32[]{:S(2)}) %collective-permute-start.1) | collective-permute-done | bytes 81952 | tf_op jit(solution)/shard_map/ppermute | solution.py:604
  42.2 2.9 %collective-permute-start.2 = (f32[27,8,128]{2,1,0:T(8,128)S(1)}, f32[27,8,128]{2,1,0:T(8,128)S(1)}, u32[]{:S(2)}, u32[]{:S(2)}) collective-permute-start(f32[27,8,128]{2,1,0:T(8,128)S(1)} %pad_maximum_fusion), channel_id=1, source_target_pairs={{0,16},{32,48},{224,240},{192,208},{193,209},{225,241},{33,49},{1,... | collective-permute-start | bytes 331784 | tf_op jit(solution)/shard_map/ppermute | solution.py:609
  45.2 0.1 collective-permute-start.3
  45.3 0.8 collective-permute-done.2.from_core
  46.1 3.6 %collective-permute-done.3.from_cross = f32[27,8,128]{2,1,0:T(8,128)S(1)} collective-permute-done((f32[27,8,128]{2,1,0:T(8,128)S(1)}, f32[27,8,128]{2,1,0:T(8,128)S(1)}, u32[]{:S(2)}, u32[]{:S(2)}) %collective-permute-start.3) | collective-permute-done | bytes 110624 | tf_op jit(solution)/shard_map/ppermute | solution.py:610
  49.7 0.0 copy-done.5
  49.7 7.6 %solve.1 = f32[8,160,128]{2,1,0:T(8,128)} custom-call(f32[16,2]{1,0:T(8,128)S(1)} %copy-done.5, f32[33,32,128]{2,1,0:T(8,128)S(1)} %get-tuple-element.10.planes, f32[33,8,128]{2,1,0:T(8,128)S(1)} %get-tuple-element.11.beside, f32[5,32,128]{2,1,0:T(8,128)S(1)} %collective-permute-done.1.from_side, f32[27,8,128]{2,1,0:T(8,128)S(1)} %collective-permute-done.2.from_core, ...), custom_call_target="tpu_custom_call" | custom-call | tf_op jit(solution)/shard_map/solve/pallas_call | solution.py:510
  57.3 3.7 %all-to-all-start.1 = ((f32[8,160,128]{2,1,0:T(8,128)}), f32[8,160,128]{2,1,0:T(8,128)S(1)}, u32[]{:S(2)}, u32[]{:S(2)}) async-start(f32[8,160,128]{2,1,0:T(8,128)} %solve.1), calls=%async_computation.1 | async-start | bytes 1310720 | tf_op jit(solution)/shard_map/all_to_all | solution.py:593
  61.0 21.1 %all-to-all-done.1.units = f32[8,160,128]{2,1,0:T(8,128)S(1)} async-done(((f32[8,160,128]{2,1,0:T(8,128)}), f32[8,160,128]{2,1,0:T(8,128)S(1)}, u32[]{:S(2)}, u32[]{:S(2)}) %all-to-all-start.1) | async-done | bytes 655392 | tf_op jit(solution)/shard_map/all_to_all | solution.py:593
  82.1 0.6 collective-permute-start.4
  82.7 0.0 copy-done.1
  82.7 0.9 %finish_own.1.refs_0_ = f32[2,2,2,2,64,256]{5,4,3,2,1,0:T(8,128)} custom-call(f32[8,160,128]{2,1,0:T(8,128)S(1)} %all-to-all-done.1.units, f32[2,2,2,2,64,256]{5,4,3,2,1,0:T(8,128)S(1)} %bitcast.6, f32[2,2,2,64,256]{4,3,2,1,0:T(8,128)S(1)} %bitcast.8, f32[2,2,2,64,256]{4,3,2,1,0:T(8,128)S(1)} %bitcast.10), custom_call_target="tpu_custom_call" | custom-call | flops 1048576 | bytes 1048576 | tf_op jit(solution)/shard_map/finish_own/pallas_call | solution.py:562
  83.7 0.4 collective-permute-done.4.units
  84.1 0.9 %finish_other.1 = f32[2,2,2,2,64,256]{5,4,3,2,1,0:T(8,128)} custom-call(f32[8,96,128]{2,1,0:T(8,128)S(1)} %collective-permute-done.4.units, f32[2,2,2,2,64,256]{5,4,3,2,1,0:T(8,128)S(1)} %bitcast.7, f32[2,2,2,64,256]{4,3,2,1,0:T(8,128)S(1)} %bitcast.9, f32[2,2,2,64,256]{4,3,2,1,0:T(8,128)S(1)} %bitcast.11, ...), custom_call_target="tpu_custom_call", output_to_operand_aliasing={{}: (4, {})} | custom-call | flops 1048576 | bytes 1048576 | tf_op jit(solution)/shard_map/finish_other/pallas_call | solution.py:562
  (6 shorter events, 0.1 us)
Async XLA Ops:
  0.0 1.2 %copy-start = (f32[2,2,256,256]{3,2,1,0:T(8,128)S(1)}, f32[2,2,256,256]{3,2,1,0:T(8,128)}, u32[]{:S(2)}) copy-start(f32[2,2,256,256]{3,2,1,0:T(8,128)} %param.6) | copy-start | bytes 3145732
  1.5 2.1 %collective-permute-start = (f32[8,96,128]{2,1,0:T(8,128)S(1)}, f32[8,96,128]{2,1,0:T(8,128)S(1)}, u32[]{:S(2)}, u32[]{:S(2)}) collective-permute-start(f32[8,96,128]{2,1,0:T(8,128)S(1)} %prepare_other.1), channel_id=1, source_target_pairs={{0,16},{16,0},{32,48},{48,32},{64,80},{80,64},{96,112},{112,96},{1... | collective-permute-start | bytes 1179656 | tf_op jit(solution)/shard_map/ppermute | solution.py:599
  3.9 33.7 %copy-start.2 = (f32[2,256,256]{2,1,0:T(8,128)S(1)}, f32[2,256,256]{2,1,0:T(8,128)}, u32[]{:S(2)}) copy-start(f32[2,256,256]{2,1,0:T(8,128)} %initial.1) | copy-start | bytes 1572868
  3.9 33.7 %copy-start.3 = (f32[2,256,256]{2,1,0:T(8,128)S(1)}, f32[2,256,256]{2,1,0:T(8,128)}, u32[]{:S(2)}) copy-start(f32[2,256,256]{2,1,0:T(8,128)} %last.1) | copy-start | bytes 1572868
  3.9 33.6 %copy-start.4 = (s32[256,256]{1,0:T(8,128)S(1)}, s32[256,256]{1,0:T(8,128)}, u32[]{:S(2)}) copy-start(s32[256,256]{1,0:T(8,128)} %cell_class.1) | copy-start | bytes 786436
  3.9 33.6 %copy-start.6 = (f32[8]{0:T(128)S(1)}, f32[8]{0:T(128)}, u32[]{:S(2)}) copy-start(f32[8]{0:T(128)} %table.1) | copy-start | bytes 100
  38.8 3.4 %collective-permute-start.1 = (f32[5,32,128]{2,1,0:T(8,128)S(1)}, f32[5,32,128]{2,1,0:T(8,128)S(1)}, u32[]{:S(2)}, u32[]{:S(2)}) collective-permute-start(f32[5,32,128]{2,1,0:T(8,128)S(1)} %get-tuple-element.12), channel_id=1, source_target_pairs={{0,16},{32,224},{224,32},{192,193},{193,192},{225,33},{33,225},{1,... | collective-permute-start | bytes 245768 | tf_op jit(solution)/shard_map/ppermute | solution.py:604
  42.2 3.9 %collective-permute-start.2 = (f32[27,8,128]{2,1,0:T(8,128)S(1)}, f32[27,8,128]{2,1,0:T(8,128)S(1)}, u32[]{:S(2)}, u32[]{:S(2)}) collective-permute-start(f32[27,8,128]{2,1,0:T(8,128)S(1)} %pad_maximum_fusion), channel_id=1, source_target_pairs={{0,16},{32,48},{224,240},{192,208},{193,209},{225,241},{33,49},{1,... | collective-permute-start | bytes 331784 | tf_op jit(solution)/shard_map/ppermute | solution.py:609
  45.2 4.6 %copy-start.5 = (f32[16,2]{1,0:T(8,128)S(1)}, f32[16,2]{1,0:T(8,128)}, u32[]{:S(2)}) copy-start(f32[16,2]{1,0:T(8,128)} %constant.19.clone.lam) | copy-start | bytes 388
  45.2 4.6 %collective-permute-start.3 = (f32[27,8,128]{2,1,0:T(8,128)S(1)}, f32[27,8,128]{2,1,0:T(8,128)S(1)}, u32[]{:S(2)}, u32[]{:S(2)}) collective-permute-start(f32[27,8,128]{2,1,0:T(8,128)S(1)} %pad_maximum_fusion.1), channel_id=1, source_target_pairs={{0,28},{32,60},{224,252},{192,220},{193,221},{225,253},{33,61},{1,... | collective-permute-start | bytes 331784 | tf_op jit(solution)/shard_map/ppermute | solution.py:610
  57.3 25.4 %copy-start.1 = (f32[2,2,256,256]{3,2,1,0:T(8,128)S(1)}, f32[2,2,256,256]{3,2,1,0:T(8,128)}, u32[]{:S(2)}) copy-start(f32[2,2,256,256]{3,2,1,0:T(8,128)} %param.6) | copy-start | bytes 3145732
  57.3 24.8 %all-to-all-start.1 = ((f32[8,160,128]{2,1,0:T(8,128)}), f32[8,160,128]{2,1,0:T(8,128)S(1)}, u32[]{:S(2)}, u32[]{:S(2)}) async-start(f32[8,160,128]{2,1,0:T(8,128)} %solve.1), calls=%async_computation.1 | async-start | bytes 1310720 | tf_op jit(solution)/shard_map/all_to_all | solution.py:593
  82.1 1.9 %collective-permute-start.4 = (f32[8,96,128]{2,1,0:T(8,128)S(1)}, f32[8,96,128]{2,1,0:T(8,128)S(1)}, u32[]{:S(2)}, u32[]{:S(2)}) collective-permute-start(f32[8,96,128]{2,1,0:T(8,128)S(1)} %constant_dynamic-slice_fusion), channel_id=1, source_target_pairs={{0,16},{16,0},{32,48},{48,32},{64,80},{80,64},{96,112},{112,96},{1... | collective-permute-start | bytes 1179656 | tf_op jit(solution)/shard_map/ppermute | solution.py:613

commit v5 on v4

--- a/solution.py
+++ b/solution.py
@@ -266,204 +266,285 @@
     return steps
 
 
-def transform_kernel(
-    table, cell_class, initial, last, received, planes_out, beside_out, side_out, core_out, cross_out
-):
-    _, _, _, core, upper, half, inner = place()[:7]
-    low8, low32 = lanes(8) < 64, lanes(32) < 64
-    lane8 = lanes(8) % 64
+def slots(m):
+    lane = lanes(8) % 64
+    return (lane >= 8 * m) & (lane < 8 * m + 8)
+
+
+def in_slots(planes, start):
+    groups = []
+    for g in range(5):
+        value = jnp.zeros((8, 128), jnp.float32)
+        for m, plane in enumerate(planes[8 * g : 8 * g + 8]):
+            value = jnp.where(slots(m), turn(plane, 8 * m - start), value)
+        groups.append(value)
+    return groups
+
+
+def block_of(value, inner):
+    return pack_left(jnp.where(inner == 1, half_turn(value), value), lanes(32) < 64)
+
+
+def beside_of(value, inner):
+    other = block_of(value, 1 - inner)
+    beside = jnp.zeros((8, 128), jnp.float32)
+    for r in range(4):
+        beside = jnp.where(slots(r), turn(other[8 * r : 8 * r + 8], 8 * r - 56 * inner), beside)
+    return beside
+
+
+def pair_fields(table, cell_class, initial, last):
+    core, upper, half = place()[3:6]
     rows = pl.ds(pl.multiple_of((upper * 2 + core) * 64, 64), 64)
     cols = pl.ds(pl.multiple_of(half * 128, 128), 128)
-    is_right = inner == 1
-
-    def slots(m):
-        return (lane8 >= 8 * m) & (lane8 < 8 * m + 8)
-
-    def own_and_beside(value):
-        turned = half_turn(value)
-        own = pack_left(jnp.where(is_right, turned, value), low32)
-        other = pack_left(jnp.where(is_right, value, turned), low32)
-        beside = jnp.zeros((8, 128), jnp.float32)
-        for r in range(4):
-            beside = jnp.where(slots(r), turn(other[8 * r : 8 * r + 8], 8 * r - 56 * inner), beside)
-        return [own[8 * r : 8 * r + 8] for r in range(4)] + [beside]
-
     classes = cell_class[rows, cols]
     courant = jnp.zeros(classes.shape, jnp.float32)
     for k in range(8):
         courant = jnp.where(classes == k, table[k], courant)
-    courant = own_and_beside(courant)
-    start_u, start_w = (
-        own_and_beside(initial[c, rows, cols] - ALPHA * last[c, rows, cols]) for c in range(2)
+    return [courant] + [initial[c, rows, cols] - ALPHA * last[c, rows, cols] for c in range(2)]
+
+
+def with_start(steps, start_u, start_w):
+    return [steps[0] + (start_w + start_u), steps[1] - np.float32(FACTOR) * start_u] + steps[2:]
+
+
+def transform_kernel(table, cell_class, initial, last, received, planes_out, side_out):
+    inner = place()[6]
+    courant, start_u, start_w = (
+        block_of(value, inner) for value in pair_fields(table, cell_class, initial, last)
     )
-
-    for r in range(5):
+    for r in range(4):
+        rows = slice(8 * r, 8 * r + 8)
         steps = []
         for t in range(8):
-            before = (t + 7) % 8
-            if r < 4:
-                part = [received[t, 32 * k + 8 * r : 32 * k + 8 * r + 8, :] for k in range(4)]
-                part[0] = part[0] + received[before, 128 + 8 * r : 136 + 8 * r, :]
-            else:
-                one, two = received[t, 160:168, :], received[t, 168:176, :]
-                part = [one + received[before, 176:184, :], turn(one, -32), two, turn(two, -32)]
+            part = [received[t, 32 * k + 8 * r : 32 * k + 8 * r + 8, :] for k in range(4)]
+            part[0] = part[0] + received[(t + 7) % 8, 128 + 8 * r : 136 + 8 * r, :]
             steps.extend(part)
-        steps[0] = steps[0] + (start_w[r] + start_u[r])
-        steps[1] = steps[1] - np.float32(FACTOR) * start_u[r]
-        planes = forward(steps) + [courant[r]]
-        if r == 4:
-            for p in range(33):
-                beside_out[p] = planes[p]
-        else:
-            for p in range(33):
-                planes_out[p, 8 * r : 8 * r + 8, :] = planes[p]
-            for g in range(5):
-                value = jnp.zeros((8, 128), jnp.float32)
-                for m, plane in enumerate(planes[8 * g : 8 * g + 8]):
-                    value = jnp.where(slots(m), turn(plane, 8 * m - 56 * inner), value)
-                side_out[g, 8 * r : 8 * r + 8, :] = value
-        if r == 0:
-            pairs = planes + [planes[32]]
-            top = [jnp.where(low8, pairs[2 * j], half_turn(pairs[2 * j + 1])) for j in range(17)]
-        if r == 3:
-            pairs = planes + [planes[32]]
-            bottom = [jnp.where(low8, half_turn(pairs[2 * j]), pairs[2 * j + 1]) for j in range(17)]
-        if r == 4:
-            for strip, start in ((top, 0), (bottom, 88)):
-                for g in range(5):
-                    value = jnp.zeros((8, 128), jnp.float32)
-                    for m, plane in enumerate(planes[8 * g : 8 * g + 8]):
-                        value = jnp.where(slots(m), turn(plane, 8 * m - start), value)
-                    strip.append(value)
-    for i in range(22):
-        core_out[i] = jnp.where(core == 0, bottom[i], top[i])
-        cross_out[i] = jnp.where(core == 0, top[i], bottom[i])
+        planes = forward(with_start(steps, start_u[rows], start_w[rows])) + [courant[rows]]
+        for p in range(33):
+            planes_out[p, rows, :] = planes[p]
+        for g, value in enumerate(in_slots(planes, 56 * inner)):
+            side_out[g, rows, :] = value
 
 
 def transform(table, cell_class, initial, last, received):
-    shapes = ((33, 32, 128), (33, 8, 128), (5, 32, 128), (22, 8, 128), (22, 8, 128))
+    shapes = ((33, 32, 128), (5, 32, 128))
     return pl.pallas_call(
         transform_kernel,
         in_specs=[pl.BlockSpec(memory_space=pltpu.SMEM)] + [pl.BlockSpec(memory_space=pltpu.VMEM)] * 4,
-        out_specs=[pl.BlockSpec(memory_space=pltpu.VMEM)] * 5,
+        out_specs=[pl.BlockSpec(memory_space=pltpu.VMEM)] * 2,
         out_shape=[jax.ShapeDtypeStruct(shape, jnp.float32) for shape in shapes],
         compiler_params=params(),
         name="transform",
     )(table, cell_class, initial, last, received)
 
 
-def around(field):
+def strips_kernel(
+    table, cell_class, initial, last, received, planes, beside_out, core_out, cross_out
+):
+    core, _, _, inner = place()[3:7]
+    low = lanes(8) < 64
+    courant, start_u, start_w = (
+        beside_of(value, inner) for value in pair_fields(table, cell_class, initial, last)
+    )
+    steps = []
+    for t in range(8):
+        one, two = received[t, 160:168, :], received[t, 168:176, :]
+        first = one + received[(t + 7) % 8, 176:184, :]
+        steps.extend([first, turn(one, -32), two, turn(two, -32)])
+    beside = forward(with_start(steps, start_u, start_w)) + [courant]
+    for p in range(33):
+        beside_out[p] = beside[p]
+    top, bottom = [], []
+    for j in range(17):
+        one, two = 2 * j, min(2 * j + 1, 32)
+        top.append(jnp.where(low, planes[one, 0:8, :], half_turn(planes[two, 0:8, :])))
+        bottom.append(jnp.where(low, half_turn(planes[one, 24:32, :]), planes[two, 24:32, :]))
+    top.extend(in_slots(beside, 0))
+    bottom.extend(in_slots(beside, 88))
+    for i in range(22):
+        core_out[i] = jnp.where(core == 0, bottom[i], top[i])
+        cross_out[i] = jnp.where(core == 0, top[i], bottom[i])
+
+
+def strips(table, cell_class, initial, last, received, planes):
+    shapes = ((33, 8, 128), (22, 8, 128), (22, 8, 128))
+    return pl.pallas_call(
+        strips_kernel,
+        in_specs=[pl.BlockSpec(memory_space=pltpu.SMEM)] + [pl.BlockSpec(memory_space=pltpu.VMEM)] * 5,
+        out_specs=[pl.BlockSpec(memory_space=pltpu.VMEM)] * 3,
+        out_shape=[jax.ShapeDtypeStruct(shape, jnp.float32) for shape in shapes],
+        compiler_params=params(),
+        cost_estimate=cost(2**20),
+        name="strips",
+    )(table, cell_class, initial, last, received, planes)
+
+
+def side_matrix():
+    rows = lax.broadcasted_iota(jnp.int32, (256, 128), 0) % 128
+    gap = (rows - lax.broadcasted_iota(jnp.int32, (256, 128), 1)) % 128
+    return jnp.where((gap == 1) | (gap == 127), 1.0, 0.0).astype(jnp.bfloat16)
+
+
+def sides_by_matrix(field, matrix):
+    value = jnp.concatenate(field, axis=0)
+    high = value.astype(jnp.bfloat16)
+    low = (value - high.astype(jnp.float32)).astype(jnp.bfloat16)
+    result = jnp.dot(jnp.concatenate([high, low], axis=1), matrix, preferred_element_type=jnp.float32)
+    return [result[8 * v : 8 * v + 8] for v in range(10)]
+
+
+def sides_by_rotation(field):
+    return [pltpu.roll(own, 1, 1) + pltpu.roll(own, 127, 1) for own in field]
+
+
+def around(field, sides):
     first = pltpu.roll(field[9], 1, 0)
     last = pltpu.roll(field[0], 7, 0)
     above = [first] + field[:9]
     below = field[1:] + [last]
-    return [
-        (up + down) + (pltpu.roll(own, 1, 1) + pltpu.roll(own, 127, 1))
-        for up, own, down in zip(above, field, below)
-    ]
-
-
-def solve_kernel(lam, planes, beside, from_side, from_core, from_cross, out, solved, wide, own):
-    core, _, _, inner, row0, col0 = place()[3:]
-    low = lanes(32) < 64
-    is_lower = core == 1
-    side_base = 120 - 56 * inner
-    beside_base = 64 + 56 * inner
-
-    def within(lane, base):
-        return (lane >= base) & (lane < base + 8)
-
-    side_lanes, beside_lanes = within(lanes(8), side_base), within(lanes(8), beside_base)
-    low8 = lanes(8) < 64
-
-    def halo(index):
-        return (
-            jnp.where(is_lower, from_core[index], from_cross[index]),
-            jnp.where(is_lower, from_cross[index], from_core[index]),
-        )
-
-    def merged(centre, side, other):
-        value = jnp.where(low8, centre, 0.0)
-        value = jnp.where(side_lanes, side, value)
-        return jnp.where(beside_lanes, other, value)
-
-    def extended(p, pair, odd, group, offset):
+    return [(up + down) + side for up, side, down in zip(above, sides, below)]
+
+
+def bases(inner):
+    return 120 - 56 * inner, 64 + 56 * inner
+
+
+def merged(centre, side, other, bases):
+    lane = lanes(8)
+    value = jnp.where(lane < 64, centre, 0.0)
+    for base, edge in zip(bases, (side, other)):
+        value = jnp.where((lane >= base) & (lane < base + 8), edge, value)
+    return value
+
+
+def in_grid(first_row, count, col0):
+    rows = lax.broadcasted_iota(jnp.int32, (count, 128), 0) + first_row
+    lane = lanes(count)
+    cols = jnp.where(lane >= 120, lane - 128, lane) + col0
+    used = (lane < 72) | (lane >= 120)
+    return used & (rows >= 0) & (rows < 1024) & (cols >= 0) & (cols < 1024)
+
+
+def coefficients(lam, j, special, g_re, g_im, courant, inside):
+    if special:
+        inv_re = inside / (lam[0, 0] + 4.0 * courant)
+        inv_im = inside / (lam[0, 1] + 4.0 * courant)
+        return g_re * inv_re, g_im * inv_im, courant * inv_re, courant * inv_im
+    diag_re = lam[j, 0] + 4.0 * courant
+    diag_im = lam[j, 1]
+    scale = inside / (diag_re * diag_re + diag_im * diag_im)
+    inv_re = diag_re * scale
+    inv_im = -diag_im * scale
+    return (
+        g_re * inv_re - g_im * inv_im,
+        g_re * inv_im + g_im * inv_re,
+        courant * inv_re,
+        courant * inv_im,
+    )
+
+
+def over_frequencies(work):
+    for j in range(4):
+        work(j, j == 0, 0, 16 * j)
+
+    def group(k, carry):
+        for i in range(4):
+            work(4 * k + i, False, k, 16 * i)
+        return carry
+
+    lax.fori_loop(1, 4, group, 0)
+
+
+def widen_kernel(lam, planes, beside, from_side, out):
+    inner, _, col0 = place()[6:]
+    both = bases(inner)
+
+    def extended(p, group, offset):
         edge = beside[p]
-        top_main, bottom_main = halo(pair)
-        if odd:
-            top_main, bottom_main = half_turn(top_main), half_turn(bottom_main)
-        top_beside, bottom_beside = halo(17 + group)
-        top_side, bottom_side = halo(22 + group)
-        parts = [
-            merged(
-                top_main,
-                turn(top_side, side_base - 64 - offset),
-                turn(top_beside, beside_base - offset),
-            )
-        ]
+        parts = []
         for r in range(8):
             part = slice(8 * (r % 4), 8 * (r % 4) + 8)
-            centre, shift = planes[p, part, :], 0 if r < 4 else 64
+            shift = 0 if r < 4 else 64
             parts.append(
                 merged(
-                    turn(centre, shift),
-                    turn(from_side[group, part, :], side_base - shift - offset),
-                    turn(edge, beside_base - shift - 8 * (r % 4)),
+                    turn(planes[p, part, :], shift),
+                    turn(from_side[group, part, :], both[0] - shift - offset),
+                    turn(edge, both[1] - shift - 8 * (r % 4)),
+                    both,
                 )
             )
-        parts.append(
-            merged(
-                bottom_main,
-                turn(bottom_side, side_base - offset),
-                turn(bottom_beside, beside_base - offset),
-            )
+        return jnp.concatenate(parts, axis=0)
+
+    mask = in_grid(0, 64, col0)
+    courant = jnp.where(mask, extended(32, 4, 0), 0.0)
+    inside = jnp.where(mask, 1.0, 0.0)
+
+    def work(j, special, group, offset):
+        g_re, g_im = extended(2 * j, group, offset), extended(2 * j + 1, group, offset + 8)
+        for i, value in enumerate(coefficients(lam, j, special, g_re, g_im, courant, inside)):
+            out[j, i, 8:72, :] = value
+
+    over_frequencies(work)
+
+
+def widen(lam, planes, beside, from_side):
+    return pl.pallas_call(
+        widen_kernel,
+        in_specs=[pl.BlockSpec(memory_space=pltpu.SMEM)] + [pl.BlockSpec(memory_space=pltpu.VMEM)] * 3,
+        out_specs=pl.BlockSpec(memory_space=pltpu.VMEM),
+        out_shape=jax.ShapeDtypeStruct((16, 4, 80, 128), jnp.float32),
+        compiler_params=params(),
+        cost_estimate=cost(2**21),
+        name="widen",
+    )(lam, planes, beside, from_side)
+
+
+def solve_kernel(lam, middle, from_core, from_cross, out, full, solved, wide):
+    core, _, _, inner, row0, col0 = place()[3:]
+    both = bases(inner)
+    low = lanes(32) < 64
+    matrix = side_matrix()
+
+    def halo(index):
+        one, two = from_core[index], from_cross[index]
+        return jnp.where(core == 1, one, two), jnp.where(core == 1, two, one)
+
+    def extended(pair, odd, group, offset):
+        centre, edge, side = halo(pair), halo(17 + group), halo(22 + group)
+        return jnp.concatenate(
+            [
+                merged(
+                    half_turn(centre[i]) if odd else centre[i],
+                    turn(side[i], both[0] - offset - (0 if i else 64)),
+                    turn(edge[i], both[1] - offset),
+                    both,
+                )
+                for i in range(2)
+            ],
+            axis=0,
         )
-        return jnp.concatenate(parts, axis=0)
-
-    def spread(slot, value):
-        wide[slot] = value
-        return [wide[slot, pl.ds(v, 8, stride=10), :] for v in range(10)]
+
+    mask = jnp.concatenate([in_grid(row0 - 8, 8, col0), in_grid(row0 + 64, 8, col0)], axis=0)
+    courant = jnp.where(mask, extended(16, False, 4, 0), 0.0)
+    inside = jnp.where(mask, 1.0, 0.0)
+
+    def work(j, special, group, offset):
+        g_re, g_im = extended(j, False, group, offset), extended(j, True, group, offset + 8)
+        for i, value in enumerate(coefficients(lam, j, special, g_re, g_im, courant, inside)):
+            full[j, i, 0:8, :] = value[:8]
+            full[j, i, 72:80, :] = value[8:]
+
+    over_frequencies(work)
 
     def keep(p, slot, field):
         for v in range(10):
             wide[slot, pl.ds(v, 8, stride=10), :] = field[v]
         solved[p] = jnp.where(low, wide[slot, 8:40, :], half_turn(wide[slot, 40:72, :]))
 
-    rows = lax.broadcasted_iota(jnp.int32, (80, 128), 0) - 8 + row0
-    lane80 = lanes(80)
-    cols = jnp.where(lane80 >= 120, lane80 - 128, lane80) + col0
-    inside = (rows >= 0) & (rows < 1024) & (cols >= 0) & (cols < 1024) & ((lane80 < 72) | (lane80 >= 120))
-    courant = spread(0, jnp.where(inside, extended(32, 16, False, 4, 0), 0.0))
-    inner = spread(1, jnp.where(inside, 1.0, 0.0))
-    for v in range(10):
-        own[0, v] = courant[v]
-        own[1, v] = inner[v]
-
-    def prepared(j, slot, special, group, offset):
-        g_re = spread(2 * slot, extended(2 * j, j, False, group, offset))
-        g_im = spread(2 * slot + 1, extended(2 * j + 1, j, True, group, offset + 8))
-        start_re, start_im, gain_re, gain_im = [], [], [], []
-        for v in range(10):
-            speed, kept = own[0, v], own[1, v]
-            if special:
-                inv_re = kept / (lam[0, 0] + 4.0 * speed)
-                inv_im = kept / (lam[0, 1] + 4.0 * speed)
-                start_re.append(g_re[v] * inv_re)
-                start_im.append(g_im[v] * inv_im)
-            else:
-                diag_re = lam[j, 0] + 4.0 * speed
-                diag_im = lam[j, 1]
-                scale = kept / (diag_re * diag_re + diag_im * diag_im)
-                inv_re = diag_re * scale
-                inv_im = -diag_im * scale
-                start_re.append(g_re[v] * inv_re - g_im[v] * inv_im)
-                start_im.append(g_re[v] * inv_im + g_im[v] * inv_re)
-            gain_re.append(speed * inv_re)
-            gain_im.append(speed * inv_im)
-        return start_re, start_im, gain_re, gain_im
-
     def swept(special, start_re, start_im, gain_re, gain_im, re, im):
-        all_re, all_im = around(re), around(im)
+        all_re = around(re, sides_by_rotation(re))
+        all_im = around(im, sides_by_matrix(im, matrix))
         if special:
             return (
                 [start_re[v] + gain_re[v] * all_re[v] for v in range(10)],
@@ -477,10 +558,10 @@
     def batch(k, has_special):
         sets, fields = [], []
         for i in range(BATCH):
-            special = has_special and i == 0
             j = k * BATCH + i
-            sets.append((special,) + prepared(j, i, special, j >> 2, (j & 3) * 16))
-            fields.append((sets[i][1], sets[i][2]))
+            parts = [[full[j, a, pl.ds(v, 8, stride=10), :] for v in range(10)] for a in range(4)]
+            sets.append((has_special and i == 0, *parts))
+            fields.append((parts[0], parts[1]))
         for _ in range(SWEEPS - 1):
             fields = [swept(*sets[i], *fields[i]) for i in range(BATCH)]
         for i in range(BATCH):
@@ -506,20 +587,23 @@
                 out[(t + 1) % 8, part, :] = value * np.float32(ALPHA) if n == 31 else value
 
 
-def solve(lam, planes, beside, from_side, from_core, from_cross):
+def solve(lam, middle, from_core, from_cross):
     return pl.pallas_call(
         solve_kernel,
-        in_specs=[pl.BlockSpec(memory_space=pltpu.SMEM)] + [pl.BlockSpec(memory_space=pltpu.VMEM)] * 5,
-        out_specs=pl.BlockSpec(memory_space=pltpu.VMEM),
-        out_shape=jax.ShapeDtypeStruct((8, 160, 128), jnp.float32),
+        in_specs=[pl.BlockSpec(memory_space=pltpu.SMEM)] + [pl.BlockSpec(memory_space=pltpu.VMEM)] * 3,
+        out_specs=[pl.BlockSpec(memory_space=pltpu.VMEM)] * 2,
+        out_shape=[
+            jax.ShapeDtypeStruct((8, 160, 128), jnp.float32),
+            jax.ShapeDtypeStruct((16, 4, 80, 128), jnp.float32),
+        ],
+        input_output_aliases={1: 1},
         scratch_shapes=[
             pltpu.VMEM((32, 32, 128), jnp.float32),
             pltpu.VMEM((2 * BATCH, 80, 128), jnp.float32),
-            pltpu.VMEM((2, 10, 8, 128), jnp.float32),
         ],
         compiler_params=params(),
         name="solve",
-    )(lam, planes, beside, from_side, from_core, from_cross)
+    )(lam, middle, from_core, from_cross)[0]
 
 
 def finish_kernel(other, units, forcing, initial, last, *refs):
@@ -598,17 +682,18 @@
     lam = jnp.asarray(lam_squares())
     theirs = lax.ppermute(prepare(forcing, 1), "tm", CORES)
     received = chips_exchange(merge(prepare(forcing, 0), theirs))
-    planes, beside, side, to_core, to_cross = transform(
-        courant_table, cell_class, initial, previous_last, received
-    )
+    fields = (courant_table, cell_class, initial, previous_last, received)
+    planes, side = transform(*fields)
     from_side = lax.ppermute(side, AXES, TO_SIDE)
+    beside, to_core, to_cross = strips(*fields, planes)
 
     def strip(main, start):
         return jnp.concatenate([main, lax.dynamic_slice_in_dim(from_side, start, 8, axis=1)], axis=0)
 
+    from_cross = lax.ppermute(strip(to_cross, 24 * core), AXES, TO_CROSS)
     from_core = lax.ppermute(strip(to_core, 24 * (1 - core)), AXES, TO_CORE)
-    from_cross = lax.ppermute(strip(to_cross, 24 * core), AXES, TO_CROSS)
-    returned = chips_exchange(solve(lam, planes, beside, from_side, from_core, from_cross))
+    middle = widen(lam, planes, beside, from_side)
+    returned = chips_exchange(solve(lam, middle, from_core, from_cross))
     wanted = lax.dynamic_slice_in_dim(returned, 64 * (1 - core), 96, axis=1)
     other = lax.ppermute(wanted, "tm", CORES)
     result = finish(returned, forcing, initial, previous_last)

time: 85.9 us -> 83.9 us (0.977)
  waiting for transfers between devices: 29.5 us -> 26.9 us
  Pallas kernels: 11.5 us -> 12.4 us
    pallas_call x0 -> x2, Pallas kernels: none -> 2.61 us  [the longest x1 1.67 us: widen(): pl.pallas_call(widen_kernel, in_specs=[pl.BlockSpec(memory_space=pltpu.SM...]
    pallas_call x1, Pallas kernels: 7.6 us -> 6.04 us  [solve(): pl.pallas_call(solve_kernel, in_specs=[pl.BlockSpec(memory_space=pltpu.SM...]
    ppermute x1, waiting for transfers between devices: 2.53 us -> 1.59 us  [per_device(): from_side = lax.ppermute(side, AXES, TO_SIDE)]
    ppermute x1, waiting for transfers between devices: 3.61 us -> 2.74 us  [per_device(): from_cross = lax.ppermute(strip(to_cross, 24 * core), AXES, TO_CROSS)]
  transfers between devices with their start and end apart: 6 -> 6, of which waited for: 6 -> 5; matrix products, arithmetic and copies ran while one was open for 0% -> 0% of each run, Pallas kernels for 1% -> 5%
where the time goes in v5:
time: 83.9 us; the launch traced here: 83 us
  blocking collectives  33.5 us (40%)
  waiting for transfers between devices  26.9 us (32%)
  Pallas kernels  12.4 us (15%)
  starting transfers between devices  8.76 us (10%)
  local copies, waits for them, and re-layouts  1.28 us (2%)
    all_to_all x1, blocking collectives, chips_exchange(): lax.all_to_all(pieces, 'tm', 0, 0, axis_index_groups=CHIPS, tiled=True)  33.5 us
    all_to_all x1, waiting for transfers between devices, chips_exchange(): lax.all_to_all(pieces, 'tm', 0, 0, axis_index_groups=CHIPS, tiled=True)  21.1 us
    pallas_call x1, Pallas kernels, solve(): pl.pallas_call(solve_kernel, in_specs=[pl.BlockSpec(memory_space=pltpu.SM...  6.04 us
    all_to_all x1, starting transfers between devices, chips_exchange(): lax.all_to_all(pieces, 'tm', 0, 0, axis_index_groups=CHIPS, tiled=True)  3.54 us
    ppermute x1, starting transfers between devices, per_device(): from_core = lax.ppermute(strip(to_core, 24 * (1 - core)), AXES, TO_CORE)  2.95 us
    ppermute x1, waiting for transfers between devices, per_device(): from_cross = lax.ppermute(strip(to_cross, 24 * core), AXES, TO_CROSS)  2.74 us
    pallas_call x2, Pallas kernels, finish(): pl.pallas_call(functools.partial(finish_kernel, int(other)), in_specs=[pl...  1.85 us
  transfers between devices with their start and end apart: 6, of which 5 were waited for; matrix products, arithmetic and copies ran while one was open for 0% of the time, Pallas kernels for 5%

profile of v5, /device:TPU:33, one launch (start us, length us, event | category | flops | bytes accessed | tf_op | source)
XLA Modules:
  0.0 83.0 jit_solution(8194142656862545080)
XLA Ops:
  0.0 0.0 copy-start
  0.0 1.2 %copy-done = f32[2,2,256,256]{3,2,1,0:T(8,128)S(1)} copy-done((f32[2,2,256,256]{3,2,1,0:T(8,128)S(1)}, f32[2,2,256,256]{3,2,1,0:T(8,128)}, u32[]{:S(2)}) %copy-start) | copy-done | bytes 1048600
  1.2 0.3 prepare_other.1
  1.6 0.8 collective-permute-start
  2.3 0.3 prepare_own.1.mine
  2.6 1.0 %collective-permute-done.received = f32[8,96,128]{2,1,0:T(8,128)S(1)} collective-permute-done((f32[8,96,128]{2,1,0:T(8,128)S(1)}, f32[8,96,128]{2,1,0:T(8,128)S(1)}, u32[]{:S(2)}, u32[]{:S(2)}) %collective-permute-start) | collective-permute-done | bytes 393248 | tf_op jit(solution)/shard_map/ppermute | solution.py:683
  3.7 0.2 merge.1
  3.9 33.5 %all_to_all.10.received = f32[8,184,128]{2,1,0:T(8,128)S(1)} all-to-all(f32[8,184,128]{2,1,0:T(8,128)S(1)} %merge.1), channel_id=1, replica_groups={{0,32,64,96,128,160,192,224},{16,48,80,112,144,176,208,240},{1,33,65,97..., dimensions={0} | all-to-all | bytes 1507328 | tf_op jit(solution)/shard_map/all_to_all | solution.py:677
  37.4 0.0 copy-done.2
  37.4 0.0 copy-done.3
  37.4 0.0 copy-done.4
  37.4 0.0 copy-done.6
  37.4 0.0 copy-start.5
  37.4 1.0 %transform.1 = (f32[33,32,128]{2,1,0:T(8,128)S(1)}, f32[5,32,128]{2,1,0:T(8,128)S(1)}) custom-call(f32[8]{0:T(128)S(1)} %copy-done.6, s32[256,256]{1,0:T(8,128)S(1)} %copy-done.4, f32[2,256,256]{2,1,0:T(8,128)S(1)} %copy-done.2, f32[2,256,256]{2,1,0:T(8,128)S(1)} %copy-done.3, f32[8,184,128]{2,1,0:T(8,128)S(1)} %all_to_all.10.received), custom_call_target="tpu_custom_call" | custom-call | tf_op jit(solution)/shard_map/transform/pallas_call | solution.py:332
  38.5 0.8 %collective-permute-start.1 = (f32[5,32,128]{2,1,0:T(8,128)S(1)}, f32[5,32,128]{2,1,0:T(8,128)S(1)}, u32[]{:S(2)}, u32[]{:S(2)}) collective-permute-start(f32[5,32,128]{2,1,0:T(8,128)S(1)} %get-tuple-element.13), channel_id=1, source_target_pairs={{0,16},{32,224},{224,32},{192,193},{193,192},{225,33},{33,225},{1,... | collective-permute-start | bytes 245768 | tf_op jit(solution)/shard_map/ppermute | solution.py:687
  39.3 0.9 %strips.1 = (f32[33,8,128]{2,1,0:T(8,128)S(1)}, f32[22,8,128]{2,1,0:T(8,128)S(1)}, f32[22,8,128]{2,1,0:T(8,128)S(1)}) custom-call(f32[8]{0:T(128)S(1)} %copy-done.6, s32[256,256]{1,0:T(8,128)S(1)} %copy-done.4, f32[2,256,256]{2,1,0:T(8,128)S(1)} %copy-done.2, f32[2,256,256]{2,1,0:T(8,128)S(1)} %copy-done.3, f32[8,184,128]{2,1,0:T(8,128)S(1)} %all_to_all.10.received, ...), custom_call_target="tpu_custom_call" | custom-call | flops 1048576 | bytes 1048576 | tf_op jit(solution)/shard_map/strips/pallas_call | solution.py:372
  40.3 1.6 %collective-permute-done.1.from_side = f32[5,32,128]{2,1,0:T(8,128)S(1)} collective-permute-done((f32[5,32,128]{2,1,0:T(8,128)S(1)}, f32[5,32,128]{2,1,0:T(8,128)S(1)}, u32[]{:S(2)}, u32[]{:S(2)}) %collective-permute-start.1) | collective-permute-done | bytes 81952 | tf_op jit(solution)/shard_map/ppermute | solution.py:687
  41.9 2.9 %collective-permute-start.2 = (f32[27,8,128]{2,1,0:T(8,128)S(1)}, f32[27,8,128]{2,1,0:T(8,128)S(1)}, u32[]{:S(2)}, u32[]{:S(2)}) collective-permute-start(f32[27,8,128]{2,1,0:T(8,128)S(1)} %pad_maximum_fusion), channel_id=1, source_target_pairs={{0,16},{32,48},{224,240},{192,208},{193,209},{225,241},{33,49},{1,... | collective-permute-start | bytes 331784 | tf_op jit(solution)/shard_map/ppermute | solution.py:694
  44.9 0.1 collective-permute-start.3
  45.0 0.0 copy-done.5
  45.0 1.7 %widen.1.middle = f32[16,4,80,128]{3,2,1,0:T(8,128)S(1)} custom-call(f32[16,2]{1,0:T(8,128)S(1)} %copy-done.5, f32[33,32,128]{2,1,0:T(8,128)S(1)} %get-tuple-element.11.planes, f32[33,8,128]{2,1,0:T(8,128)S(1)} %get-tuple-element.12.beside, f32[5,32,128]{2,1,0:T(8,128)S(1)} %collective-permute-done.1.from_side), custom_call_target="tpu_custom_call" | custom-call | flops 2097152 | bytes 2097152 | tf_op jit(solution)/shard_map/widen/pallas_call | solution.py:492
  46.6 0.0 copy-start.1
  46.7 0.0 collective-permute-done.2.from_core
  46.7 2.7 %collective-permute-done.3.from_cross = f32[27,8,128]{2,1,0:T(8,128)S(1)} collective-permute-done((f32[27,8,128]{2,1,0:T(8,128)S(1)}, f32[27,8,128]{2,1,0:T(8,128)S(1)}, u32[]{:S(2)}, u32[]{:S(2)}) %collective-permute-start.3) | collective-permute-done | bytes 110624 | tf_op jit(solution)/shard_map/ppermute | solution.py:693
  49.4 6.0 %solve.1 = (f32[8,160,128]{2,1,0:T(8,128)}, f32[16,4,80,128]{3,2,1,0:T(8,128)S(1)}) custom-call(f32[16,2]{1,0:T(8,128)S(1)} %copy-done.5, f32[16,4,80,128]{3,2,1,0:T(8,128)S(1)} %widen.1.middle, f32[27,8,128]{2,1,0:T(8,128)S(1)} %collective-permute-done.2.from_core, f32[27,8,128]{2,1,0:T(8,128)S(1)} %collective-permute-done.3.from_cross), custom_call_target="tpu_custom_call", output_to_operand_aliasing={{1}: (1, {})} | custom-call | tf_op jit(solution)/shard_map/solve/pallas_call | solution.py:591
  55.5 3.5 %all-to-all-start.1 = ((f32[8,160,128]{2,1,0:T(8,128)}), f32[8,160,128]{2,1,0:T(8,128)S(1)}, u32[]{:S(2)}, u32[]{:S(2)}) async-start(f32[8,160,128]{2,1,0:T(8,128)} %get-tuple-element.16), calls=%async_computation.1 | async-start | bytes 1310720 | tf_op jit(solution)/shard_map/all_to_all | solution.py:677
  59.0 21.1 %all-to-all-done.1.units = f32[8,160,128]{2,1,0:T(8,128)S(1)} async-done(((f32[8,160,128]{2,1,0:T(8,128)}), f32[8,160,128]{2,1,0:T(8,128)S(1)}, u32[]{:S(2)}, u32[]{:S(2)}) %all-to-all-start.1) | async-done | bytes 655392 | tf_op jit(solution)/shard_map/all_to_all | solution.py:677
  80.1 0.6 collective-permute-start.4
  80.7 0.0 copy-done.1
  80.7 0.9 %finish_own.1.refs_0_ = f32[2,2,2,2,64,256]{5,4,3,2,1,0:T(8,128)} custom-call(f32[8,160,128]{2,1,0:T(8,128)S(1)} %all-to-all-done.1.units, f32[2,2,2,2,64,256]{5,4,3,2,1,0:T(8,128)S(1)} %bitcast.6, f32[2,2,2,64,256]{4,3,2,1,0:T(8,128)S(1)} %bitcast.8, f32[2,2,2,64,256]{4,3,2,1,0:T(8,128)S(1)} %bitcast.10), custom_call_target="tpu_custom_call" | custom-call | flops 1048576 | bytes 1048576 | tf_op jit(solution)/shard_map/finish_own/pallas_call | solution.py:646
  81.6 0.4 collective-permute-done.4.units
  82.0 0.9 %finish_other.1 = f32[2,2,2,2,64,256]{5,4,3,2,1,0:T(8,128)} custom-call(f32[8,96,128]{2,1,0:T(8,128)S(1)} %collective-permute-done.4.units, f32[2,2,2,2,64,256]{5,4,3,2,1,0:T(8,128)S(1)} %bitcast.7, f32[2,2,2,64,256]{4,3,2,1,0:T(8,128)S(1)} %bitcast.9, f32[2,2,2,64,256]{4,3,2,1,0:T(8,128)S(1)} %bitcast.11, ...), custom_call_target="tpu_custom_call", output_to_operand_aliasing={{}: (4, {})} | custom-call | flops 1048576 | bytes 1048576 | tf_op jit(solution)/shard_map/finish_other/pallas_call | solution.py:646
  (8 shorter events, 0.1 us)
Async XLA Ops:
  0.0 1.2 %copy-start = (f32[2,2,256,256]{3,2,1,0:T(8,128)S(1)}, f32[2,2,256,256]{3,2,1,0:T(8,128)}, u32[]{:S(2)}) copy-start(f32[2,2,256,256]{3,2,1,0:T(8,128)} %param.6) | copy-start | bytes 3145732
  1.2 36.2 %copy-start.2 = (f32[2,256,256]{2,1,0:T(8,128)S(1)}, f32[2,256,256]{2,1,0:T(8,128)}, u32[]{:S(2)}) copy-start(f32[2,256,256]{2,1,0:T(8,128)} %initial.3) | copy-start | bytes 1572868
  1.2 36.2 %copy-start.3 = (f32[2,256,256]{2,1,0:T(8,128)S(1)}, f32[2,256,256]{2,1,0:T(8,128)}, u32[]{:S(2)}) copy-start(f32[2,256,256]{2,1,0:T(8,128)} %last.3) | copy-start | bytes 1572868
  1.2 36.2 %copy-start.4 = (s32[256,256]{1,0:T(8,128)S(1)}, s32[256,256]{1,0:T(8,128)}, u32[]{:S(2)}) copy-start(s32[256,256]{1,0:T(8,128)} %cell_class.3) | copy-start | bytes 786436
  1.2 36.2 %copy-start.6 = (f32[8]{0:T(128)S(1)}, f32[8]{0:T(128)}, u32[]{:S(2)}) copy-start(f32[8]{0:T(128)} %table.3) | copy-start | bytes 100
  1.6 2.1 %collective-permute-start = (f32[8,96,128]{2,1,0:T(8,128)S(1)}, f32[8,96,128]{2,1,0:T(8,128)S(1)}, u32[]{:S(2)}, u32[]{:S(2)}) collective-permute-start(f32[8,96,128]{2,1,0:T(8,128)S(1)} %prepare_other.1), channel_id=1, source_target_pairs={{0,16},{16,0},{32,48},{48,32},{64,80},{80,64},{96,112},{112,96},{1... | collective-permute-start | bytes 1179656 | tf_op jit(solution)/shard_map/ppermute | solution.py:683
  37.4 7.5 %copy-start.5 = (f32[16,2]{1,0:T(8,128)S(1)}, f32[16,2]{1,0:T(8,128)}, u32[]{:S(2)}) copy-start(f32[16,2]{1,0:T(8,128)} %constant.19.clone.lam) | copy-start | bytes 388
  38.5 3.4 %collective-permute-start.1 = (f32[5,32,128]{2,1,0:T(8,128)S(1)}, f32[5,32,128]{2,1,0:T(8,128)S(1)}, u32[]{:S(2)}, u32[]{:S(2)}) collective-permute-start(f32[5,32,128]{2,1,0:T(8,128)S(1)} %get-tuple-element.13), channel_id=1, source_target_pairs={{0,16},{32,224},{224,32},{192,193},{193,192},{225,33},{33,225},{1,... | collective-permute-start | bytes 245768 | tf_op jit(solution)/shard_map/ppermute | solution.py:687
  41.9 4.8 %collective-permute-start.2 = (f32[27,8,128]{2,1,0:T(8,128)S(1)}, f32[27,8,128]{2,1,0:T(8,128)S(1)}, u32[]{:S(2)}, u32[]{:S(2)}) collective-permute-start(f32[27,8,128]{2,1,0:T(8,128)S(1)} %pad_maximum_fusion), channel_id=1, source_target_pairs={{0,16},{32,48},{224,240},{192,208},{193,209},{225,241},{33,49},{1,... | collective-permute-start | bytes 331784 | tf_op jit(solution)/shard_map/ppermute | solution.py:694
  44.9 4.6 %collective-permute-start.3 = (f32[27,8,128]{2,1,0:T(8,128)S(1)}, f32[27,8,128]{2,1,0:T(8,128)S(1)}, u32[]{:S(2)}, u32[]{:S(2)}) collective-permute-start(f32[27,8,128]{2,1,0:T(8,128)S(1)} %pad_maximum_fusion.1), channel_id=1, source_target_pairs={{0,28},{32,60},{224,252},{192,220},{193,221},{225,253},{33,61},{1,... | collective-permute-start | bytes 331784 | tf_op jit(solution)/shard_map/ppermute | solution.py:693
  46.6 34.1 %copy-start.1 = (f32[2,2,256,256]{3,2,1,0:T(8,128)S(1)}, f32[2,2,256,256]{3,2,1,0:T(8,128)}, u32[]{:S(2)}) copy-start(f32[2,2,256,256]{3,2,1,0:T(8,128)} %param.6) | copy-start | bytes 3145732
  55.5 24.6 %all-to-all-start.1 = ((f32[8,160,128]{2,1,0:T(8,128)}), f32[8,160,128]{2,1,0:T(8,128)S(1)}, u32[]{:S(2)}, u32[]{:S(2)}) async-start(f32[8,160,128]{2,1,0:T(8,128)} %get-tuple-element.16), calls=%async_computation.1 | async-start | bytes 1310720 | tf_op jit(solution)/shard_map/all_to_all | solution.py:677
  80.1 1.9 %collective-permute-start.4 = (f32[8,96,128]{2,1,0:T(8,128)S(1)}, f32[8,96,128]{2,1,0:T(8,128)S(1)}, u32[]{:S(2)}, u32[]{:S(2)}) collective-permute-start(f32[8,96,128]{2,1,0:T(8,128)S(1)} %constant_dynamic-slice_fusion), channel_id=1, source_target_pairs={{0,16},{16,0},{32,48},{48,32},{64,80},{80,64},{96,112},{112,96},{1... | collective-permute-start | bytes 1179656 | tf_op jit(solution)/shard_map/ppermute | solution.py:698

commit v6 on v5

--- a/solution.py
+++ b/solution.py
@@ -96,15 +96,8 @@
     return pltpu.roll(value, lax.rem(shift + 256, 128), 1)
 
 
-def prepare_kernel(other, forcing, out, held, arrived):
-    tm, odd_x, odd_y, core = place()[:4]
-    core = core ^ other
-    copies = []
-    for upper in range(2):
-        copies.append(
-            pltpu.make_async_copy(forcing.at[:, :, upper, core], held.at[upper], arrived.at[upper])
-        )
-        copies[upper].start()
+def prepare_kernel(forcing, out):
+    tm, odd_x, odd_y = place()[:3]
     low = lanes(32) < 64
     weight = jnp.float32(1.0)
     for bit in range(4):
@@ -113,11 +106,10 @@
     weight_two = weight * np.float32(FACTOR)
     weight_three = weight * np.float32(-FACTOR * FACTOR)
     for upper in range(2):
-        copies[upper].wait()
         for half in range(2):
             cols = slice(128 * half, 128 * half + 128)
-            first_u, second_u = held[upper, 0, 0, :, cols], held[upper, 0, 1, :, cols]
-            first_w, second_w = held[upper, 1, 0, :, cols], held[upper, 1, 1, :, cols]
+            first_u, second_u = forcing[0, 0, upper, :, cols], forcing[0, 1, upper, :, cols]
+            first_w, second_w = forcing[1, 0, upper, :, cols], forcing[1, 1, upper, :, cols]
             units = (
                 weight * (first_w + first_u),
                 weight_two * (second_w + second_u - first_u),
@@ -131,17 +123,17 @@
                 out[right, rows, :] = pack_right(unit, low)
 
 
-def prepare(forcing, other):
+def prepare(forcing, core, name):
+    rows = lax.dynamic_index_in_dim(forcing.reshape(2, 2, 2, 2, 64, 256), core, 3, keepdims=False)
     return pl.pallas_call(
-        functools.partial(prepare_kernel, other),
-        in_specs=[pl.BlockSpec(memory_space=pltpu.HBM)],
+        prepare_kernel,
+        in_specs=[pl.BlockSpec(memory_space=pltpu.VMEM)],
         out_specs=pl.BlockSpec(memory_space=pltpu.VMEM),
         out_shape=jax.ShapeDtypeStruct((8, 96, 128), jnp.float32),
-        scratch_shapes=[pltpu.VMEM((2, 2, 2, 64, 256), jnp.float32), pltpu.SemaphoreType.DMA((2,))],
         compiler_params=params(),
         cost_estimate=cost(2**20),
-        name="prepare_other" if other else "prepare_own",
-    )(forcing.reshape(2, 2, 2, 2, 64, 256))
+        name=name,
+    )(rows)
 
 
 def merge_kernel(mine, received, out):
@@ -680,8 +672,10 @@
 def per_device(forcing, initial, previous_last, cell_class, courant_table):
     core = lax.axis_index("tm") & 1
     lam = jnp.asarray(lam_squares())
-    theirs = lax.ppermute(prepare(forcing, 1), "tm", CORES)
-    received = chips_exchange(merge(prepare(forcing, 0), theirs))
+    theirs = prepare(forcing, 1 - core, "prepare_other")
+    theirs, rest = lax.optimization_barrier((theirs, forcing))
+    theirs = lax.ppermute(theirs, "tm", CORES)
+    received = chips_exchange(merge(prepare(rest, core, "prepare_own"), theirs))
     fields = (courant_table, cell_class, initial, previous_last, received)
     planes, side = transform(*fields)
     from_side = lax.ppermute(side, AXES, TO_SIDE)
@@ -693,8 +687,9 @@
     from_cross = lax.ppermute(strip(to_cross, 24 * core), AXES, TO_CROSS)
     from_core = lax.ppermute(strip(to_core, 24 * (1 - core)), AXES, TO_CORE)
     middle = widen(lam, planes, beside, from_side)
-    returned = chips_exchange(solve(lam, middle, from_core, from_cross))
-    wanted = lax.dynamic_slice_in_dim(returned, 64 * (1 - core), 96, axis=1)
+    solved, is_first = lax.optimization_barrier((solve(lam, middle, from_core, from_cross), core == 0))
+    returned = chips_exchange(solved)
+    wanted = jnp.where(is_first, returned[:, 64:160], returned[:, 0:96])
     other = lax.ppermute(wanted, "tm", CORES)
     result = finish(returned, forcing, initial, previous_last)
     result = finish(other, forcing, initial, previous_last, result)

time: 83.9 us -> 82.6 us (0.985)
  blocking collectives: 33.5 us -> 57.9 us
  waiting for transfers between devices: 26.9 us -> 4.83 us
  starting transfers between devices: 8.76 us -> 5.22 us
  Pallas kernels: 12.4 us -> 11.3 us
  local copies, waits for them, and re-layouts: 1.28 us -> 2.2 us
    all_to_all x1 -> x2, blocking collectives: 33.5 us -> 57.9 us  [chips_exchange(): lax.all_to_all(pieces, 'tm', 0, 0, axis_index_groups=CHIPS, tiled=True)]
    all_to_all x1 -> x0, waiting for transfers between devices: 21.1 us -> none  [chips_exchange(): lax.all_to_all(pieces, 'tm', 0, 0, axis_index_groups=CHIPS, tiled=True)]
    all_to_all x1 -> x0, starting transfers between devices: 3.54 us -> none  [chips_exchange(): lax.all_to_all(pieces, 'tm', 0, 0, axis_index_groups=CHIPS, tiled=True)]
    squeeze x0 -> x2, local copies, waits for them, and re-layouts: none -> 2.15 us  [prepare(): lax.dynamic_index_in_dim(forcing.reshape(2, 2, 2, 2, 64, 256), core, 3, k...]
    unnamed x14 -> x12, local copies, waits for them, and re-layouts: 1.25 us -> 0.04 us
    ppermute x1, waiting for transfers between devices: 1.04 us -> 0.08 us  [per_device(): theirs = lax.ppermute(theirs, 'tm', CORES)]
    pallas_call x1, Pallas kernels: 6.04 us -> 5.2 us  [solve(): pl.pallas_call(solve_kernel, in_specs=[pl.BlockSpec(memory_space=pltpu.SM...]
  transfers between devices with their start and end apart: 6 -> 5, of which waited for: 5 -> 4; matrix products, arithmetic and copies ran while one was open for 0% -> 1% of each run, Pallas kernels for 5% -> 5%
where the time goes in v6:
time: 82.6 us; the launch traced here: 81.7 us
  blocking collectives  57.9 us (70%)
  Pallas kernels  11.3 us (14%)
  starting transfers between devices  5.22 us (6%)
  waiting for transfers between devices  4.83 us (6%)
  local copies, waits for them, and re-layouts  2.2 us (3%)
    all_to_all x2, blocking collectives, chips_exchange(): lax.all_to_all(pieces, 'tm', 0, 0, axis_index_groups=CHIPS, tiled=True)  57.9 us
    pallas_call x1, Pallas kernels, solve(): pl.pallas_call(solve_kernel, in_specs=[pl.BlockSpec(memory_space=pltpu.SM...  5.2 us
    ppermute x1, starting transfers between devices, per_device(): from_core = lax.ppermute(strip(to_core, 24 * (1 - core)), AXES, TO_CORE)  2.95 us
    ppermute x1, waiting for transfers between devices, per_device(): from_cross = lax.ppermute(strip(to_cross, 24 * core), AXES, TO_CROSS)  2.74 us
    squeeze x2, local copies, waits for them, and re-layouts, prepare(): lax.dynamic_index_in_dim(forcing.reshape(2, 2, 2, 2, 64, 256), core, 3, k...  2.15 us
    pallas_call x2, Pallas kernels, finish(): pl.pallas_call(functools.partial(finish_kernel, int(other)), in_specs=[pl...  1.85 us
    pallas_call x1, Pallas kernels, widen(): pl.pallas_call(widen_kernel, in_specs=[pl.BlockSpec(memory_space=pltpu.SM...  1.67 us
  transfers between devices with their start and end apart: 5, of which 4 were waited for; matrix products, arithmetic and copies ran while one was open for 1% of the time, Pallas kernels for 5%

profile of v6, /device:TPU:33, one launch (start us, length us, event | category | flops | bytes accessed | tf_op | source)
XLA Modules:
  0.0 81.7 jit_solution(17659449061670270840)
XLA Ops:
  0.0 1.1 %dynamic-slice_bitcast_fusion.1.forcing = f32[2,2,2,64,256]{4,3,2,1,0:T(8,128)S(1)} fusion(f32[2,2,2,2,64,256]{5,4,3,2,1,0:T(8,128)} %bitcast.11, s32[]{:T(128)S(6)} %select_n.21), kind=kLoop, calls=%fused_computation.1 | loop fusion | bytes 1048580 | tf_op jit(solution)/shard_map/jit(dynamic_index_in_dim)/squeeze | solution.py:127
  1.1 0.2 prepare_other.1
  1.3 0.0 copy-start.1
  1.3 0.0 copy-start.2
  1.3 0.0 copy-start.3
  1.3 0.0 copy-start.5
  1.3 0.8 collective-permute-start
  2.1 1.1 %dynamic-slice_bitcast_fusion.forcing = f32[2,2,2,64,256]{4,3,2,1,0:T(8,128)S(1)} fusion(f32[2,2,2,2,64,256]{5,4,3,2,1,0:T(8,128)} %bitcast.12, s32[]{:T(128)S(6)} %select_n.22), kind=kLoop, calls=%fused_computation | loop fusion | bytes 1048580 | tf_op jit(solution)/shard_map/jit(dynamic_index_in_dim)/squeeze | solution.py:127
  3.2 0.2 prepare_own.1.mine
  3.3 0.1 collective-permute-done.received
  3.4 0.2 merge.1
  3.7 33.5 %all_to_all.10.received = f32[8,184,128]{2,1,0:T(8,128)S(1)} all-to-all(f32[8,184,128]{2,1,0:T(8,128)S(1)} %merge.1), channel_id=1, replica_groups={{0,32,64,96,128,160,192,224},{16,48,80,112,144,176,208,240},{1,33,65,97..., dimensions={0} | all-to-all | bytes 1507328 | tf_op jit(solution)/shard_map/all_to_all | solution.py:669
  37.2 0.0 copy-done.1
  37.2 0.0 copy-done.2
  37.2 0.0 copy-done.3
  37.2 0.0 copy-start.4
  37.2 1.0 %transform.1 = (f32[33,32,128]{2,1,0:T(8,128)S(1)}, f32[5,32,128]{2,1,0:T(8,128)S(1)}) custom-call(f32[8]{0:T(128)S(1)} %copy-done.5, s32[256,256]{1,0:T(8,128)S(1)} %copy-done.3, f32[2,256,256]{2,1,0:T(8,128)S(1)} %copy-done.1, f32[2,256,256]{2,1,0:T(8,128)S(1)} %copy-done.2, f32[8,184,128]{2,1,0:T(8,128)S(1)} %all_to_all.10.received), custom_call_target="tpu_custom_call" | custom-call | tf_op jit(solution)/shard_map/transform/pallas_call | solution.py:324
  38.2 0.8 %collective-permute-start.1 = (f32[5,32,128]{2,1,0:T(8,128)S(1)}, f32[5,32,128]{2,1,0:T(8,128)S(1)}, u32[]{:S(2)}, u32[]{:S(2)}) collective-permute-start(f32[5,32,128]{2,1,0:T(8,128)S(1)} %get-tuple-element.19), channel_id=1, source_target_pairs={{0,16},{32,224},{224,32},{192,193},{193,192},{225,33},{33,225},{1,... | collective-permute-start | bytes 245768 | tf_op jit(solution)/shard_map/ppermute | solution.py:681
  39.1 0.9 %strips.1 = (f32[33,8,128]{2,1,0:T(8,128)S(1)}, f32[22,8,128]{2,1,0:T(8,128)S(1)}, f32[22,8,128]{2,1,0:T(8,128)S(1)}) custom-call(f32[8]{0:T(128)S(1)} %copy-done.5, s32[256,256]{1,0:T(8,128)S(1)} %copy-done.3, f32[2,256,256]{2,1,0:T(8,128)S(1)} %copy-done.1, f32[2,256,256]{2,1,0:T(8,128)S(1)} %copy-done.2, f32[8,184,128]{2,1,0:T(8,128)S(1)} %all_to_all.10.received, ...), custom_call_target="tpu_custom_call" | custom-call | flops 1048576 | bytes 1048576 | tf_op jit(solution)/shard_map/strips/pallas_call | solution.py:364
  40.0 1.6 %collective-permute-done.1.from_side = f32[5,32,128]{2,1,0:T(8,128)S(1)} collective-permute-done((f32[5,32,128]{2,1,0:T(8,128)S(1)}, f32[5,32,128]{2,1,0:T(8,128)S(1)}, u32[]{:S(2)}, u32[]{:S(2)}) %collective-permute-start.1) | collective-permute-done | bytes 81952 | tf_op jit(solution)/shard_map/ppermute | solution.py:681
  41.6 2.9 %collective-permute-start.2 = (f32[27,8,128]{2,1,0:T(8,128)S(1)}, f32[27,8,128]{2,1,0:T(8,128)S(1)}, u32[]{:S(2)}, u32[]{:S(2)}) collective-permute-start(f32[27,8,128]{2,1,0:T(8,128)S(1)} %pad_maximum_fusion), channel_id=1, source_target_pairs={{0,16},{32,48},{224,240},{192,208},{193,209},{225,241},{33,49},{1,... | collective-permute-start | bytes 331784 | tf_op jit(solution)/shard_map/ppermute | solution.py:688
  44.6 0.1 collective-permute-start.3
  44.7 1.7 %widen.1.middle = f32[16,4,80,128]{3,2,1,0:T(8,128)S(1)} custom-call(f32[16,2]{1,0:T(8,128)S(1)} %copy-done.4, f32[33,32,128]{2,1,0:T(8,128)S(1)} %get-tuple-element.17.planes, f32[33,8,128]{2,1,0:T(8,128)S(1)} %get-tuple-element.18.beside, f32[5,32,128]{2,1,0:T(8,128)S(1)} %collective-permute-done.1.from_side), custom_call_target="tpu_custom_call" | custom-call | flops 2097152 | bytes 2097152 | tf_op jit(solution)/shard_map/widen/pallas_call | solution.py:484
  46.4 0.0 copy-start
  46.4 0.0 collective-permute-done.2.from_core
  46.4 2.7 %collective-permute-done.3.from_cross = f32[27,8,128]{2,1,0:T(8,128)S(1)} collective-permute-done((f32[27,8,128]{2,1,0:T(8,128)S(1)}, f32[27,8,128]{2,1,0:T(8,128)S(1)}, u32[]{:S(2)}, u32[]{:S(2)}) %collective-permute-start.3) | collective-permute-done | bytes 110624 | tf_op jit(solution)/shard_map/ppermute | solution.py:687
  49.2 5.2 %solve.1 = (f32[8,160,128]{2,1,0:T(8,128)S(1)}, f32[16,4,80,128]{3,2,1,0:T(8,128)S(1)}) custom-call(f32[16,2]{1,0:T(8,128)S(1)} %copy-done.4, f32[16,4,80,128]{3,2,1,0:T(8,128)S(1)} %widen.1.middle, f32[27,8,128]{2,1,0:T(8,128)S(1)} %collective-permute-done.2.from_core, ...), custom_call_target="tpu_custom_call", output_to_operand_aliasing={{1}: (1, {})} | custom-call | tf_op jit(solution)/shard_map/solve/pallas_call | solution.py:583
  54.4 24.4 %all_to_all.11.units = f32[8,160,128]{2,1,0:T(8,128)S(1)} all-to-all(f32[8,160,128]{2,1,0:T(8,128)S(1)} %get-tuple-element.24), channel_id=1, replica_groups={{0,32,64,96,128,160,192,224},{16,48,80,112,144,176,208,240},{1,33,65,97..., dimensions={0} | all-to-all | bytes 1310720 | tf_op jit(solution)/shard_map/all_to_all | solution.py:669
  78.8 0.6 collective-permute-start.4
  79.4 0.9 %finish_own.1.refs_0_ = f32[2,2,2,2,64,256]{5,4,3,2,1,0:T(8,128)} custom-call(f32[8,160,128]{2,1,0:T(8,128)S(1)} %all_to_all.11.units, f32[2,2,2,2,64,256]{5,4,3,2,1,0:T(8,128)S(1)} %bitcast.13, f32[2,2,2,64,256]{4,3,2,1,0:T(8,128)S(1)} %bitcast.15, f32[2,2,2,64,256]{4,3,2,1,0:T(8,128)S(1)} %bitcast.17), custom_call_target="tpu_custom_call" | custom-call | flops 1048576 | bytes 1048576 | tf_op jit(solution)/shard_map/finish_own/pallas_call | solution.py:638
  80.3 0.4 collective-permute-done.4.units
  80.8 0.9 %finish_other.1 = f32[2,2,2,2,64,256]{5,4,3,2,1,0:T(8,128)} custom-call(f32[8,96,128]{2,1,0:T(8,128)S(1)} %collective-permute-done.4.units, f32[2,2,2,2,64,256]{5,4,3,2,1,0:T(8,128)S(1)} %bitcast.14, f32[2,2,2,64,256]{4,3,2,1,0:T(8,128)S(1)} %bitcast.16, f32[2,2,2,64,256]{4,3,2,1,0:T(8,128)S(1)} %bitcast.18, ...), custom_call_target="tpu_custom_call", output_to_operand_aliasing={{}: (4, {})} | custom-call | flops 1048576 | bytes 1048576 | tf_op jit(solution)/shard_map/finish_other/pallas_call | solution.py:638
  (7 shorter events, 0.1 us)
Async XLA Ops:
  1.3 35.9 %copy-start.1 = (f32[2,256,256]{2,1,0:T(8,128)S(1)}, f32[2,256,256]{2,1,0:T(8,128)}, u32[]{:S(2)}) copy-start(f32[2,256,256]{2,1,0:T(8,128)} %initial.3) | copy-start | bytes 1572868
  1.3 35.9 %copy-start.2 = (f32[2,256,256]{2,1,0:T(8,128)S(1)}, f32[2,256,256]{2,1,0:T(8,128)}, u32[]{:S(2)}) copy-start(f32[2,256,256]{2,1,0:T(8,128)} %last.3) | copy-start | bytes 1572868
  1.3 35.9 %copy-start.3 = (s32[256,256]{1,0:T(8,128)S(1)}, s32[256,256]{1,0:T(8,128)}, u32[]{:S(2)}) copy-start(s32[256,256]{1,0:T(8,128)} %cell_class.3) | copy-start | bytes 786436
  1.3 35.9 %copy-start.5 = (f32[8]{0:T(128)S(1)}, f32[8]{0:T(128)}, u32[]{:S(2)}) copy-start(f32[8]{0:T(128)} %table.3) | copy-start | bytes 100
  1.3 2.1 %collective-permute-start = (f32[8,96,128]{2,1,0:T(8,128)S(1)}, f32[8,96,128]{2,1,0:T(8,128)S(1)}, u32[]{:S(2)}, u32[]{:S(2)}) collective-permute-start(f32[8,96,128]{2,1,0:T(8,128)S(1)} %prepare_other.1), channel_id=1, source_target_pairs={{0,16},{16,0},{32,48},{48,32},{64,80},{80,64},{96,112},{112,96},{1... | collective-permute-start | bytes 1179656 | tf_op jit(solution)/shard_map/ppermute | solution.py:677
  37.2 7.5 %copy-start.4 = (f32[16,2]{1,0:T(8,128)S(1)}, f32[16,2]{1,0:T(8,128)}, u32[]{:S(2)}) copy-start(f32[16,2]{1,0:T(8,128)} %constant.24.clone.lam) | copy-start | bytes 388
  38.2 3.4 %collective-permute-start.1 = (f32[5,32,128]{2,1,0:T(8,128)S(1)}, f32[5,32,128]{2,1,0:T(8,128)S(1)}, u32[]{:S(2)}, u32[]{:S(2)}) collective-permute-start(f32[5,32,128]{2,1,0:T(8,128)S(1)} %get-tuple-element.19), channel_id=1, source_target_pairs={{0,16},{32,224},{224,32},{192,193},{193,192},{225,33},{33,225},{1,... | collective-permute-start | bytes 245768 | tf_op jit(solution)/shard_map/ppermute | solution.py:681
  41.6 4.8 %collective-permute-start.2 = (f32[27,8,128]{2,1,0:T(8,128)S(1)}, f32[27,8,128]{2,1,0:T(8,128)S(1)}, u32[]{:S(2)}, u32[]{:S(2)}) collective-permute-start(f32[27,8,128]{2,1,0:T(8,128)S(1)} %pad_maximum_fusion), channel_id=1, source_target_pairs={{0,16},{32,48},{224,240},{192,208},{193,209},{225,241},{33,49},{1,... | collective-permute-start | bytes 331784 | tf_op jit(solution)/shard_map/ppermute | solution.py:688
  44.6 4.6 %collective-permute-start.3 = (f32[27,8,128]{2,1,0:T(8,128)S(1)}, f32[27,8,128]{2,1,0:T(8,128)S(1)}, u32[]{:S(2)}, u32[]{:S(2)}) collective-permute-start(f32[27,8,128]{2,1,0:T(8,128)S(1)} %pad_maximum_fusion.1), channel_id=1, source_target_pairs={{0,28},{32,60},{224,252},{192,220},{193,221},{225,253},{33,61},{1,... | collective-permute-start | bytes 331784 | tf_op jit(solution)/shard_map/ppermute | solution.py:687
  46.4 33.0 %copy-start = (f32[2,2,256,256]{3,2,1,0:T(8,128)S(1)}, f32[2,2,256,256]{3,2,1,0:T(8,128)}, u32[]{:S(2)}) copy-start(f32[2,2,256,256]{3,2,1,0:T(8,128)} %param.6) | copy-start | bytes 3145732
  78.8 1.9 %collective-permute-start.4 = (f32[8,96,128]{2,1,0:T(8,128)S(1)}, f32[8,96,128]{2,1,0:T(8,128)S(1)}, u32[]{:S(2)}, u32[]{:S(2)}) collective-permute-start(f32[8,96,128]{2,1,0:T(8,128)S(1)} %slice_select_fusion), channel_id=1, source_target_pairs={{0,16},{16,0},{32,48},{48,32},{64,80},{80,64},{96,112},{112,96},{1... | collective-permute-start | bytes 1179656 | tf_op jit(solution)/shard_map/ppermute | solution.py:693

commit v7 on v6

--- a/solution.py
+++ b/solution.py
@@ -265,7 +265,7 @@
 
 def in_slots(planes, start):
     groups = []
-    for g in range(5):
+    for g in range((len(planes) + 7) // 8):
         value = jnp.zeros((8, 128), jnp.float32)
         for m, plane in enumerate(planes[8 * g : 8 * g + 8]):
             value = jnp.where(slots(m), turn(plane, 8 * m - start), value)
@@ -277,12 +277,15 @@
     return pack_left(jnp.where(inner == 1, half_turn(value), value), lanes(32) < 64)
 
 
+def columns_in_slots(block, inner):
+    result = jnp.zeros((8, 128), jnp.float32)
+    for r in range(4):
+        result = jnp.where(slots(r), turn(block[8 * r : 8 * r + 8], 8 * r - 56 * inner), result)
+    return result
+
+
 def beside_of(value, inner):
-    other = block_of(value, 1 - inner)
-    beside = jnp.zeros((8, 128), jnp.float32)
-    for r in range(4):
-        beside = jnp.where(slots(r), turn(other[8 * r : 8 * r + 8], 8 * r - 56 * inner), beside)
-    return beside
+    return columns_in_slots(block_of(value, 1 - inner), inner)
 
 
 def pair_fields(table, cell_class, initial, last):
@@ -312,15 +315,17 @@
             part = [received[t, 32 * k + 8 * r : 32 * k + 8 * r + 8, :] for k in range(4)]
             part[0] = part[0] + received[(t + 7) % 8, 128 + 8 * r : 136 + 8 * r, :]
             steps.extend(part)
-        planes = forward(with_start(steps, start_u[rows], start_w[rows])) + [courant[rows]]
-        for p in range(33):
+        planes = forward(with_start(steps, start_u[rows], start_w[rows]))
+        for p in range(32):
             planes_out[p, rows, :] = planes[p]
         for g, value in enumerate(in_slots(planes, 56 * inner)):
-            side_out[g, rows, :] = value
+            side_out[4 * g + r] = value
+    planes_out[32] = courant
+    side_out[16] = columns_in_slots(courant, inner)
 
 
 def transform(table, cell_class, initial, last, received):
-    shapes = ((33, 32, 128), (5, 32, 128))
+    shapes = ((33, 32, 128), (17, 8, 128))
     return pl.pallas_call(
         transform_kernel,
         in_specs=[pl.BlockSpec(memory_space=pltpu.SMEM)] + [pl.BlockSpec(memory_space=pltpu.VMEM)] * 4,
@@ -352,7 +357,7 @@
         one, two = 2 * j, min(2 * j + 1, 32)
         top.append(jnp.where(low, planes[one, 0:8, :], half_turn(planes[two, 0:8, :])))
         bottom.append(jnp.where(low, half_turn(planes[one, 24:32, :]), planes[two, 24:32, :]))
-    top.extend(in_slots(beside, 0))
+    top.extend(in_slots(beside, -64))
     bottom.extend(in_slots(beside, 88))
     for i in range(22):
         core_out[i] = jnp.where(core == 0, bottom[i], top[i])
@@ -458,10 +463,11 @@
         for r in range(8):
             part = slice(8 * (r % 4), 8 * (r % 4) + 8)
             shift = 0 if r < 4 else 64
+            tile, start = (16, 8 * (r % 4)) if group is None else (4 * group + r % 4, offset)
             parts.append(
                 merged(
                     turn(planes[p, part, :], shift),
-                    turn(from_side[group, part, :], both[0] - shift - offset),
+                    turn(from_side[tile], both[0] - shift - start),
                     turn(edge, both[1] - shift - 8 * (r % 4)),
                     both,
                 )
@@ -469,7 +475,7 @@
         return jnp.concatenate(parts, axis=0)
 
     mask = in_grid(0, 64, col0)
-    courant = jnp.where(mask, extended(32, 4, 0), 0.0)
+    courant = jnp.where(mask, extended(32, None, 0), 0.0)
     inside = jnp.where(mask, 1.0, 0.0)
 
     def work(j, special, group, offset):
@@ -492,7 +498,7 @@
     )(lam, planes, beside, from_side)
 
 
-def solve_kernel(lam, middle, from_core, from_cross, out, full, solved, wide):
+def solve_kernel(lam, middle, from_cross, from_core, out, full, solved, wide):
     core, _, _, inner, row0, col0 = place()[3:]
     both = bases(inner)
     low = lanes(32) < 64
@@ -502,14 +508,14 @@
         one, two = from_core[index], from_cross[index]
         return jnp.where(core == 1, one, two), jnp.where(core == 1, two, one)
 
-    def extended(pair, odd, group, offset):
-        centre, edge, side = halo(pair), halo(17 + group), halo(22 + group)
+    def extended(pair, odd, group, offset, in_slot=0):
+        centre, corners = halo(pair), halo(17 + group)
         return jnp.concatenate(
             [
                 merged(
                     half_turn(centre[i]) if odd else centre[i],
-                    turn(side[i], both[0] - offset - (0 if i else 64)),
-                    turn(edge[i], both[1] - offset),
+                    turn(corners[i], both[0] - offset - (0 if i else 64 + in_slot)),
+                    turn(corners[i], both[1] - offset - (64 if i else 0)),
                     both,
                 )
                 for i in range(2)
@@ -518,7 +524,7 @@
         )
 
     mask = jnp.concatenate([in_grid(row0 - 8, 8, col0), in_grid(row0 + 64, 8, col0)], axis=0)
-    courant = jnp.where(mask, extended(16, False, 4, 0), 0.0)
+    courant = jnp.where(mask, extended(16, False, 4, 0, 24), 0.0)
     inside = jnp.where(mask, 1.0, 0.0)
 
     def work(j, special, group, offset):
@@ -579,7 +585,7 @@
                 out[(t + 1) % 8, part, :] = value * np.float32(ALPHA) if n == 31 else value
 
 
-def solve(lam, middle, from_core, from_cross):
+def solve(lam, middle, from_cross, from_core):
     return pl.pallas_call(
         solve_kernel,
         in_specs=[pl.BlockSpec(memory_space=pltpu.SMEM)] + [pl.BlockSpec(memory_space=pltpu.VMEM)] * 3,
@@ -595,7 +601,7 @@
         ],
         compiler_params=params(),
         name="solve",
-    )(lam, middle, from_core, from_cross)[0]
+    )(lam, middle, from_cross, from_core)[0]
 
 
 def finish_kernel(other, units, forcing, initial, last, *refs):
@@ -675,21 +681,28 @@
     theirs = prepare(forcing, 1 - core, "prepare_other")
     theirs, rest = lax.optimization_barrier((theirs, forcing))
     theirs = lax.ppermute(theirs, "tm", CORES)
-    received = chips_exchange(merge(prepare(rest, core, "prepare_own"), theirs))
+    merged_units, is_upper, is_lower = lax.optimization_barrier(
+        (merge(prepare(rest, core, "prepare_own"), theirs), core == 0, core == 1)
+    )
+    received = chips_exchange(merged_units)
     fields = (courant_table, cell_class, initial, previous_last, received)
     planes, side = transform(*fields)
     from_side = lax.ppermute(side, AXES, TO_SIDE)
     beside, to_core, to_cross = strips(*fields, planes)
 
-    def strip(main, start):
-        return jnp.concatenate([main, lax.dynamic_slice_in_dim(from_side, start, 8, axis=1)], axis=0)
-
-    from_cross = lax.ppermute(strip(to_cross, 24 * core), AXES, TO_CROSS)
-    from_core = lax.ppermute(strip(to_core, 24 * (1 - core)), AXES, TO_CORE)
+    rows = from_side[:16].reshape(4, 4, 8, 128)
+    low = lax.broadcasted_iota(jnp.int32, (5, 8, 128), 2) < 64
+
+    def strip(main, is_bottom):
+        side = jnp.where(is_bottom, rows[:, 3], rows[:, 0])
+        side = jnp.concatenate([side, from_side[16:]], axis=0)
+        return jnp.concatenate([main[:17], jnp.where(low != is_bottom, side, main[17:])], axis=0)
+
+    from_cross = lax.ppermute(strip(to_cross, is_lower), AXES, TO_CROSS)
+    from_core = lax.ppermute(strip(to_core, is_upper), AXES, TO_CORE)
     middle = widen(lam, planes, beside, from_side)
-    solved, is_first = lax.optimization_barrier((solve(lam, middle, from_core, from_cross), core == 0))
-    returned = chips_exchange(solved)
-    wanted = jnp.where(is_first, returned[:, 64:160], returned[:, 0:96])
+    returned = chips_exchange(solve(lam, middle, from_cross, from_core))
+    wanted = jnp.where(is_upper, returned[:, 64:160], returned[:, 0:96])
     other = lax.ppermute(wanted, "tm", CORES)
     result = finish(returned, forcing, initial, previous_last)
     result = finish(other, forcing, initial, previous_last, result)

time: 82.6 us -> 81.1 us (0.982)
  waiting for transfers between devices: 4.83 us -> 2.16 us
  blocking collectives: 57.9 us -> 59.7 us
    ppermute x2, waiting for transfers between devices: 2.74 us -> 0.25 us  [the longest x1 0.25 us: per_device(): from_cross = lax.ppermute(strip(to_cross, is_lower), AXES, TO_CROSS)]
    all_to_all x2, blocking collectives: 57.9 us -> 59.7 us  [chips_exchange(): lax.all_to_all(pieces, 'tm', 0, 0, axis_index_groups=CHIPS, tiled=True)]
where the time goes in v7:
time: 81.1 us; the launch traced here: 80.9 us
  blocking collectives  59.7 us (74%)
  Pallas kernels  11.3 us (14%)
  starting transfers between devices  5.24 us (6%)
  local copies, waits for them, and re-layouts  2.21 us (3%)
  waiting for transfers between devices  2.16 us (3%)
    all_to_all x2, blocking collectives, chips_exchange(): lax.all_to_all(pieces, 'tm', 0, 0, axis_index_groups=CHIPS, tiled=True)  59.7 us
    pallas_call x1, Pallas kernels, solve(): pl.pallas_call(solve_kernel, in_specs=[pl.BlockSpec(memory_space=pltpu.SM...  5.22 us
    ppermute x1, starting transfers between devices, per_device(): from_cross = lax.ppermute(strip(to_cross, is_lower), AXES, TO_CROSS)  2.8 us
    squeeze x2, local copies, waits for them, and re-layouts, prepare(): lax.dynamic_index_in_dim(forcing.reshape(2, 2, 2, 2, 64, 256), core, 3, k...  2.15 us
    pallas_call x2, Pallas kernels, finish(): pl.pallas_call(functools.partial(finish_kernel, int(other)), in_specs=[pl...  1.85 us
    pallas_call x1, Pallas kernels, widen(): pl.pallas_call(widen_kernel, in_specs=[pl.BlockSpec(memory_space=pltpu.SM...  1.68 us
  transfers between devices with their start and end apart: 5, of which 4 were waited for; matrix products, arithmetic and copies ran while one was open for 1% of the time, Pallas kernels for 5%

profile of v7, /device:TPU:33, one launch (start us, length us, event | category | flops | bytes accessed | tf_op | source)
XLA Modules:
  0.0 80.9 jit_solution(9781091073880017732)
XLA Ops:
  0.0 1.1 %dynamic-slice_bitcast_fusion.1.forcing = f32[2,2,2,64,256]{4,3,2,1,0:T(8,128)S(1)} fusion(f32[2,2,2,2,64,256]{5,4,3,2,1,0:T(8,128)} %bitcast.28, s32[]{:T(128)S(6)} %select_n.42), kind=kLoop, calls=%fused_computation.1 | loop fusion | bytes 1048580 | tf_op jit(solution)/shard_map/jit(dynamic_index_in_dim)/squeeze | solution.py:127
  1.1 0.2 prepare_other.1
  1.3 0.0 copy-start.1
  1.3 0.0 copy-start.2
  1.3 0.0 copy-start.3
  1.3 0.0 copy-start.5
  1.3 0.8 collective-permute-start
  2.1 1.1 %dynamic-slice_bitcast_fusion.forcing = f32[2,2,2,64,256]{4,3,2,1,0:T(8,128)S(1)} fusion(f32[2,2,2,2,64,256]{5,4,3,2,1,0:T(8,128)} %bitcast.29, s32[]{:T(128)S(6)} %select_n.43), kind=kLoop, calls=%fused_computation | loop fusion | bytes 1048580 | tf_op jit(solution)/shard_map/jit(dynamic_index_in_dim)/squeeze | solution.py:127
  3.2 0.2 prepare_own.1.mine
  3.3 0.1 collective-permute-done.received
  3.4 0.3 merge.1
  3.7 33.5 %all_to_all.10.received = f32[8,184,128]{2,1,0:T(8,128)S(1)} all-to-all(f32[8,184,128]{2,1,0:T(8,128)S(1)} %merge.1), channel_id=1, replica_groups={{0,32,64,96,128,160,192,224},{16,48,80,112,144,176,208,240},{1,33,65,97..., dimensions={0} | all-to-all | bytes 1507328 | tf_op jit(solution)/shard_map/all_to_all | solution.py:675
  37.2 0.0 copy-done.1
  37.2 0.0 copy-done.2
  37.2 0.0 copy-done.5
  37.2 0.0 copy-start.4
  37.2 1.0 %transform.1 = (f32[33,32,128]{2,1,0:T(8,128)S(1)}, f32[17,8,128]{2,1,0:T(8,128)S(1)}) custom-call(f32[8]{0:T(128)S(1)} %copy-done.5, s32[256,256]{1,0:T(8,128)S(1)} %copy-done.3, f32[2,256,256]{2,1,0:T(8,128)S(1)} %copy-done.1, f32[2,256,256]{2,1,0:T(8,128)S(1)} %copy-done.2, f32[8,184,128]{2,1,0:T(8,128)S(1)} %all_to_all.10.received), custom_call_target="tpu_custom_call" | custom-call | tf_op jit(solution)/shard_map/transform/pallas_call | solution.py:329
  38.2 0.8 %collective-permute-start.1 = (f32[17,8,128]{2,1,0:T(8,128)S(1)}, f32[17,8,128]{2,1,0:T(8,128)S(1)}, u32[]{:S(2)}, u32[]{:S(2)}) collective-permute-start(f32[17,8,128]{2,1,0:T(8,128)S(1)} %get-tuple-element.22), channel_id=1, source_target_pairs={{0,16},{32,224},{224,32},{192,193},{193,192},{225,33},{33,225},{1,... | collective-permute-start | bytes 208904 | tf_op jit(solution)/shard_map/ppermute | solution.py:690
  39.1 0.9 %strips.1 = (f32[33,8,128]{2,1,0:T(8,128)S(1)}, f32[22,8,128]{2,1,0:T(8,128)S(1)}, f32[22,8,128]{2,1,0:T(8,128)S(1)}) custom-call(f32[8]{0:T(128)S(1)} %copy-done.5, s32[256,256]{1,0:T(8,128)S(1)} %copy-done.3, f32[2,256,256]{2,1,0:T(8,128)S(1)} %copy-done.1, f32[2,256,256]{2,1,0:T(8,128)S(1)} %copy-done.2, f32[8,184,128]{2,1,0:T(8,128)S(1)} %all_to_all.10.received, ...), custom_call_target="tpu_custom_call" | custom-call | flops 1048576 | bytes 1048576 | tf_op jit(solution)/shard_map/strips/pallas_call | solution.py:369
  40.1 1.4 %collective-permute-done.1.from_side = f32[17,8,128]{2,1,0:T(8,128)S(1)} collective-permute-done((f32[17,8,128]{2,1,0:T(8,128)S(1)}, f32[17,8,128]{2,1,0:T(8,128)S(1)}, u32[]{:S(2)}, u32[]{:S(2)}) %collective-permute-start.1) | collective-permute-done | bytes 69664 | tf_op jit(solution)/shard_map/ppermute | solution.py:690
  41.5 2.8 %collective-permute-start.2 = (f32[22,8,128]{2,1,0:T(8,128)S(1)}, f32[22,8,128]{2,1,0:T(8,128)S(1)}, u32[]{:S(2)}, u32[]{:S(2)}) collective-permute-start(f32[22,8,128]{2,1,0:T(8,128)S(1)} %pad_maximum_fusion), channel_id=1, source_target_pairs={{0,28},{32,60},{224,252},{192,220},{193,221},{225,253},{33,61},{1,... | collective-permute-start | bytes 270344 | tf_op jit(solution)/shard_map/ppermute | solution.py:701
  44.4 0.3 collective-permute-start.3
  44.6 1.7 %widen.1.middle = f32[16,4,80,128]{3,2,1,0:T(8,128)S(1)} custom-call(f32[16,2]{1,0:T(8,128)S(1)} %copy-done.4, f32[33,32,128]{2,1,0:T(8,128)S(1)} %get-tuple-element.20.planes, f32[33,8,128]{2,1,0:T(8,128)S(1)} %get-tuple-element.21.beside, f32[17,8,128]{2,1,0:T(8,128)S(1)} %collective-permute-done.1.from_side), custom_call_target="tpu_custom_call" | custom-call | flops 2097152 | bytes 2097152 | tf_op jit(solution)/shard_map/widen/pallas_call | solution.py:490
  46.3 0.0 copy-start
  46.3 0.2 collective-permute-done.2.from_cross
  46.6 0.0 collective-permute-done.3.from_core
  46.6 5.2 %solve.1 = (f32[8,160,128]{2,1,0:T(8,128)S(1)}, f32[16,4,80,128]{3,2,1,0:T(8,128)S(1)}) custom-call(f32[16,2]{1,0:T(8,128)S(1)} %copy-done.4, f32[16,4,80,128]{3,2,1,0:T(8,128)S(1)} %widen.1.middle, f32[22,8,128]{2,1,0:T(8,128)S(1)} %collective-permute-done.2.from_cross, ...), custom_call_target="tpu_custom_call", output_to_operand_aliasing={{1}: (1, {})} | custom-call | tf_op jit(solution)/shard_map/solve/pallas_call | solution.py:589
  51.8 26.2 %all_to_all.11.units = f32[8,160,128]{2,1,0:T(8,128)S(1)} all-to-all(f32[8,160,128]{2,1,0:T(8,128)S(1)} %get-tuple-element.26), channel_id=1, replica_groups={{0,32,64,96,128,160,192,224},{16,48,80,112,144,176,208,240},{1,33,65,97..., dimensions={0} | all-to-all | bytes 1310720 | tf_op jit(solution)/shard_map/all_to_all | solution.py:675
  78.0 0.6 collective-permute-start.4
  78.6 0.9 %finish_own.1.refs_0_ = f32[2,2,2,2,64,256]{5,4,3,2,1,0:T(8,128)} custom-call(f32[8,160,128]{2,1,0:T(8,128)S(1)} %all_to_all.11.units, f32[2,2,2,2,64,256]{5,4,3,2,1,0:T(8,128)S(1)} %bitcast.30, f32[2,2,2,64,256]{4,3,2,1,0:T(8,128)S(1)} %bitcast.32, f32[2,2,2,64,256]{4,3,2,1,0:T(8,128)S(1)} %bitcast.34), custom_call_target="tpu_custom_call" | custom-call | flops 1048576 | bytes 1048576 | tf_op jit(solution)/shard_map/finish_own/pallas_call | solution.py:644
  79.6 0.4 collective-permute-done.4.units
  80.0 0.9 %finish_other.1 = f32[2,2,2,2,64,256]{5,4,3,2,1,0:T(8,128)} custom-call(f32[8,96,128]{2,1,0:T(8,128)S(1)} %collective-permute-done.4.units, f32[2,2,2,2,64,256]{5,4,3,2,1,0:T(8,128)S(1)} %bitcast.31, f32[2,2,2,64,256]{4,3,2,1,0:T(8,128)S(1)} %bitcast.33, f32[2,2,2,64,256]{4,3,2,1,0:T(8,128)S(1)} %bitcast.35, ...), custom_call_target="tpu_custom_call", output_to_operand_aliasing={{}: (4, {})} | custom-call | flops 1048576 | bytes 1048576 | tf_op jit(solution)/shard_map/finish_other/pallas_call | solution.py:644
  (13 shorter events, 0.1 us)
Async XLA Ops:
  1.3 35.9 %copy-start.1 = (f32[2,256,256]{2,1,0:T(8,128)S(1)}, f32[2,256,256]{2,1,0:T(8,128)}, u32[]{:S(2)}) copy-start(f32[2,256,256]{2,1,0:T(8,128)} %initial.3) | copy-start | bytes 1572868
  1.3 35.9 %copy-start.2 = (f32[2,256,256]{2,1,0:T(8,128)S(1)}, f32[2,256,256]{2,1,0:T(8,128)}, u32[]{:S(2)}) copy-start(f32[2,256,256]{2,1,0:T(8,128)} %last.3) | copy-start | bytes 1572868
  1.3 35.9 %copy-start.3 = (s32[256,256]{1,0:T(8,128)S(1)}, s32[256,256]{1,0:T(8,128)}, u32[]{:S(2)}) copy-start(s32[256,256]{1,0:T(8,128)} %cell_class.3) | copy-start | bytes 786436
  1.3 35.9 %copy-start.5 = (f32[8]{0:T(128)S(1)}, f32[8]{0:T(128)}, u32[]{:S(2)}) copy-start(f32[8]{0:T(128)} %table.3) | copy-start | bytes 100
  1.3 2.1 %collective-permute-start = (f32[8,96,128]{2,1,0:T(8,128)S(1)}, f32[8,96,128]{2,1,0:T(8,128)S(1)}, u32[]{:S(2)}, u32[]{:S(2)}) collective-permute-start(f32[8,96,128]{2,1,0:T(8,128)S(1)} %prepare_other.1), channel_id=1, source_target_pairs={{0,16},{16,0},{32,48},{48,32},{64,80},{80,64},{96,112},{112,96},{1... | collective-permute-start | bytes 1179656 | tf_op jit(solution)/shard_map/ppermute | solution.py:683
  37.2 7.4 %copy-start.4 = (f32[16,2]{1,0:T(8,128)S(1)}, f32[16,2]{1,0:T(8,128)}, u32[]{:S(2)}) copy-start(f32[16,2]{1,0:T(8,128)} %constant.22.clone.lam) | copy-start | bytes 388
  38.2 3.2 %collective-permute-start.1 = (f32[17,8,128]{2,1,0:T(8,128)S(1)}, f32[17,8,128]{2,1,0:T(8,128)S(1)}, u32[]{:S(2)}, u32[]{:S(2)}) collective-permute-start(f32[17,8,128]{2,1,0:T(8,128)S(1)} %get-tuple-element.22), channel_id=1, source_target_pairs={{0,16},{32,224},{224,32},{192,193},{193,192},{225,33},{33,225},{1,... | collective-permute-start | bytes 208904 | tf_op jit(solution)/shard_map/ppermute | solution.py:690
  41.5 5.0 %collective-permute-start.2 = (f32[22,8,128]{2,1,0:T(8,128)S(1)}, f32[22,8,128]{2,1,0:T(8,128)S(1)}, u32[]{:S(2)}, u32[]{:S(2)}) collective-permute-start(f32[22,8,128]{2,1,0:T(8,128)S(1)} %pad_maximum_fusion), channel_id=1, source_target_pairs={{0,28},{32,60},{224,252},{192,220},{193,221},{225,253},{33,61},{1,... | collective-permute-start | bytes 270344 | tf_op jit(solution)/shard_map/ppermute | solution.py:701
  44.4 2.2 %collective-permute-start.3 = (f32[22,8,128]{2,1,0:T(8,128)S(1)}, f32[22,8,128]{2,1,0:T(8,128)S(1)}, u32[]{:S(2)}, u32[]{:S(2)}) collective-permute-start(f32[22,8,128]{2,1,0:T(8,128)S(1)} %pad_maximum_fusion.1), channel_id=1, source_target_pairs={{0,16},{32,48},{224,240},{192,208},{193,209},{225,241},{33,49},{1,... | collective-permute-start | bytes 270344 | tf_op jit(solution)/shard_map/ppermute | solution.py:702
  46.3 32.3 %copy-start = (f32[2,2,256,256]{3,2,1,0:T(8,128)S(1)}, f32[2,2,256,256]{3,2,1,0:T(8,128)}, u32[]{:S(2)}) copy-start(f32[2,2,256,256]{3,2,1,0:T(8,128)} %param.6) | copy-start | bytes 3145732
  78.0 1.9 %collective-permute-start.4 = (f32[8,96,128]{2,1,0:T(8,128)S(1)}, f32[8,96,128]{2,1,0:T(8,128)S(1)}, u32[]{:S(2)}, u32[]{:S(2)}) collective-permute-start(f32[8,96,128]{2,1,0:T(8,128)S(1)} %slice_select_fusion), channel_id=1, source_target_pairs={{0,16},{16,0},{32,48},{48,32},{64,80},{80,64},{96,112},{112,96},{1... | collective-permute-start | bytes 1179656 | tf_op jit(solution)/shard_map/ppermute | solution.py:706

commit v8 on v7

--- a/solution.py
+++ b/solution.py
@@ -336,8 +336,22 @@
     )(table, cell_class, initial, last, received)
 
 
+def bases(inner):
+    return 120 - 56 * inner, 64 + 56 * inner
+
+
+def placed(value, edge, base):
+    lane = lanes(8)
+    return jnp.where((lane >= base) & (lane < base + 8), edge, value)
+
+
+def merged(centre, side, other, bases):
+    value = jnp.where(lanes(8) < 64, centre, 0.0)
+    return placed(placed(value, side, bases[0]), other, bases[1])
+
+
 def strips_kernel(
-    table, cell_class, initial, last, received, planes, beside_out, core_out, cross_out
+    table, cell_class, initial, last, received, planes, wide_out, core_out, cross_out
 ):
     core, _, _, inner = place()[3:7]
     low = lanes(8) < 64
@@ -350,8 +364,12 @@
         first = one + received[(t + 7) % 8, 176:184, :]
         steps.extend([first, turn(one, -32), two, turn(two, -32)])
     beside = forward(with_start(steps, start_u, start_w)) + [courant]
+    base = bases(inner)[1]
     for p in range(33):
-        beside_out[p] = beside[p]
+        for r in range(8):
+            shift, start = 64 * (r // 4), 8 * (r % 4)
+            value = jnp.where(lanes(8) < 64, turn(planes[p, start : start + 8, :], shift), 0.0)
+            wide_out[p, 8 * r : 8 * r + 8, :] = placed(value, turn(beside[p], base - shift - start), base)
     top, bottom = [], []
     for j in range(17):
         one, two = 2 * j, min(2 * j + 1, 32)
@@ -365,7 +383,7 @@
 
 
 def strips(table, cell_class, initial, last, received, planes):
-    shapes = ((33, 8, 128), (22, 8, 128), (22, 8, 128))
+    shapes = ((33, 64, 128), (22, 8, 128), (22, 8, 128))
     return pl.pallas_call(
         strips_kernel,
         in_specs=[pl.BlockSpec(memory_space=pltpu.SMEM)] + [pl.BlockSpec(memory_space=pltpu.VMEM)] * 5,
@@ -401,18 +419,6 @@
     above = [first] + field[:9]
     below = field[1:] + [last]
     return [(up + down) + side for up, side, down in zip(above, sides, below)]
-
-
-def bases(inner):
-    return 120 - 56 * inner, 64 + 56 * inner
-
-
-def merged(centre, side, other, bases):
-    lane = lanes(8)
-    value = jnp.where(lane < 64, centre, 0.0)
-    for base, edge in zip(bases, (side, other)):
-        value = jnp.where((lane >= base) & (lane < base + 8), edge, value)
-    return value
 
 
 def in_grid(first_row, count, col0):
@@ -453,25 +459,17 @@
     lax.fori_loop(1, 4, group, 0)
 
 
-def widen_kernel(lam, planes, beside, from_side, out):
+def widen_kernel(lam, wide, from_side, out):
     inner, _, col0 = place()[6:]
-    both = bases(inner)
+    base = bases(inner)[0]
 
     def extended(p, group, offset):
-        edge = beside[p]
         parts = []
         for r in range(8):
-            part = slice(8 * (r % 4), 8 * (r % 4) + 8)
-            shift = 0 if r < 4 else 64
+            shift = 64 * (r // 4)
             tile, start = (16, 8 * (r % 4)) if group is None else (4 * group + r % 4, offset)
-            parts.append(
-                merged(
-                    turn(planes[p, part, :], shift),
-                    turn(from_side[tile], both[0] - shift - start),
-                    turn(edge, both[1] - shift - 8 * (r % 4)),
-                    both,
-                )
-            )
+            edge = turn(from_side[tile], base - shift - start)
+            parts.append(placed(wide[p, 8 * r : 8 * r + 8, :], edge, base))
         return jnp.concatenate(parts, axis=0)
 
     mask = in_grid(0, 64, col0)
@@ -486,16 +484,16 @@
     over_frequencies(work)
 
 
-def widen(lam, planes, beside, from_side):
+def widen(lam, wide, from_side):
     return pl.pallas_call(
         widen_kernel,
-        in_specs=[pl.BlockSpec(memory_space=pltpu.SMEM)] + [pl.BlockSpec(memory_space=pltpu.VMEM)] * 3,
+        in_specs=[pl.BlockSpec(memory_space=pltpu.SMEM)] + [pl.BlockSpec(memory_space=pltpu.VMEM)] * 2,
         out_specs=pl.BlockSpec(memory_space=pltpu.VMEM),
         out_shape=jax.ShapeDtypeStruct((16, 4, 80, 128), jnp.float32),
         compiler_params=params(),
         cost_estimate=cost(2**21),
         name="widen",
-    )(lam, planes, beside, from_side)
+    )(lam, wide, from_side)
 
 
 def solve_kernel(lam, middle, from_cross, from_core, out, full, solved, wide):
@@ -688,7 +686,7 @@
     fields = (courant_table, cell_class, initial, previous_last, received)
     planes, side = transform(*fields)
     from_side = lax.ppermute(side, AXES, TO_SIDE)
-    beside, to_core, to_cross = strips(*fields, planes)
+    wide, to_core, to_cross = strips(*fields, planes)
 
     rows = from_side[:16].reshape(4, 4, 8, 128)
     low = lax.broadcasted_iota(jnp.int32, (5, 8, 128), 2) < 64
@@ -700,7 +698,7 @@
 
     from_cross = lax.ppermute(strip(to_cross, is_lower), AXES, TO_CROSS)
     from_core = lax.ppermute(strip(to_core, is_upper), AXES, TO_CORE)
-    middle = widen(lam, planes, beside, from_side)
+    middle = widen(lam, wide, from_side)
     returned = chips_exchange(solve(lam, middle, from_cross, from_core))
     wanted = jnp.where(is_upper, returned[:, 64:160], returned[:, 0:96])
     other = lax.ppermute(wanted, "tm", CORES)

time: 81.1 us -> 81.1 us (level)
  no operation moved by 1% of the time
where the time goes in v8:
time: 81.1 us; the launch traced here: 80.9 us
  blocking collectives  59.7 us (74%)
  Pallas kernels  11.4 us (14%)
  starting transfers between devices  5.24 us (6%)
  local copies, waits for them, and re-layouts  2.21 us (3%)
  waiting for transfers between devices  2.11 us (3%)
    all_to_all x2, blocking collectives, chips_exchange(): lax.all_to_all(pieces, 'tm', 0, 0, axis_index_groups=CHIPS, tiled=True)  59.7 us
    pallas_call x1, Pallas kernels, solve(): pl.pallas_call(solve_kernel, in_specs=[pl.BlockSpec(memory_space=pltpu.SM...  5.22 us
    ppermute x1, starting transfers between devices, per_device(): from_cross = lax.ppermute(strip(to_cross, is_lower), AXES, TO_CROSS)  2.8 us
    squeeze x2, local copies, waits for them, and re-layouts, prepare(): lax.dynamic_index_in_dim(forcing.reshape(2, 2, 2, 2, 64, 256), core, 3, k...  2.15 us
    pallas_call x2, Pallas kernels, finish(): pl.pallas_call(functools.partial(finish_kernel, int(other)), in_specs=[pl...  1.85 us
  transfers between devices with their start and end apart: 5, of which 4 were waited for; matrix products, arithmetic and copies ran while one was open for 1% of the time, Pallas kernels for 5%

profile of v8, /device:TPU:33, one launch (start us, length us, event | category | flops | bytes accessed | tf_op | source)
XLA Modules:
  0.0 80.9 jit_solution(9172876113783292047)
XLA Ops:
  0.0 1.1 %dynamic-slice_bitcast_fusion.1.forcing = f32[2,2,2,64,256]{4,3,2,1,0:T(8,128)S(1)} fusion(f32[2,2,2,2,64,256]{5,4,3,2,1,0:T(8,128)} %bitcast.28, s32[]{:T(128)S(6)} %select_n.42), kind=kLoop, calls=%fused_computation.1 | loop fusion | bytes 1048580 | tf_op jit(solution)/shard_map/jit(dynamic_index_in_dim)/squeeze | solution.py:127
  1.1 0.2 prepare_other.1
  1.3 0.0 copy-start.1
  1.3 0.0 copy-start.2
  1.3 0.0 copy-start.3
  1.3 0.0 copy-start.5
  1.3 0.8 collective-permute-start
  2.1 1.1 %dynamic-slice_bitcast_fusion.forcing = f32[2,2,2,64,256]{4,3,2,1,0:T(8,128)S(1)} fusion(f32[2,2,2,2,64,256]{5,4,3,2,1,0:T(8,128)} %bitcast.29, s32[]{:T(128)S(6)} %select_n.43), kind=kLoop, calls=%fused_computation | loop fusion | bytes 1048580 | tf_op jit(solution)/shard_map/jit(dynamic_index_in_dim)/squeeze | solution.py:127
  3.2 0.2 prepare_own.1.mine
  3.3 0.1 collective-permute-done.received
  3.4 0.3 merge.1
  3.7 33.5 %all_to_all.10.received = f32[8,184,128]{2,1,0:T(8,128)S(1)} all-to-all(f32[8,184,128]{2,1,0:T(8,128)S(1)} %merge.1), channel_id=1, replica_groups={{0,32,64,96,128,160,192,224},{16,48,80,112,144,176,208,240},{1,33,65,97..., dimensions={0} | all-to-all | bytes 1507328 | tf_op jit(solution)/shard_map/all_to_all | solution.py:673
  37.2 0.0 copy-done.1
  37.2 0.0 copy-done.3
  37.2 0.0 copy-start.4
  37.2 1.0 %transform.1 = (f32[33,32,128]{2,1,0:T(8,128)S(1)}, f32[17,8,128]{2,1,0:T(8,128)S(1)}) custom-call(f32[8]{0:T(128)S(1)} %copy-done.5, s32[256,256]{1,0:T(8,128)S(1)} %copy-done.3, f32[2,256,256]{2,1,0:T(8,128)S(1)} %copy-done.1, f32[2,256,256]{2,1,0:T(8,128)S(1)} %copy-done.2, f32[8,184,128]{2,1,0:T(8,128)S(1)} %all_to_all.10.received), custom_call_target="tpu_custom_call" | custom-call | tf_op jit(solution)/shard_map/transform/pallas_call | solution.py:329
  38.2 0.8 %collective-permute-start.1 = (f32[17,8,128]{2,1,0:T(8,128)S(1)}, f32[17,8,128]{2,1,0:T(8,128)S(1)}, u32[]{:S(2)}, u32[]{:S(2)}) collective-permute-start(f32[17,8,128]{2,1,0:T(8,128)S(1)} %get-tuple-element.22), channel_id=1, source_target_pairs={{0,16},{32,224},{224,32},{192,193},{193,192},{225,33},{33,225},{1,... | collective-permute-start | bytes 208904 | tf_op jit(solution)/shard_map/ppermute | solution.py:688
  39.1 1.4 %strips.1 = (f32[33,64,128]{2,1,0:T(8,128)S(1)}, f32[22,8,128]{2,1,0:T(8,128)S(1)}, f32[22,8,128]{2,1,0:T(8,128)S(1)}) custom-call(f32[8]{0:T(128)S(1)} %copy-done.5, s32[256,256]{1,0:T(8,128)S(1)} %copy-done.3, f32[2,256,256]{2,1,0:T(8,128)S(1)} %copy-done.1, f32[2,256,256]{2,1,0:T(8,128)S(1)} %copy-done.2, f32[8,184,128]{2,1,0:T(8,128)S(1)} %all_to_all.10.received, ...), custom_call_target="tpu_custom_call" | custom-call | flops 1048576 | bytes 1048576 | tf_op jit(solution)/shard_map/strips/pallas_call | solution.py:387
  40.5 0.9 %collective-permute-done.1.from_side = f32[17,8,128]{2,1,0:T(8,128)S(1)} collective-permute-done((f32[17,8,128]{2,1,0:T(8,128)S(1)}, f32[17,8,128]{2,1,0:T(8,128)S(1)}, u32[]{:S(2)}, u32[]{:S(2)}) %collective-permute-start.1) | collective-permute-done | bytes 69664 | tf_op jit(solution)/shard_map/ppermute | solution.py:688
  41.5 2.8 %collective-permute-start.2 = (f32[22,8,128]{2,1,0:T(8,128)S(1)}, f32[22,8,128]{2,1,0:T(8,128)S(1)}, u32[]{:S(2)}, u32[]{:S(2)}) collective-permute-start(f32[22,8,128]{2,1,0:T(8,128)S(1)} %pad_maximum_fusion), channel_id=1, source_target_pairs={{0,28},{32,60},{224,252},{192,220},{193,221},{225,253},{33,61},{1,... | collective-permute-start | bytes 270344 | tf_op jit(solution)/shard_map/ppermute | solution.py:699
  44.4 0.3 collective-permute-start.3
  44.6 1.3 %widen.1.middle = f32[16,4,80,128]{3,2,1,0:T(8,128)S(1)} custom-call(f32[16,2]{1,0:T(8,128)S(1)} %copy-done.4, f32[33,64,128]{2,1,0:T(8,128)S(1)} %get-tuple-element.21.wide, f32[17,8,128]{2,1,0:T(8,128)S(1)} %collective-permute-done.1.from_side), custom_call_target="tpu_custom_call" | custom-call | flops 2097152 | bytes 2097152 | tf_op jit(solution)/shard_map/widen/pallas_call | solution.py:488
  45.9 0.0 copy-start
  45.9 0.7 collective-permute-done.2.from_cross
  46.6 0.0 collective-permute-done.3.from_core
  46.6 5.2 %solve.1 = (f32[8,160,128]{2,1,0:T(8,128)S(1)}, f32[16,4,80,128]{3,2,1,0:T(8,128)S(1)}) custom-call(f32[16,2]{1,0:T(8,128)S(1)} %copy-done.4, f32[16,4,80,128]{3,2,1,0:T(8,128)S(1)} %widen.1.middle, f32[22,8,128]{2,1,0:T(8,128)S(1)} %collective-permute-done.2.from_cross, ...), custom_call_target="tpu_custom_call", output_to_operand_aliasing={{1}: (1, {})} | custom-call | tf_op jit(solution)/shard_map/solve/pallas_call | solution.py:587
  51.8 26.2 %all_to_all.11.units = f32[8,160,128]{2,1,0:T(8,128)S(1)} all-to-all(f32[8,160,128]{2,1,0:T(8,128)S(1)} %get-tuple-element.26), channel_id=1, replica_groups={{0,32,64,96,128,160,192,224},{16,48,80,112,144,176,208,240},{1,33,65,97..., dimensions={0} | all-to-all | bytes 1310720 | tf_op jit(solution)/shard_map/all_to_all | solution.py:673
  78.0 0.6 collective-permute-start.4
  78.6 0.0 copy-done
  78.6 0.9 %finish_own.1.refs_0_ = f32[2,2,2,2,64,256]{5,4,3,2,1,0:T(8,128)} custom-call(f32[8,160,128]{2,1,0:T(8,128)S(1)} %all_to_all.11.units, f32[2,2,2,2,64,256]{5,4,3,2,1,0:T(8,128)S(1)} %bitcast.30, f32[2,2,2,64,256]{4,3,2,1,0:T(8,128)S(1)} %bitcast.32, f32[2,2,2,64,256]{4,3,2,1,0:T(8,128)S(1)} %bitcast.34), custom_call_target="tpu_custom_call" | custom-call | flops 1048576 | bytes 1048576 | tf_op jit(solution)/shard_map/finish_own/pallas_call | solution.py:642
  79.6 0.4 collective-permute-done.4.units
  80.0 0.9 %finish_other.1 = f32[2,2,2,2,64,256]{5,4,3,2,1,0:T(8,128)} custom-call(f32[8,96,128]{2,1,0:T(8,128)S(1)} %collective-permute-done.4.units, f32[2,2,2,2,64,256]{5,4,3,2,1,0:T(8,128)S(1)} %bitcast.31, f32[2,2,2,64,256]{4,3,2,1,0:T(8,128)S(1)} %bitcast.33, f32[2,2,2,64,256]{4,3,2,1,0:T(8,128)S(1)} %bitcast.35, ...), custom_call_target="tpu_custom_call", output_to_operand_aliasing={{}: (4, {})} | custom-call | flops 1048576 | bytes 1048576 | tf_op jit(solution)/shard_map/finish_other/pallas_call | solution.py:642
  (13 shorter events, 0.1 us)
Async XLA Ops:
  1.3 35.9 %copy-start.1 = (f32[2,256,256]{2,1,0:T(8,128)S(1)}, f32[2,256,256]{2,1,0:T(8,128)}, u32[]{:S(2)}) copy-start(f32[2,256,256]{2,1,0:T(8,128)} %initial.3) | copy-start | bytes 1572868
  1.3 35.9 %copy-start.2 = (f32[2,256,256]{2,1,0:T(8,128)S(1)}, f32[2,256,256]{2,1,0:T(8,128)}, u32[]{:S(2)}) copy-start(f32[2,256,256]{2,1,0:T(8,128)} %last.3) | copy-start | bytes 1572868
  1.3 35.9 %copy-start.3 = (s32[256,256]{1,0:T(8,128)S(1)}, s32[256,256]{1,0:T(8,128)}, u32[]{:S(2)}) copy-start(s32[256,256]{1,0:T(8,128)} %cell_class.3) | copy-start | bytes 786436
  1.3 35.9 %copy-start.5 = (f32[8]{0:T(128)S(1)}, f32[8]{0:T(128)}, u32[]{:S(2)}) copy-start(f32[8]{0:T(128)} %table.3) | copy-start | bytes 100
  1.3 2.1 %collective-permute-start = (f32[8,96,128]{2,1,0:T(8,128)S(1)}, f32[8,96,128]{2,1,0:T(8,128)S(1)}, u32[]{:S(2)}, u32[]{:S(2)}) collective-permute-start(f32[8,96,128]{2,1,0:T(8,128)S(1)} %prepare_other.1), channel_id=1, source_target_pairs={{0,16},{16,0},{32,48},{48,32},{64,80},{80,64},{96,112},{112,96},{1... | collective-permute-start | bytes 1179656 | tf_op jit(solution)/shard_map/ppermute | solution.py:681
  37.2 7.4 %copy-start.4 = (f32[16,2]{1,0:T(8,128)S(1)}, f32[16,2]{1,0:T(8,128)}, u32[]{:S(2)}) copy-start(f32[16,2]{1,0:T(8,128)} %constant.22.clone.lam) | copy-start | bytes 388
  38.2 3.2 %collective-permute-start.1 = (f32[17,8,128]{2,1,0:T(8,128)S(1)}, f32[17,8,128]{2,1,0:T(8,128)S(1)}, u32[]{:S(2)}, u32[]{:S(2)}) collective-permute-start(f32[17,8,128]{2,1,0:T(8,128)S(1)} %get-tuple-element.22), channel_id=1, source_target_pairs={{0,16},{32,224},{224,32},{192,193},{193,192},{225,33},{33,225},{1,... | collective-permute-start | bytes 208904 | tf_op jit(solution)/shard_map/ppermute | solution.py:688
  41.5 5.0 %collective-permute-start.2 = (f32[22,8,128]{2,1,0:T(8,128)S(1)}, f32[22,8,128]{2,1,0:T(8,128)S(1)}, u32[]{:S(2)}, u32[]{:S(2)}) collective-permute-start(f32[22,8,128]{2,1,0:T(8,128)S(1)} %pad_maximum_fusion), channel_id=1, source_target_pairs={{0,28},{32,60},{224,252},{192,220},{193,221},{225,253},{33,61},{1,... | collective-permute-start | bytes 270344 | tf_op jit(solution)/shard_map/ppermute | solution.py:699
  44.4 2.2 %collective-permute-start.3 = (f32[22,8,128]{2,1,0:T(8,128)S(1)}, f32[22,8,128]{2,1,0:T(8,128)S(1)}, u32[]{:S(2)}, u32[]{:S(2)}) collective-permute-start(f32[22,8,128]{2,1,0:T(8,128)S(1)} %pad_maximum_fusion.1), channel_id=1, source_target_pairs={{0,16},{32,48},{224,240},{192,208},{193,209},{225,241},{33,49},{1,... | collective-permute-start | bytes 270344 | tf_op jit(solution)/shard_map/ppermute | solution.py:700
  45.9 32.7 %copy-start = (f32[2,2,256,256]{3,2,1,0:T(8,128)S(1)}, f32[2,2,256,256]{3,2,1,0:T(8,128)}, u32[]{:S(2)}) copy-start(f32[2,2,256,256]{3,2,1,0:T(8,128)} %param.6) | copy-start | bytes 3145732
  78.0 1.9 %collective-permute-start.4 = (f32[8,96,128]{2,1,0:T(8,128)S(1)}, f32[8,96,128]{2,1,0:T(8,128)S(1)}, u32[]{:S(2)}, u32[]{:S(2)}) collective-permute-start(f32[8,96,128]{2,1,0:T(8,128)S(1)} %slice_select_fusion), channel_id=1, source_target_pairs={{0,16},{16,0},{32,48},{48,32},{64,80},{80,64},{96,112},{112,96},{1... | collective-permute-start | bytes 1179656 | tf_op jit(solution)/shard_map/ppermute | solution.py:704

commit v9 on v8

--- a/solution.py
+++ b/solution.py
@@ -12,6 +12,7 @@
 STEPS = 32
 SWEEPS = 8
 BATCH = 8
+ROOM = 96
 ALPHA = 0.1
 DECAY = math.log(ALPHA) / STEPS
 FACTOR = math.exp(DECAY)
@@ -489,7 +490,7 @@
         widen_kernel,
         in_specs=[pl.BlockSpec(memory_space=pltpu.SMEM)] + [pl.BlockSpec(memory_space=pltpu.VMEM)] * 2,
         out_specs=pl.BlockSpec(memory_space=pltpu.VMEM),
-        out_shape=jax.ShapeDtypeStruct((16, 4, 80, 128), jnp.float32),
+        out_shape=jax.ShapeDtypeStruct((16, 4, ROOM, 128), jnp.float32),
         compiler_params=params(),
         cost_estimate=cost(2**21),
         name="widen",
@@ -590,12 +591,12 @@
         out_specs=[pl.BlockSpec(memory_space=pltpu.VMEM)] * 2,
         out_shape=[
             jax.ShapeDtypeStruct((8, 160, 128), jnp.float32),
-            jax.ShapeDtypeStruct((16, 4, 80, 128), jnp.float32),
+            jax.ShapeDtypeStruct((16, 4, ROOM, 128), jnp.float32),
         ],
         input_output_aliases={1: 1},
         scratch_shapes=[
             pltpu.VMEM((32, 32, 128), jnp.float32),
-            pltpu.VMEM((2 * BATCH, 80, 128), jnp.float32),
+            pltpu.VMEM((2 * BATCH, ROOM, 128), jnp.float32),
         ],
         compiler_params=params(),
         name="solve",

time: 81.1 us -> 81.2 us (level)
  no operation moved by 1% of the time
where the time goes in v9:
time: 81.2 us; the launch traced here: 81 us
  blocking collectives  59.7 us (74%)
  Pallas kernels  11.5 us (14%)
  starting transfers between devices  5.24 us (6%)
  local copies, waits for them, and re-layouts  2.21 us (3%)
  waiting for transfers between devices  2.12 us (3%)
    all_to_all x2, blocking collectives, chips_exchange(): lax.all_to_all(pieces, 'tm', 0, 0, axis_index_groups=CHIPS, tiled=True)  59.7 us
    pallas_call x1, Pallas kernels, solve(): pl.pallas_call(solve_kernel, in_specs=[pl.BlockSpec(memory_space=pltpu.SM...  5.29 us
    ppermute x1, starting transfers between devices, per_device(): from_cross = lax.ppermute(strip(to_cross, is_lower), AXES, TO_CROSS)  2.8 us
    squeeze x2, local copies, waits for them, and re-layouts, prepare(): lax.dynamic_index_in_dim(forcing.reshape(2, 2, 2, 2, 64, 256), core, 3, k...  2.15 us
    pallas_call x2, Pallas kernels, finish(): pl.pallas_call(functools.partial(finish_kernel, int(other)), in_specs=[pl...  1.85 us
  transfers between devices with their start and end apart: 5, of which 4 were waited for; matrix products, arithmetic and copies ran while one was open for 1% of the time, Pallas kernels for 5%

profile of v9, /device:TPU:33, one launch (start us, length us, event | category | flops | bytes accessed | tf_op | source)
XLA Modules:
  0.0 81.0 jit_solution(4700288134376263899)
XLA Ops:
  0.0 1.1 %dynamic-slice_bitcast_fusion.1.forcing = f32[2,2,2,64,256]{4,3,2,1,0:T(8,128)S(1)} fusion(f32[2,2,2,2,64,256]{5,4,3,2,1,0:T(8,128)} %bitcast.28, s32[]{:T(128)S(6)} %select_n.42), kind=kLoop, calls=%fused_computation.1 | loop fusion | bytes 1048580 | tf_op jit(solution)/shard_map/jit(dynamic_index_in_dim)/squeeze | solution.py:128
  1.1 0.0 copy-start.1
  1.1 0.0 copy-start.2
  1.1 0.0 copy-start.3
  1.1 0.0 copy-start.5
  1.1 0.2 prepare_other.1
  1.3 0.8 collective-permute-start
  2.1 1.1 %dynamic-slice_bitcast_fusion.forcing = f32[2,2,2,64,256]{4,3,2,1,0:T(8,128)S(1)} fusion(f32[2,2,2,2,64,256]{5,4,3,2,1,0:T(8,128)} %bitcast.29, s32[]{:T(128)S(6)} %select_n.43), kind=kLoop, calls=%fused_computation | loop fusion | bytes 1048580 | tf_op jit(solution)/shard_map/jit(dynamic_index_in_dim)/squeeze | solution.py:128
  3.2 0.2 prepare_own.1.mine
  3.3 0.1 collective-permute-done.received
  3.4 0.3 merge.1
  3.7 33.5 %all_to_all.10.received = f32[8,184,128]{2,1,0:T(8,128)S(1)} all-to-all(f32[8,184,128]{2,1,0:T(8,128)S(1)} %merge.1), channel_id=1, replica_groups={{0,32,64,96,128,160,192,224},{16,48,80,112,144,176,208,240},{1,33,65,97..., dimensions={0} | all-to-all | bytes 1507328 | tf_op jit(solution)/shard_map/all_to_all | solution.py:674
  37.2 0.0 copy-done.1
  37.2 0.0 copy-done.2
  37.2 0.0 copy-done.3
  37.2 0.0 copy-start.4
  37.2 1.0 %transform.1 = (f32[33,32,128]{2,1,0:T(8,128)S(1)}, f32[17,8,128]{2,1,0:T(8,128)S(1)}) custom-call(f32[8]{0:T(128)S(1)} %copy-done.5, s32[256,256]{1,0:T(8,128)S(1)} %copy-done.3, f32[2,256,256]{2,1,0:T(8,128)S(1)} %copy-done.1, f32[2,256,256]{2,1,0:T(8,128)S(1)} %copy-done.2, f32[8,184,128]{2,1,0:T(8,128)S(1)} %all_to_all.10.received), custom_call_target="tpu_custom_call" | custom-call | tf_op jit(solution)/shard_map/transform/pallas_call | solution.py:330
  38.2 0.8 %collective-permute-start.1 = (f32[17,8,128]{2,1,0:T(8,128)S(1)}, f32[17,8,128]{2,1,0:T(8,128)S(1)}, u32[]{:S(2)}, u32[]{:S(2)}) collective-permute-start(f32[17,8,128]{2,1,0:T(8,128)S(1)} %get-tuple-element.22), channel_id=1, source_target_pairs={{0,16},{32,224},{224,32},{192,193},{193,192},{225,33},{33,225},{1,... | collective-permute-start | bytes 208904 | tf_op jit(solution)/shard_map/ppermute | solution.py:689
  39.1 1.4 %strips.1 = (f32[33,64,128]{2,1,0:T(8,128)S(1)}, f32[22,8,128]{2,1,0:T(8,128)S(1)}, f32[22,8,128]{2,1,0:T(8,128)S(1)}) custom-call(f32[8]{0:T(128)S(1)} %copy-done.5, s32[256,256]{1,0:T(8,128)S(1)} %copy-done.3, f32[2,256,256]{2,1,0:T(8,128)S(1)} %copy-done.1, f32[2,256,256]{2,1,0:T(8,128)S(1)} %copy-done.2, f32[8,184,128]{2,1,0:T(8,128)S(1)} %all_to_all.10.received, ...), custom_call_target="tpu_custom_call" | custom-call | flops 1048576 | bytes 1048576 | tf_op jit(solution)/shard_map/strips/pallas_call | solution.py:388
  40.5 0.9 %collective-permute-done.1.from_side = f32[17,8,128]{2,1,0:T(8,128)S(1)} collective-permute-done((f32[17,8,128]{2,1,0:T(8,128)S(1)}, f32[17,8,128]{2,1,0:T(8,128)S(1)}, u32[]{:S(2)}, u32[]{:S(2)}) %collective-permute-start.1) | collective-permute-done | bytes 69664 | tf_op jit(solution)/shard_map/ppermute | solution.py:689
  41.5 2.8 %collective-permute-start.2 = (f32[22,8,128]{2,1,0:T(8,128)S(1)}, f32[22,8,128]{2,1,0:T(8,128)S(1)}, u32[]{:S(2)}, u32[]{:S(2)}) collective-permute-start(f32[22,8,128]{2,1,0:T(8,128)S(1)} %pad_maximum_fusion), channel_id=1, source_target_pairs={{0,28},{32,60},{224,252},{192,220},{193,221},{225,253},{33,61},{1,... | collective-permute-start | bytes 270344 | tf_op jit(solution)/shard_map/ppermute | solution.py:700
  44.4 0.3 collective-permute-start.3
  44.6 1.3 %widen.1.middle = f32[16,4,96,128]{3,2,1,0:T(8,128)S(1)} custom-call(f32[16,2]{1,0:T(8,128)S(1)} %copy-done.4, f32[33,64,128]{2,1,0:T(8,128)S(1)} %get-tuple-element.21.wide, f32[17,8,128]{2,1,0:T(8,128)S(1)} %collective-permute-done.1.from_side), custom_call_target="tpu_custom_call" | custom-call | flops 2097152 | bytes 2097152 | tf_op jit(solution)/shard_map/widen/pallas_call | solution.py:489
  45.9 0.0 copy-start
  45.9 0.7 collective-permute-done.2.from_cross
  46.6 0.0 collective-permute-done.3.from_core
  46.6 5.3 %solve.1 = (f32[8,160,128]{2,1,0:T(8,128)S(1)}, f32[16,4,96,128]{3,2,1,0:T(8,128)S(1)}) custom-call(f32[16,2]{1,0:T(8,128)S(1)} %copy-done.4, f32[16,4,96,128]{3,2,1,0:T(8,128)S(1)} %widen.1.middle, f32[22,8,128]{2,1,0:T(8,128)S(1)} %collective-permute-done.2.from_cross, ...), custom_call_target="tpu_custom_call", output_to_operand_aliasing={{1}: (1, {})} | custom-call | tf_op jit(solution)/shard_map/solve/pallas_call | solution.py:588
  51.9 26.2 %all_to_all.11.units = f32[8,160,128]{2,1,0:T(8,128)S(1)} all-to-all(f32[8,160,128]{2,1,0:T(8,128)S(1)} %get-tuple-element.26), channel_id=1, replica_groups={{0,32,64,96,128,160,192,224},{16,48,80,112,144,176,208,240},{1,33,65,97..., dimensions={0} | all-to-all | bytes 1310720 | tf_op jit(solution)/shard_map/all_to_all | solution.py:674
  78.1 0.6 collective-permute-start.4
  78.7 0.9 %finish_own.1.refs_0_ = f32[2,2,2,2,64,256]{5,4,3,2,1,0:T(8,128)} custom-call(f32[8,160,128]{2,1,0:T(8,128)S(1)} %all_to_all.11.units, f32[2,2,2,2,64,256]{5,4,3,2,1,0:T(8,128)S(1)} %bitcast.30, f32[2,2,2,64,256]{4,3,2,1,0:T(8,128)S(1)} %bitcast.32, f32[2,2,2,64,256]{4,3,2,1,0:T(8,128)S(1)} %bitcast.34), custom_call_target="tpu_custom_call" | custom-call | flops 1048576 | bytes 1048576 | tf_op jit(solution)/shard_map/finish_own/pallas_call | solution.py:643
  79.6 0.4 collective-permute-done.4.units
  80.0 0.9 %finish_other.1 = f32[2,2,2,2,64,256]{5,4,3,2,1,0:T(8,128)} custom-call(f32[8,96,128]{2,1,0:T(8,128)S(1)} %collective-permute-done.4.units, f32[2,2,2,2,64,256]{5,4,3,2,1,0:T(8,128)S(1)} %bitcast.31, f32[2,2,2,64,256]{4,3,2,1,0:T(8,128)S(1)} %bitcast.33, f32[2,2,2,64,256]{4,3,2,1,0:T(8,128)S(1)} %bitcast.35, ...), custom_call_target="tpu_custom_call", output_to_operand_aliasing={{}: (4, {})} | custom-call | flops 1048576 | bytes 1048576 | tf_op jit(solution)/shard_map/finish_other/pallas_call | solution.py:643
  (13 shorter events, 0.1 us)
Async XLA Ops:
  1.1 36.1 %copy-start.1 = (f32[2,256,256]{2,1,0:T(8,128)S(1)}, f32[2,256,256]{2,1,0:T(8,128)}, u32[]{:S(2)}) copy-start(f32[2,256,256]{2,1,0:T(8,128)} %initial.3) | copy-start | bytes 1572868
  1.1 36.1 %copy-start.2 = (f32[2,256,256]{2,1,0:T(8,128)S(1)}, f32[2,256,256]{2,1,0:T(8,128)}, u32[]{:S(2)}) copy-start(f32[2,256,256]{2,1,0:T(8,128)} %last.3) | copy-start | bytes 1572868
  1.1 36.1 %copy-start.3 = (s32[256,256]{1,0:T(8,128)S(1)}, s32[256,256]{1,0:T(8,128)}, u32[]{:S(2)}) copy-start(s32[256,256]{1,0:T(8,128)} %cell_class.3) | copy-start | bytes 786436
  1.1 36.1 %copy-start.5 = (f32[8]{0:T(128)S(1)}, f32[8]{0:T(128)}, u32[]{:S(2)}) copy-start(f32[8]{0:T(128)} %table.3) | copy-start | bytes 100
  1.3 2.1 %collective-permute-start = (f32[8,96,128]{2,1,0:T(8,128)S(1)}, f32[8,96,128]{2,1,0:T(8,128)S(1)}, u32[]{:S(2)}, u32[]{:S(2)}) collective-permute-start(f32[8,96,128]{2,1,0:T(8,128)S(1)} %prepare_other.1), channel_id=1, source_target_pairs={{0,16},{16,0},{32,48},{48,32},{64,80},{80,64},{96,112},{112,96},{1... | collective-permute-start | bytes 1179656 | tf_op jit(solution)/shard_map/ppermute | solution.py:682
  37.2 7.4 %copy-start.4 = (f32[16,2]{1,0:T(8,128)S(1)}, f32[16,2]{1,0:T(8,128)}, u32[]{:S(2)}) copy-start(f32[16,2]{1,0:T(8,128)} %constant.22.clone.lam) | copy-start | bytes 388
  38.2 3.2 %collective-permute-start.1 = (f32[17,8,128]{2,1,0:T(8,128)S(1)}, f32[17,8,128]{2,1,0:T(8,128)S(1)}, u32[]{:S(2)}, u32[]{:S(2)}) collective-permute-start(f32[17,8,128]{2,1,0:T(8,128)S(1)} %get-tuple-element.22), channel_id=1, source_target_pairs={{0,16},{32,224},{224,32},{192,193},{193,192},{225,33},{33,225},{1,... | collective-permute-start | bytes 208904 | tf_op jit(solution)/shard_map/ppermute | solution.py:689
  41.5 5.0 %collective-permute-start.2 = (f32[22,8,128]{2,1,0:T(8,128)S(1)}, f32[22,8,128]{2,1,0:T(8,128)S(1)}, u32[]{:S(2)}, u32[]{:S(2)}) collective-permute-start(f32[22,8,128]{2,1,0:T(8,128)S(1)} %pad_maximum_fusion), channel_id=1, source_target_pairs={{0,28},{32,60},{224,252},{192,220},{193,221},{225,253},{33,61},{1,... | collective-permute-start | bytes 270344 | tf_op jit(solution)/shard_map/ppermute | solution.py:700
  44.4 2.2 %collective-permute-start.3 = (f32[22,8,128]{2,1,0:T(8,128)S(1)}, f32[22,8,128]{2,1,0:T(8,128)S(1)}, u32[]{:S(2)}, u32[]{:S(2)}) collective-permute-start(f32[22,8,128]{2,1,0:T(8,128)S(1)} %pad_maximum_fusion.1), channel_id=1, source_target_pairs={{0,16},{32,48},{224,240},{192,208},{193,209},{225,241},{33,49},{1,... | collective-permute-start | bytes 270344 | tf_op jit(solution)/shard_map/ppermute | solution.py:701
  45.9 32.8 %copy-start = (f32[2,2,256,256]{3,2,1,0:T(8,128)S(1)}, f32[2,2,256,256]{3,2,1,0:T(8,128)}, u32[]{:S(2)}) copy-start(f32[2,2,256,256]{3,2,1,0:T(8,128)} %param.6) | copy-start | bytes 3145732
  78.1 1.9 %collective-permute-start.4 = (f32[8,96,128]{2,1,0:T(8,128)S(1)}, f32[8,96,128]{2,1,0:T(8,128)S(1)}, u32[]{:S(2)}, u32[]{:S(2)}) collective-permute-start(f32[8,96,128]{2,1,0:T(8,128)S(1)} %slice_select_fusion), channel_id=1, source_target_pairs={{0,16},{16,0},{32,48},{48,32},{64,80},{80,64},{96,112},{112,96},{1... | collective-permute-start | bytes 1179656 | tf_op jit(solution)/shard_map/ppermute | solution.py:705

commit v10 on v9

--- a/solution.py
+++ b/solution.py
@@ -632,10 +632,15 @@
                 held[upper, 0, 1, rows, cols] = after
                 held[upper, 1, 0, rows, cols] = now - before - start
                 held[upper, 1, 1, rows, cols] = after - now - forcing[0, 1, upper, core, rows, cols]
-        copies.append(pltpu.make_async_copy(held.at[upper], out.at[:, :, upper, core], sent.at[upper]))
-        copies[upper].start()
-    for upper in range(2):
-        copies[upper].wait()
+            piece = 2 * upper + half
+            copies.append(
+                pltpu.make_async_copy(
+                    held.at[upper, :, :, :, cols], out.at[:, :, upper, core, :, cols], sent.at[piece]
+                )
+            )
+            copies[piece].start()
+    for copy in copies:
+        copy.wait()
 
 
 def finish(units, forcing, initial, last, result=None):
@@ -646,7 +651,7 @@
         + [pl.BlockSpec(memory_space=pltpu.HBM)] * other,
         out_specs=pl.BlockSpec(memory_space=pltpu.HBM),
         out_shape=jax.ShapeDtypeStruct((2, 2, 2, 2, 64, 256), jnp.float32),
-        scratch_shapes=[pltpu.VMEM((2, 2, 2, 64, 256), jnp.float32), pltpu.SemaphoreType.DMA((2,))],
+        scratch_shapes=[pltpu.VMEM((2, 2, 2, 64, 256), jnp.float32), pltpu.SemaphoreType.DMA((4,))],
         input_output_aliases={4: 0} if other else {},
         compiler_params=params(),
         cost_estimate=cost(2**20),

time: 81.2 us -> 81.3 us (level)
  no operation moved by 1% of the time
where the time goes in v10:
time: 81.3 us; the launch traced here: 81.1 us
  blocking collectives  59.7 us (73%)
  Pallas kernels  11.8 us (15%)
  starting transfers between devices  5.24 us (6%)
  local copies, waits for them, and re-layouts  2.21 us (3%)
  waiting for transfers between devices  1.97 us (2%)
    all_to_all x2, blocking collectives, chips_exchange(): lax.all_to_all(pieces, 'tm', 0, 0, axis_index_groups=CHIPS, tiled=True)  59.7 us
    pallas_call x1, Pallas kernels, solve(): pl.pallas_call(solve_kernel, in_specs=[pl.BlockSpec(memory_space=pltpu.SM...  5.29 us
    ppermute x1, starting transfers between devices, per_device(): from_cross = lax.ppermute(strip(to_cross, is_lower), AXES, TO_CROSS)  2.8 us
    pallas_call x2, Pallas kernels, finish(): pl.pallas_call(functools.partial(finish_kernel, int(other)), in_specs=[pl...  2.16 us
    squeeze x2, local copies, waits for them, and re-layouts, prepare(): lax.dynamic_index_in_dim(forcing.reshape(2, 2, 2, 2, 64, 256), core, 3, k...  2.15 us
  transfers between devices with their start and end apart: 5, of which 4 were waited for; matrix products, arithmetic and copies ran while one was open for 1% of the time, Pallas kernels for 5%

profile of v10, /device:TPU:33, one launch (start us, length us, event | category | flops | bytes accessed | tf_op | source)
XLA Modules:
  0.0 81.1 jit_solution(2648086205779866988)
XLA Ops:
  0.0 1.1 %dynamic-slice_bitcast_fusion.1.forcing = f32[2,2,2,64,256]{4,3,2,1,0:T(8,128)S(1)} fusion(f32[2,2,2,2,64,256]{5,4,3,2,1,0:T(8,128)} %bitcast.28, s32[]{:T(128)S(6)} %select_n.42), kind=kLoop, calls=%fused_computation.1 | loop fusion | bytes 1048580 | tf_op jit(solution)/shard_map/jit(dynamic_index_in_dim)/squeeze | solution.py:128
  1.1 0.0 copy-start.1
  1.1 0.0 copy-start.2
  1.1 0.0 copy-start.3
  1.1 0.0 copy-start.5
  1.1 0.2 prepare_other.1
  1.3 0.8 collective-permute-start
  2.1 1.1 %dynamic-slice_bitcast_fusion.forcing = f32[2,2,2,64,256]{4,3,2,1,0:T(8,128)S(1)} fusion(f32[2,2,2,2,64,256]{5,4,3,2,1,0:T(8,128)} %bitcast.29, s32[]{:T(128)S(6)} %select_n.43), kind=kLoop, calls=%fused_computation | loop fusion | bytes 1048580 | tf_op jit(solution)/shard_map/jit(dynamic_index_in_dim)/squeeze | solution.py:128
  3.2 0.2 prepare_own.1.mine
  3.3 0.1 collective-permute-done.received
  3.4 0.3 merge.1
  3.7 33.5 %all_to_all.10.received = f32[8,184,128]{2,1,0:T(8,128)S(1)} all-to-all(f32[8,184,128]{2,1,0:T(8,128)S(1)} %merge.1), channel_id=1, replica_groups={{0,32,64,96,128,160,192,224},{16,48,80,112,144,176,208,240},{1,33,65,97..., dimensions={0} | all-to-all | bytes 1507328 | tf_op jit(solution)/shard_map/all_to_all | solution.py:679
  37.2 0.0 copy-done.1
  37.2 0.0 copy-done.2
  37.2 0.0 copy-done.3
  37.2 0.0 copy-start.4
  37.2 1.0 %transform.1 = (f32[33,32,128]{2,1,0:T(8,128)S(1)}, f32[17,8,128]{2,1,0:T(8,128)S(1)}) custom-call(f32[8]{0:T(128)S(1)} %copy-done.5, s32[256,256]{1,0:T(8,128)S(1)} %copy-done.3, f32[2,256,256]{2,1,0:T(8,128)S(1)} %copy-done.1, f32[2,256,256]{2,1,0:T(8,128)S(1)} %copy-done.2, f32[8,184,128]{2,1,0:T(8,128)S(1)} %all_to_all.10.received), custom_call_target="tpu_custom_call" | custom-call | tf_op jit(solution)/shard_map/transform/pallas_call | solution.py:330
  38.2 0.8 %collective-permute-start.1 = (f32[17,8,128]{2,1,0:T(8,128)S(1)}, f32[17,8,128]{2,1,0:T(8,128)S(1)}, u32[]{:S(2)}, u32[]{:S(2)}) collective-permute-start(f32[17,8,128]{2,1,0:T(8,128)S(1)} %get-tuple-element.22), channel_id=1, source_target_pairs={{0,16},{32,224},{224,32},{192,193},{193,192},{225,33},{33,225},{1,... | collective-permute-start | bytes 208904 | tf_op jit(solution)/shard_map/ppermute | solution.py:694
  39.1 1.4 %strips.1 = (f32[33,64,128]{2,1,0:T(8,128)S(1)}, f32[22,8,128]{2,1,0:T(8,128)S(1)}, f32[22,8,128]{2,1,0:T(8,128)S(1)}) custom-call(f32[8]{0:T(128)S(1)} %copy-done.5, s32[256,256]{1,0:T(8,128)S(1)} %copy-done.3, f32[2,256,256]{2,1,0:T(8,128)S(1)} %copy-done.1, f32[2,256,256]{2,1,0:T(8,128)S(1)} %copy-done.2, f32[8,184,128]{2,1,0:T(8,128)S(1)} %all_to_all.10.received, ...), custom_call_target="tpu_custom_call" | custom-call | flops 1048576 | bytes 1048576 | tf_op jit(solution)/shard_map/strips/pallas_call | solution.py:388
  40.5 0.9 %collective-permute-done.1.from_side = f32[17,8,128]{2,1,0:T(8,128)S(1)} collective-permute-done((f32[17,8,128]{2,1,0:T(8,128)S(1)}, f32[17,8,128]{2,1,0:T(8,128)S(1)}, u32[]{:S(2)}, u32[]{:S(2)}) %collective-permute-start.1) | collective-permute-done | bytes 69664 | tf_op jit(solution)/shard_map/ppermute | solution.py:694
  41.5 2.8 %collective-permute-start.2 = (f32[22,8,128]{2,1,0:T(8,128)S(1)}, f32[22,8,128]{2,1,0:T(8,128)S(1)}, u32[]{:S(2)}, u32[]{:S(2)}) collective-permute-start(f32[22,8,128]{2,1,0:T(8,128)S(1)} %pad_maximum_fusion), channel_id=1, source_target_pairs={{0,28},{32,60},{224,252},{192,220},{193,221},{225,253},{33,61},{1,... | collective-permute-start | bytes 270344 | tf_op jit(solution)/shard_map/ppermute | solution.py:705
  44.4 0.3 collective-permute-start.3
  44.6 1.3 %widen.1.middle = f32[16,4,96,128]{3,2,1,0:T(8,128)S(1)} custom-call(f32[16,2]{1,0:T(8,128)S(1)} %copy-done.4, f32[33,64,128]{2,1,0:T(8,128)S(1)} %get-tuple-element.21.wide, f32[17,8,128]{2,1,0:T(8,128)S(1)} %collective-permute-done.1.from_side), custom_call_target="tpu_custom_call" | custom-call | flops 2097152 | bytes 2097152 | tf_op jit(solution)/shard_map/widen/pallas_call | solution.py:489
  45.9 0.0 copy-start
  45.9 0.7 collective-permute-done.2.from_cross
  46.6 0.0 collective-permute-done.3.from_core
  46.6 5.3 %solve.1 = (f32[8,160,128]{2,1,0:T(8,128)S(1)}, f32[16,4,96,128]{3,2,1,0:T(8,128)S(1)}) custom-call(f32[16,2]{1,0:T(8,128)S(1)} %copy-done.4, f32[16,4,96,128]{3,2,1,0:T(8,128)S(1)} %widen.1.middle, f32[22,8,128]{2,1,0:T(8,128)S(1)} %collective-permute-done.2.from_cross, ...), custom_call_target="tpu_custom_call", output_to_operand_aliasing={{1}: (1, {})} | custom-call | tf_op jit(solution)/shard_map/solve/pallas_call | solution.py:588
  51.9 26.2 %all_to_all.11.units = f32[8,160,128]{2,1,0:T(8,128)S(1)} all-to-all(f32[8,160,128]{2,1,0:T(8,128)S(1)} %get-tuple-element.26), channel_id=1, replica_groups={{0,32,64,96,128,160,192,224},{16,48,80,112,144,176,208,240},{1,33,65,97..., dimensions={0} | all-to-all | bytes 1310720 | tf_op jit(solution)/shard_map/all_to_all | solution.py:679
  78.1 0.6 collective-permute-start.4
  78.7 1.1 %finish_own.1.refs_0_ = f32[2,2,2,2,64,256]{5,4,3,2,1,0:T(8,128)} custom-call(f32[8,160,128]{2,1,0:T(8,128)S(1)} %all_to_all.11.units, f32[2,2,2,2,64,256]{5,4,3,2,1,0:T(8,128)S(1)} %bitcast.30, f32[2,2,2,64,256]{4,3,2,1,0:T(8,128)S(1)} %bitcast.32, f32[2,2,2,64,256]{4,3,2,1,0:T(8,128)S(1)} %bitcast.34), custom_call_target="tpu_custom_call" | custom-call | flops 1048576 | bytes 1048576 | tf_op jit(solution)/shard_map/finish_own/pallas_call | solution.py:648
  79.8 0.3 collective-permute-done.4.units
  80.0 1.1 %finish_other.1 = f32[2,2,2,2,64,256]{5,4,3,2,1,0:T(8,128)} custom-call(f32[8,96,128]{2,1,0:T(8,128)S(1)} %collective-permute-done.4.units, f32[2,2,2,2,64,256]{5,4,3,2,1,0:T(8,128)S(1)} %bitcast.31, f32[2,2,2,64,256]{4,3,2,1,0:T(8,128)S(1)} %bitcast.33, f32[2,2,2,64,256]{4,3,2,1,0:T(8,128)S(1)} %bitcast.35, ...), custom_call_target="tpu_custom_call", output_to_operand_aliasing={{}: (4, {})} | custom-call | flops 1048576 | bytes 1048576 | tf_op jit(solution)/shard_map/finish_other/pallas_call | solution.py:648
  (13 shorter events, 0.1 us)
Async XLA Ops:
  1.1 36.1 %copy-start.1 = (f32[2,256,256]{2,1,0:T(8,128)S(1)}, f32[2,256,256]{2,1,0:T(8,128)}, u32[]{:S(2)}) copy-start(f32[2,256,256]{2,1,0:T(8,128)} %initial.3) | copy-start | bytes 1572868
  1.1 36.1 %copy-start.2 = (f32[2,256,256]{2,1,0:T(8,128)S(1)}, f32[2,256,256]{2,1,0:T(8,128)}, u32[]{:S(2)}) copy-start(f32[2,256,256]{2,1,0:T(8,128)} %last.3) | copy-start | bytes 1572868
  1.1 36.1 %copy-start.3 = (s32[256,256]{1,0:T(8,128)S(1)}, s32[256,256]{1,0:T(8,128)}, u32[]{:S(2)}) copy-start(s32[256,256]{1,0:T(8,128)} %cell_class.3) | copy-start | bytes 786436
  1.1 36.1 %copy-start.5 = (f32[8]{0:T(128)S(1)}, f32[8]{0:T(128)}, u32[]{:S(2)}) copy-start(f32[8]{0:T(128)} %table.3) | copy-start | bytes 100
  1.3 2.1 %collective-permute-start = (f32[8,96,128]{2,1,0:T(8,128)S(1)}, f32[8,96,128]{2,1,0:T(8,128)S(1)}, u32[]{:S(2)}, u32[]{:S(2)}) collective-permute-start(f32[8,96,128]{2,1,0:T(8,128)S(1)} %prepare_other.1), channel_id=1, source_target_pairs={{0,16},{16,0},{32,48},{48,32},{64,80},{80,64},{96,112},{112,96},{1... | collective-permute-start | bytes 1179656 | tf_op jit(solution)/shard_map/ppermute | solution.py:687
  37.2 7.4 %copy-start.4 = (f32[16,2]{1,0:T(8,128)S(1)}, f32[16,2]{1,0:T(8,128)}, u32[]{:S(2)}) copy-start(f32[16,2]{1,0:T(8,128)} %constant.22.clone.lam) | copy-start | bytes 388
  38.2 3.2 %collective-permute-start.1 = (f32[17,8,128]{2,1,0:T(8,128)S(1)}, f32[17,8,128]{2,1,0:T(8,128)S(1)}, u32[]{:S(2)}, u32[]{:S(2)}) collective-permute-start(f32[17,8,128]{2,1,0:T(8,128)S(1)} %get-tuple-element.22), channel_id=1, source_target_pairs={{0,16},{32,224},{224,32},{192,193},{193,192},{225,33},{33,225},{1,... | collective-permute-start | bytes 208904 | tf_op jit(solution)/shard_map/ppermute | solution.py:694
  41.5 5.0 %collective-permute-start.2 = (f32[22,8,128]{2,1,0:T(8,128)S(1)}, f32[22,8,128]{2,1,0:T(8,128)S(1)}, u32[]{:S(2)}, u32[]{:S(2)}) collective-permute-start(f32[22,8,128]{2,1,0:T(8,128)S(1)} %pad_maximum_fusion), channel_id=1, source_target_pairs={{0,28},{32,60},{224,252},{192,220},{193,221},{225,253},{33,61},{1,... | collective-permute-start | bytes 270344 | tf_op jit(solution)/shard_map/ppermute | solution.py:705
  44.4 2.2 %collective-permute-start.3 = (f32[22,8,128]{2,1,0:T(8,128)S(1)}, f32[22,8,128]{2,1,0:T(8,128)S(1)}, u32[]{:S(2)}, u32[]{:S(2)}) collective-permute-start(f32[22,8,128]{2,1,0:T(8,128)S(1)} %pad_maximum_fusion.1), channel_id=1, source_target_pairs={{0,16},{32,48},{224,240},{192,208},{193,209},{225,241},{33,49},{1,... | collective-permute-start | bytes 270344 | tf_op jit(solution)/shard_map/ppermute | solution.py:706
  45.9 32.8 %copy-start = (f32[2,2,256,256]{3,2,1,0:T(8,128)S(1)}, f32[2,2,256,256]{3,2,1,0:T(8,128)}, u32[]{:S(2)}) copy-start(f32[2,2,256,256]{3,2,1,0:T(8,128)} %param.6) | copy-start | bytes 3145732
  78.1 1.9 %collective-permute-start.4 = (f32[8,96,128]{2,1,0:T(8,128)S(1)}, f32[8,96,128]{2,1,0:T(8,128)S(1)}, u32[]{:S(2)}, u32[]{:S(2)}) collective-permute-start(f32[8,96,128]{2,1,0:T(8,128)S(1)} %slice_select_fusion), channel_id=1, source_target_pairs={{0,16},{16,0},{32,48},{48,32},{64,80},{80,64},{96,112},{112,96},{1... | collective-permute-start | bytes 1179656 | tf_op jit(solution)/shard_map/ppermute | solution.py:710
